TPU v7x, 32 devices: a whole 2x2x4 slice. The times are simulated.
32 devices in a mesh: seq: 4 (over y, core), dp: 8 (over z, x).
Axes of the slice: x: 2, y: 2, z: 4, core: 2. Of those that a mesh axis runs over, the one named last changes fastest.
Arguments:
- tokens: bfloat16 [8, 2048, 768], P('dp', 'seq'), may hold values from -6 to 6
- item_lengths: int32 [8, 4], P('dp'), may hold values from 1 to 2045, as said below
- w_query: bfloat16 [768, 768], replicated, may hold values from -0.21875 to 0.21875
- w_key: bfloat16 [768, 768], replicated, may hold values from -0.21875 to 0.21875
- w_value: bfloat16 [768, 768], replicated, may hold values from -0.21875 to 0.21875
- w_out: bfloat16 [768, 768], replicated, may hold values from -2.5 to 2.5
- w_in: bfloat16 [768, 3072], replicated, may hold values from -0.21875 to 0.21875
- w_back: bfloat16 [3072, 768], replicated, may hold values from -0.109375 to 0.109375
- norm1_gain: float32 [768], replicated, may hold values from 0.5 to 1.5
- norm1_bias: float32 [768], replicated, may hold values from -1 to 1
- norm2_gain: float32 [768], replicated, may hold values from 0.5 to 1.5
- norm2_bias: float32 [768], replicated, may hold values from -1 to 1
- pool_weight: float32 [768, 5], replicated, may hold values from 0.1 to 0.5
- out_grad: bfloat16 [8, 2048, 768], P('dp', 'seq'), may hold values from -6 to 6
Outputs:
- mixed: bfloat16 [8, 2048, 768], P('dp', 'seq')
- tokens_grad: bfloat16 [8, 2048, 768], P('dp', 'seq')
- grad_w_query: float32 [768, 768], P(('seq', 'dp'))
- grad_w_key: float32 [768, 768], P(('seq', 'dp'))
- grad_w_value: float32 [768, 768], P(('seq', 'dp'))
- grad_w_out: float32 [768, 768], P(('seq', 'dp'))
- grad_w_in: float32 [768, 3072], P(('seq', 'dp'))
- grad_w_back: float32 [3072, 768], P(('seq', 'dp'))
- grad_norm1_gain: float32 [768], P(('seq', 'dp'))
- grad_norm1_bias: float32 [768], P(('seq', 'dp'))
- grad_norm2_gain: float32 [768], P(('seq', 'dp'))
- grad_norm2_bias: float32 [768], P(('seq', 'dp'))
- grad_pool_weight: float32 [768, 5], P(('seq', 'dp'))
Inputs may be any that keep to these rules, and one draw needn't show every extreme that they name: `item_lengths`: in each row the lengths sum to 2048 or less; one item, at a slot drawn per row, starts within the row's first 512 tokens and ends within its last 512.
All inputs are finite; a program needn't handle non-finite values.
Results may differ from a plain program's by a relative error of at most 0.014.
Values may be sent and summed in bfloat16 or wider, within the bound.
A program may use at most 192 MiB of HBM per device.

v0:
```python
from functools import partial

import jax
import jax.numpy as jnp
from jax import lax
from jax.sharding import PartitionSpec as P

H = 12
DH = 64
HALF = 64
PWIN = 512


def with_halo(cells, sides, width):
    for axis, dim in sides:
        count = lax.axis_size(axis)
        ends = count - 1
        head = lax.slice_in_dim(cells, 0, width, axis=dim)
        tail = lax.slice_in_dim(cells, cells.shape[dim] - width, cells.shape[dim], axis=dim)
        cells = jnp.concatenate(
            [
                lax.ppermute(tail, axis, [(i, (i + 1) % count) for i in range(ends)]),
                cells,
                lax.ppermute(head, axis, [((i + 1) % count, i) for i in range(ends)]),
            ],
            axis=dim,
        )
    return cells


def shifted_2(shard, axis, by):
    size = lax.axis_size(axis)
    pairs = [(i, i + by) for i in range(size) if 0 <= i + by < size]
    return lax.ppermute(shard, axis, pairs)


def layer_norm(values, gain, offset):
    center = jnp.mean(values, axis=-1, keepdims=True)
    shifted = values - center
    spread = jnp.mean(shifted * shifted, axis=-1, keepdims=True)
    return shifted * lax.rsqrt(spread + 1e-05) * gain + offset


def score_pair(query_group, pair_group, pool_group, near_mask, pool_mask):
    group_size = query_group.shape[0]
    span = pair_group.shape[2]
    pool_count = pool_group.shape[2]
    key_heads = pair_group[:, 0].reshape(group_size, span, H, DH)
    pool_heads = pool_group[:, 0].reshape(group_size, pool_count, H, DH)
    near_scores = (
        jnp.einsum("gthe,gkhe->ghtk", query_group, key_heads, preferred_element_type=jnp.float32)
        * 0.125
    )
    pool_scores = (
        jnp.einsum("gthe,gkhe->ghtk", query_group, pool_heads, preferred_element_type=jnp.float32)
        * 0.125
    )
    near_scores = jnp.where(near_mask[:, None], near_scores, -1e30)
    pool_scores = jnp.where(pool_mask[:, None], pool_scores, -1e30)
    value_heads = pair_group[:, 1].reshape(group_size, span, H, DH)
    pool_values = pool_group[:, 1].reshape(group_size, pool_count, H, DH)
    return (near_scores, pool_scores, key_heads, pool_heads, value_heads, pool_values)


def attend_forward(items):
    query_group, pair_group, pool_group, near_mask, pool_mask = items
    near_scores, pool_scores, key_heads, pool_heads, value_heads, pool_values = score_pair(
        query_group, pair_group, pool_group, near_mask, pool_mask
    )
    top = jnp.maximum(jnp.max(near_scores, axis=3), jnp.max(pool_scores, axis=3))
    near_exp = jnp.exp(near_scores - top[..., None])
    pool_exp = jnp.exp(pool_scores - top[..., None])
    total = jnp.sum(near_exp, axis=3) + jnp.sum(pool_exp, axis=3)
    near_probs = (near_exp / total[..., None]).astype(jnp.bfloat16)
    pool_probs = (pool_exp / total[..., None]).astype(jnp.bfloat16)
    mixed = jnp.einsum(
        "ghtk,gkhe->gthe", near_probs, value_heads, preferred_element_type=jnp.float32
    )
    mixed = mixed + jnp.einsum(
        "ghtk,gkhe->gthe", pool_probs, pool_values, preferred_element_type=jnp.float32
    )
    return (mixed.reshape(mixed.shape[0], mixed.shape[1], H * DH), top + jnp.log(total))


def attend_backward(items):
    query_group, pair_group, pool_group, near_mask, pool_mask, log_total, grad_group = items
    near_scores, pool_scores, key_heads, pool_heads, value_heads, pool_values = score_pair(
        query_group, pair_group, pool_group, near_mask, pool_mask
    )
    group_size, tok_count = (query_group.shape[0], query_group.shape[1])
    span, pool_count = (key_heads.shape[1], pool_heads.shape[1])
    near_probs = jnp.exp(near_scores - log_total[..., None])
    pool_probs = jnp.exp(pool_scores - log_total[..., None])
    near_low = near_probs.astype(jnp.bfloat16)
    pool_low = pool_probs.astype(jnp.bfloat16)
    grad_heads = grad_group.reshape(group_size, tok_count, H, DH)
    near_dprob = jnp.einsum(
        "gthe,gkhe->ghtk", grad_heads, value_heads, preferred_element_type=jnp.float32
    )
    pool_dprob = jnp.einsum(
        "gthe,gkhe->ghtk", grad_heads, pool_values, preferred_element_type=jnp.float32
    )
    inner_sum = jnp.sum(near_probs * near_dprob, axis=3) + jnp.sum(pool_probs * pool_dprob, axis=3)
    near_dscore = (near_probs * (near_dprob - inner_sum[..., None])).astype(jnp.bfloat16)
    pool_dscore = (pool_probs * (pool_dprob - inner_sum[..., None])).astype(jnp.bfloat16)
    grad_query = jnp.einsum(
        "ghtk,gkhe->gthe", near_dscore, key_heads, preferred_element_type=jnp.float32
    )
    grad_query = (
        grad_query
        + jnp.einsum("ghtk,gkhe->gthe", pool_dscore, pool_heads, preferred_element_type=jnp.float32)
    ) * 0.125
    near_key_grad = (
        jnp.einsum("ghtk,gthe->gkhe", near_dscore, query_group, preferred_element_type=jnp.float32)
        * 0.125
    )
    near_value_grad = jnp.einsum(
        "ghtk,gthe->gkhe", near_low, grad_heads, preferred_element_type=jnp.float32
    )
    pool_key_grad = (
        jnp.einsum("ghtk,gthe->gkhe", pool_dscore, query_group, preferred_element_type=jnp.float32)
        * 0.125
    )
    pool_value_grad = jnp.einsum(
        "ghtk,gthe->gkhe", pool_low, grad_heads, preferred_element_type=jnp.float32
    )
    width_all = H * DH
    near_grads = jnp.stack(
        [
            near_key_grad.reshape(group_size, span, width_all),
            near_value_grad.reshape(group_size, span, width_all),
        ],
        axis=1,
    )
    pool_grads = jnp.stack(
        [
            pool_key_grad.reshape(group_size, pool_count, width_all),
            pool_value_grad.reshape(group_size, pool_count, width_all),
        ],
        axis=1,
    )
    return (grad_query.reshape(group_size, tok_count, width_all), near_grads, pool_grads)


def per_device(
    tokens,
    item_lengths,
    w_query,
    w_key,
    w_value,
    w_out,
    w_in,
    w_back,
    norm1_gain,
    norm1_bias,
    norm2_gain,
    norm2_bias,
    pool_weight,
    out_grad,
):
    row_count, tok_count, model_width = tokens.shape
    row_len = tok_count * lax.axis_size("seq")
    row_start = lax.axis_index("seq") * tok_count
    span = tok_count + 2 * HALF
    pool_all = row_len // 4
    places = jnp.arange(row_len, dtype=jnp.int32)
    bounds = jnp.cumsum(item_lengths, axis=1)
    segment_all = jnp.sum((places[None, :, None] >= bounds[:, None, :]).astype(jnp.int32), axis=2)
    segment_pad = jnp.pad(segment_all, ((0, 0), (HALF, HALF)), constant_values=-2)
    key_segments = lax.dynamic_slice_in_dim(segment_pad, row_start, span, 1)
    query_segments = key_segments[:, HALF : HALF + tok_count]
    pool_segments = segment_all[:, ::4]
    query_place = row_start + jnp.arange(tok_count, dtype=jnp.int32)
    key_place = row_start - HALF + jnp.arange(span, dtype=jnp.int32)
    pool_place = 4 * jnp.arange(pool_all, dtype=jnp.int32)
    near_mask = (jnp.abs(query_place[:, None] - key_place[None, :]) <= HALF)[None] & (
        query_segments[:, :, None] == key_segments[:, None, :]
    )
    pool_mask = (jnp.abs(query_place[:, None] - pool_place[None, :]) <= 2 * PWIN)[None] & (
        query_segments[:, :, None] == pool_segments[:, None, :]
    )
    tap_masks = []
    for tap_index in range(5):
        begin = HALF + tap_index - 2
        tap_masks.append(
            (key_segments[:, begin : begin + tok_count : 4] == query_segments[:, ::4]).astype(
                jnp.float32
            )
        )
    flat_tokens = tokens.reshape(row_count * tok_count, model_width)
    queries = jnp.dot(flat_tokens, w_query, preferred_element_type=jnp.float32).astype(jnp.bfloat16)
    keys_low = jnp.dot(flat_tokens, w_key, preferred_element_type=jnp.float32).astype(jnp.bfloat16)
    values_low = jnp.dot(flat_tokens, w_value, preferred_element_type=jnp.float32).astype(
        jnp.bfloat16
    )
    key_value = jnp.stack(
        [
            keys_low.reshape(row_count, tok_count, model_width),
            values_low.reshape(row_count, tok_count, model_width),
        ],
        axis=1,
    )
    pair_halo = with_halo(key_value, (("seq", 2),), HALF)
    pooled_sum = jnp.zeros((row_count, 2, tok_count // 4, model_width), jnp.float32)
    for tap_index in range(5):
        begin = HALF + tap_index - 2
        taken = pair_halo[:, :, begin : begin + tok_count : 4].astype(jnp.float32)
        pooled_sum = (
            pooled_sum + taken * tap_masks[tap_index][:, None, :, None] * pool_weight[:, tap_index]
        )
    pooled_low = pooled_sum.astype(jnp.bfloat16)
    pooled_rows = lax.all_gather(pooled_low, "seq", axis=2, tiled=True)
    group_size = min(row_count, max(1, 512 // tok_count))
    group_count = row_count // group_size

    def grouped(array):
        return array.reshape((group_count, group_size) + array.shape[1:])

    query_heads = queries.reshape(row_count, tok_count, H, DH)
    shared = (
        grouped(query_heads),
        grouped(pair_halo),
        grouped(pooled_rows),
        grouped(near_mask),
        grouped(pool_mask),
    )
    attention, log_total = lax.map(attend_forward, shared)
    attended = attention.reshape(row_count * tok_count, model_width).astype(jnp.bfloat16)
    branch = jnp.dot(attended, w_out, preferred_element_type=jnp.float32)
    first, first_back = jax.vjp(
        layer_norm, flat_tokens.astype(jnp.float32) + branch, norm1_gain, norm1_bias
    )
    first_low = first.astype(jnp.bfloat16)
    inner = jnp.dot(first_low, w_in, preferred_element_type=jnp.float32)
    activated, gelu_back = jax.vjp(partial(jax.nn.gelu, approximate=False), inner)
    activated_low = activated.astype(jnp.bfloat16)
    feed = jnp.dot(activated_low, w_back, preferred_element_type=jnp.float32)
    output, second_back = jax.vjp(layer_norm, first + feed, norm2_gain, norm2_bias)
    mixed = output.astype(jnp.bfloat16).reshape(row_count, tok_count, model_width)
    upstream = out_grad.reshape(row_count * tok_count, model_width).astype(jnp.float32)
    z_grad, grad_gain_two, grad_bias_two = second_back(upstream)
    feed_grad = z_grad.astype(jnp.bfloat16)
    grad_back_weight = jnp.einsum(
        "nf,nd->fd", activated_low, feed_grad, preferred_element_type=jnp.float32
    )
    activated_grad = jnp.einsum("nd,fd->nf", feed_grad, w_back, preferred_element_type=jnp.float32)
    (inner_grad,) = gelu_back(activated_grad)
    inner_low = inner_grad.astype(jnp.bfloat16)
    grad_in_weight = jnp.einsum(
        "nd,nf->df", first_low, inner_low, preferred_element_type=jnp.float32
    )
    first_grad = z_grad + jnp.einsum(
        "nf,df->nd", inner_low, w_in, preferred_element_type=jnp.float32
    )
    sum_grad, grad_gain_one, grad_bias_one = first_back(first_grad)
    branch_grad = sum_grad.astype(jnp.bfloat16)
    grad_out_weight = jnp.einsum(
        "nd,ne->de", attended, branch_grad, preferred_element_type=jnp.float32
    )
    attended_grad = jnp.einsum(
        "ne,de->nd", branch_grad, w_out, preferred_element_type=jnp.float32
    ).astype(jnp.bfloat16)
    query_grad, near_grads, pool_grads = lax.map(
        attend_backward,
        shared + (log_total, grouped(attended_grad.reshape(row_count, tok_count, model_width))),
    )
    pool_grads = pool_grads.reshape(row_count, 2, pool_all, model_width)
    pooled_grad = lax.psum_scatter(
        pool_grads.astype(jnp.bfloat16), "seq", scatter_dimension=2, tiled=True
    ).astype(jnp.float32)
    halo_grad = near_grads.reshape(row_count, 2, span, model_width)
    tap_columns = []
    for tap_index in range(5):
        begin = HALF + tap_index - 2
        weighted = pooled_grad * tap_masks[tap_index][:, None, :, None]
        taken = pair_halo[:, :, begin : begin + tok_count : 4].astype(jnp.float32)
        tap_columns.append(jnp.sum(weighted * taken, axis=(0, 1, 2)))
        halo_grad = halo_grad.at[:, :, begin : begin + tok_count : 4].add(
            weighted * pool_weight[:, tap_index]
        )
    grad_pool = jnp.stack(tap_columns, axis=1)
    from_above = shifted_2(halo_grad[:, :, :HALF].astype(jnp.bfloat16), "seq", -1).astype(
        jnp.float32
    )
    from_below = shifted_2(
        halo_grad[:, :, HALF + tok_count :].astype(jnp.bfloat16), "seq", 1
    ).astype(jnp.float32)
    own_grad = halo_grad[:, :, HALF : HALF + tok_count]
    own_grad = own_grad.at[:, :, :HALF].add(from_below)
    own_grad = own_grad.at[:, :, tok_count - HALF :].add(from_above)
    key_grad = own_grad[:, 0].reshape(row_count * tok_count, model_width).astype(jnp.bfloat16)
    value_grad = own_grad[:, 1].reshape(row_count * tok_count, model_width).astype(jnp.bfloat16)
    query_low = query_grad.reshape(row_count * tok_count, model_width).astype(jnp.bfloat16)
    grad_query_weight = jnp.einsum(
        "nd,ne->de", flat_tokens, query_low, preferred_element_type=jnp.float32
    )
    grad_key_weight = jnp.einsum(
        "nd,ne->de", flat_tokens, key_grad, preferred_element_type=jnp.float32
    )
    grad_value_weight = jnp.einsum(
        "nd,ne->de", flat_tokens, value_grad, preferred_element_type=jnp.float32
    )
    input_grad = sum_grad + jnp.einsum(
        "ne,de->nd", query_low, w_query, preferred_element_type=jnp.float32
    )
    input_grad = input_grad + jnp.einsum(
        "ne,de->nd", key_grad, w_key, preferred_element_type=jnp.float32
    )
    input_grad = input_grad + jnp.einsum(
        "ne,de->nd", value_grad, w_value, preferred_element_type=jnp.float32
    )
    tokens_grad = input_grad.astype(jnp.bfloat16).reshape(row_count, tok_count, model_width)
    summed = (
        lax.psum_scatter(grad_query_weight, ("seq", "dp"), scatter_dimension=0, tiled=True),
        lax.psum_scatter(grad_key_weight, ("seq", "dp"), scatter_dimension=0, tiled=True),
        lax.psum_scatter(grad_value_weight, ("seq", "dp"), scatter_dimension=0, tiled=True),
        lax.psum_scatter(grad_out_weight, ("seq", "dp"), scatter_dimension=0, tiled=True),
        lax.psum_scatter(grad_in_weight, ("seq", "dp"), scatter_dimension=0, tiled=True),
        lax.psum_scatter(grad_back_weight, ("seq", "dp"), scatter_dimension=0, tiled=True),
        lax.psum_scatter(grad_gain_one, ("seq", "dp"), scatter_dimension=0, tiled=True),
        lax.psum_scatter(grad_bias_one, ("seq", "dp"), scatter_dimension=0, tiled=True),
        lax.psum_scatter(grad_gain_two, ("seq", "dp"), scatter_dimension=0, tiled=True),
        lax.psum_scatter(grad_bias_two, ("seq", "dp"), scatter_dimension=0, tiled=True),
        lax.psum_scatter(grad_pool, ("seq", "dp"), scatter_dimension=0, tiled=True),
    )
    return (
        mixed,
        tokens_grad,
        summed[0],
        summed[1],
        summed[2],
        summed[3],
        summed[4],
        summed[5],
        summed[6],
        summed[7],
        summed[8],
        summed[9],
        summed[10],
    )


def solution(mesh):
    return jax.shard_map(
        per_device,
        mesh=mesh,
        in_specs=(
            P("dp", "seq", None),
            P("dp", None),
            P(),
            P(),
            P(),
            P(),
            P(),
            P(),
            P(),
            P(),
            P(),
            P(),
            P(),
            P("dp", "seq", None),
        ),
        out_specs=(
            P("dp", "seq", None),
            P("dp", "seq", None),
            P(("seq", "dp"), None),
            P(("seq", "dp"), None),
            P(("seq", "dp"), None),
            P(("seq", "dp"), None),
            P(("seq", "dp"), None),
            P(("seq", "dp"), None),
            P(("seq", "dp")),
            P(("seq", "dp")),
            P(("seq", "dp")),
            P(("seq", "dp")),
            P(("seq", "dp"), None),
        ),
        check_vma=False,
    )
```

profile of v0, /device:TPU:0, one launch (start us, length us, event | category | flops | bytes accessed | tf_op | source)
XLA Modules:
  0.0 940.2 jit_solution(14607886784213334314)
XLA Ops:
  59.4 7.8 fusion.105
  85.6 7.7 fusion
  93.9 6.5 fusion.17
  108.9 20.2 %multiply_convert_fusion.2 = (bf16[512,3072]{1,0:T(8,128)(2,1)S(1)}, f32[512,3072]{1,0:T(8,128)}, f32[512,3072]{1,0:T(8,128)}) fusion(bf16[768,3072]{1,0:T(8,128)(2,1)} %param.24, f32[512,768]{1,0:T(8,128)S(1)} %get-tuple-element.202, f32[768]{0:T(1024)S(1)} %copy-done.73, f32[768]{0:T(1024)S(1)} %copy-done.64, f32[512]{0:T(512)S(1)} %fusion.79, ...), kind=kOutput, calls=%fused_computation.29 | convolution fusion | flops 2520121344 | bytes 22030336 | tf_op jit(solution)/shard_map/dot_general | solution.py:234
  135.2 8.9 add_convert_fusion
  153.6 7.4 fusion.25
  161.1 9.8 %multiply_reduce_fusion.1 = (f32[12,512]{1,0:T(8,128)S(1)}, f32[12,512,512]{1,2,0:T(8,128)}) fusion(f32[12,512]{1,0:T(8,128)S(1)} %copy-done.33, f32[12,512,512]{1,2,0:T(8,128)} %copy-done.2, pred[512,512]{0,1:T(8,128)(4,1)S(1)} %copy-done.19, bf16[512,12,64]{0,2,1:T(8,128)(2,1)S(1)} %bitcast.195, bf16[512,12,64]{0,2,1:T(8,128)(2,1)S(1)} %bitcast.207), kind=kOutput, calls=%fused_computation.13 | convolution fusion | flops 418375680 | bytes 27049984 | tf_op jit(solution)/shard_map/while/body/eval_jaxpr/gthe,gkhe->ghtk/dot_general | solution.py:100
  170.9 9.7 %multiply_reduce_fusion = (f32[12,512]{1,0:T(8,128)S(1)}, f32[12,512,640]{2,1,0:T(8,128)}) fusion(f32[12,512,640]{2,1,0:T(8,128)S(1)} %bitcast.187, f32[12,512]{1,0:T(8,128)S(1)} %copy-done.33, bf16[512,12,64]{0,2,1:T(8,128)(2,1)S(1)} %bitcast.196, bf16[640,12,64]{0,2,1:T(8,128)(2,1)} %bitcast.204), kind=kOutput, calls=%fused_computation.6 | convolution fusion | flops 515106816 | bytes 33275904 | tf_op jit(solution)/shard_map/while/body/eval_jaxpr/gthe,gkhe->ghtk/dot_general | solution.py:97
  182.9 10.0 %multiply_convert_fusion.1 = bf16[12,512,512]{1,2,0:T(8,128)(2,1)S(1)} fusion(f32[12,512,512]{1,2,0:T(8,128)} %get-tuple-element.210, f32[12,512]{1,0:T(8,128)S(1)} %add.275, f32[12,512]{1,0:T(8,128)S(1)} %copy-done.33, f32[12,512,512]{1,2,0:T(8,128)} %copy-done.2, pred[512,512]{0,1:T(8,128)(4,1)S(1)} %copy-done.19), kind=kLoop, calls=%fused_computation.12 | loop fusion | flops 18874368 | bytes 31768576 | tf_op jit(solution)/shard_map/while/body/eval_jaxpr/convert_element_type | solution.py:105
  206.2 8.8 fusion.4
  222.6 11.3 %multiply_convert_fusion = bf16[12,512,640]{2,1,0:T(8,128)(2,1)S(1)} fusion(f32[12,512,640]{2,1,0:T(8,128)} %get-tuple-element.208, f32[12,512,640]{2,1,0:T(8,128)} %get-tuple-element.198, f32[12,512]{1,0:T(8,128)S(1)} %add.275, f32[12,512]{1,0:T(8,128)S(1)} %copy-done.33), kind=kLoop, calls=%fused_computation.5 | loop fusion | flops 15728640 | bytes 39370752 | tf_op jit(solution)/shard_map/while/body/eval_jaxpr/convert_element_type | solution.py:104
  257.6 7.6 maximum_bitcast_fusion
  274.6 18.4 %scatter_fusion = f32[2,640,768]{2,0,1:T(2,128)} fusion(f32[2,640,768]{2,0,1:T(2,128)} %maximum_bitcast_fusion, s32[128]{0:T(128)S(1)} %copy-done.72, f32[128,2,768]{2,1,0:T(2,128)} %copy.117), kind=kCustom, calls=%fused_computation | custom fusion | flops 196608 | bytes 2359808 | tf_op jit(solution)/shard_map/scatter-add | solution.py:278
  293.0 18.2 %scatter_fusion.1 = f32[2,640,768]{2,0,1:T(2,128)} fusion(f32[2,640,768]{2,0,1:T(2,128)} %scatter_fusion, s32[128]{0:T(128)S(1)} %copy-done.71, f32[128,2,768]{2,1,0:T(2,128)} %copy.118), kind=kCustom, calls=%fused_computation.1 | custom fusion | flops 196608 | bytes 2359808 | tf_op jit(solution)/shard_map/scatter-add | solution.py:278
  311.2 18.2 %scatter_fusion.2 = f32[2,640,768]{2,0,1:T(2,128)} fusion(f32[2,640,768]{2,0,1:T(2,128)} %scatter_fusion.1, s32[128]{0:T(128)S(1)} %copy-done.70, f32[128,2,768]{2,1,0:T(2,128)} %copy.119), kind=kCustom, calls=%fused_computation.2 | custom fusion | flops 196608 | bytes 2359808 | tf_op jit(solution)/shard_map/scatter-add | solution.py:278
  329.5 18.2 %scatter_fusion.3 = f32[2,640,768]{2,0,1:T(2,128)} fusion(f32[2,640,768]{2,0,1:T(2,128)} %scatter_fusion.2, s32[128]{0:T(128)S(1)} %copy-done.69, f32[128,2,768]{2,1,0:T(2,128)} %copy.120), kind=kCustom, calls=%fused_computation.3 | custom fusion | flops 196608 | bytes 2359808 | tf_op jit(solution)/shard_map/scatter-add | solution.py:278
  347.7 16.6 %scatter_fusion.4 = f32[2,640,768]{2,0,1:T(2,128)} fusion(f32[2,640,768]{2,0,1:T(2,128)} %scatter_fusion.3, s32[128]{0:T(128)S(1)} %copy-done.68, f32[128,2,768]{2,1,0:T(2,128)S(1)} %copy.121), kind=kCustom, calls=%fused_computation.4 | custom fusion | flops 196608 | bytes 2359808 | tf_op jit(solution)/shard_map/scatter-add | solution.py:278
  390.8 8.9 fusion.93
  400.4 8.8 fusion.90
  414.0 42.9 %all-reduce.6 = (f32[768]{0:T(1024)S(1)}, f32[768]{0:T(1024)S(1)}, f32[768]{0:T(1024)S(1)}, f32[768]{0:T(1024)S(1)}, f32[768,5]{0,1:T(8,128)S(1)}) all-reduce(f32[768]{0:T(1024)S(1)} %copy-done.62, f32[768]{0:T(1024)S(1)} %copy-done.63, f32[768]{0:T(1024)S(1)} %copy-done.51, ...), channel_id=9, replica_groups=mesh['seq'=4,'dp'=8] {'seq','dp'}, use_global_device_ids=true, to_apply=%region_29.30.clone | all-reduce | flops 6912 | bytes 55296
  466.2 80.0 %reduce-scatter.27.cloned.1.call-done = f32[24,768]{1,0:T(8,128)} async-done(((f32[768,768]{1,0:T(8,128)}), f32[24,768]{1,0:T(8,128)}) %reduce-scatter.27.cloned.1.call-update) | async-done | bytes 73744
  546.2 103.7 %reduce-scatter.25.cloned.1.call-done = f32[24,768]{1,0:T(8,128)} async-done(((f32[768,768]{1,0:T(8,128)}), f32[24,768]{1,0:T(8,128)}) %reduce-scatter.25.cloned.1.call-update) | async-done | bytes 73744
  649.9 142.0 %reduce-scatter.19.cloned.1.call-done = f32[24,3072]{1,0:T(8,128)} async-done(((f32[768,3072]{1,0:T(8,128)}), f32[24,3072]{1,0:T(8,128)}) %reduce-scatter.19.cloned.1.call-update) | async-done | bytes 294928 | tf_op jit(solution)/shard_map/reduce_scatter | solution.py:318
  791.9 141.3 %reduce-scatter.21.cloned.1.call-done = f32[96,768]{1,0:T(8,128)} async-done(((f32[3072,768]{1,0:T(8,128)}), f32[96,768]{1,0:T(8,128)}) %reduce-scatter.21.cloned.1.call-update) | async-done | bytes 294928 | tf_op jit(solution)/shard_map/reduce_scatter | solution.py:319
  (318 shorter events, 191.7 us)
Async XLA Ops:
  7.2 100.4 %copy-start = (bf16[768,768]{1,0:T(8,128)(2,1)S(1)}, bf16[768,768]{1,0:T(8,128)(2,1)}, u32[]{:S(2)}) copy-start(bf16[768,768]{1,0:T(8,128)(2,1)} %param.23) | copy-start | bytes 3538948
  7.2 65.1 %all-gather.2.cloned.1.call-start = ((), (), s32[]{:S(2)}) async-start(), calls=%async_computation.7 | async-start | bytes 1966080 | tf_op jit(solution)/shard_map/all_gather | solution.py:212
  13.0 16.9 %collective-permute-start = (bf16[1,2,64,768]{3,2,1,0:T(8,128)(2,1)}, bf16[1,2,64,768]{3,2,1,0:T(8,128)(2,1)S(1)}, u32[]{:S(2)}, u32[]{:S(2)}) collective-permute-start(bf16[1,2,64,768]{3,2,1,0:T(8,128)(2,1)} %get-tuple-element.185), channel_id=1, source_target_pairs={{0,8},{8,16},{16,24},{1,9},{9,17},{17,25},{2,10},{10,18},{18,26},{... | collective-permute-start | bytes 589832 | tf_op jit(solution)/shard_map/ppermute | solution.py:22
  15.4 15.2 %collective-permute-start.1 = (bf16[1,2,64,768]{3,2,1,0:T(8,128)(2,1)S(1)}, bf16[1,2,64,768]{3,2,1,0:T(8,128)(2,1)}, u32[]{:S(2)}, u32[]{:S(2)}) collective-permute-start(bf16[1,2,64,768]{3,2,1,0:T(8,128)(2,1)S(1)} %get-tuple-element.186), channel_id=1, source_target_pairs={{8,0},{16,8},{24,16},{9,1},{17,9},{25,17},{10,2},{18,10},{26,18},{... | collective-permute-start | bytes 589832 | tf_op jit(solution)/shard_map/ppermute | solution.py:24
  47.9 217.3 %reduce-scatter.15.cloned.1.call-start = ((), (), s32[]{:S(2)}) async-start(), calls=%async_computation.8 | async-start | bytes 1966080 | tf_op jit(solution)/shard_map/reduce_scatter | solution.py:268
  53.2 40.7 %copy-start.18 = (pred[512,512]{0,1:T(8,128)(4,1)}, pred[512,512]{0,1:T(8,128)(4,1)S(1)}, u32[]{:S(2)}) copy-start(pred[512,512]{0,1:T(8,128)(4,1)S(1)} %fusion.33) | copy-start | bytes 786436
  108.5 41.3 %copy-start.20 = (f32[512,768]{1,0:T(8,128)}, f32[512,768]{1,0:T(8,128)S(1)}, u32[]{:S(2)}) copy-start(f32[512,768]{1,0:T(8,128)S(1)} %get-tuple-element.202) | copy-start | bytes 4718596
  108.5 41.3 %copy-start.44 = (f32[512]{0:T(512)}, f32[512]{0:T(512)S(1)}, u32[]{:S(2)}) copy-start(f32[512]{0:T(512)S(1)} %broadcast_multiply_fusion.1) | copy-start | bytes 6148
  108.8 40.9 %copy-start.59 = (f32[512]{0:T(512)}, f32[512]{0:T(512)S(1)}, u32[]{:S(2)}) copy-start(f32[512]{0:T(512)S(1)} %fusion.79) | copy-start | bytes 6148
  150.4 69.8 %copy-start.48 = (f32[512]{0:T(512)}, f32[512]{0:T(512)S(1)}, u32[]{:S(2)}) copy-start(f32[512]{0:T(512)S(1)} %negate_multiply_fusion.1) | copy-start | bytes 6148
  203.6 262.6 %reduce-scatter.17.cloned.1.call-start = ((), (), s32[]{:S(2)}) async-start(), calls=%async_computation.9 | async-start | bytes 2433024 | tf_op jit(solution)/shard_map/reduce_scatter | solution.py:317
  222.5 243.7 %reduce-scatter.23.cloned.1.call-start = ((), (), s32[]{:S(2)}) async-start(), calls=%async_computation.12 | async-start | bytes 2433024
  257.1 289.0 %reduce-scatter.27.cloned.1.call-start = ((), (), s32[]{:S(2)}) async-start(), calls=%async_computation.14 | async-start | bytes 2433024
  270.9 22.1 %copy-start.71 = (s32[128]{0:T(128)S(1)}, s32[128]{0:T(128)}, u32[]{:S(2)}) copy-start(s32[128]{0:T(128)} %add_bitcast_fusion.3) | copy-start | bytes 1540
  272.5 38.8 %copy-start.70 = (s32[128]{0:T(128)S(1)}, s32[128]{0:T(128)}, u32[]{:S(2)}) copy-start(s32[128]{0:T(128)} %add_bitcast_fusion.2) | copy-start | bytes 1540
  274.6 54.9 %copy-start.69 = (s32[128]{0:T(128)S(1)}, s32[128]{0:T(128)}, u32[]{:S(2)}) copy-start(s32[128]{0:T(128)} %add_bitcast_fusion.1) | copy-start | bytes 1540
  293.0 54.7 %copy-start.68 = (s32[128]{0:T(128)S(1)}, s32[128]{0:T(128)}, u32[]{:S(2)}) copy-start(s32[128]{0:T(128)} %add_bitcast_fusion) | copy-start | bytes 1540
  368.2 4.6 collective-permute-start.2
  370.5 3.4 collective-permute-start.3
  383.7 266.2 %reduce-scatter.25.cloned.1.call-start = ((), (), s32[]{:S(2)}) async-start(), calls=%async_computation.13 | async-start | bytes 2433024
  390.5 401.3 %reduce-scatter.19.cloned.1.call-start = ((), (), s32[]{:S(2)}) async-start(), calls=%async_computation.10 | async-start | bytes 9732096 | tf_op jit(solution)/shard_map/reduce_scatter | solution.py:318
  399.7 533.4 %reduce-scatter.21.cloned.1.call-start = ((), (), s32[]{:S(2)}) async-start(), calls=%async_computation.11 | async-start | bytes 9732096 | tf_op jit(solution)/shard_map/reduce_scatter | solution.py:319
  410.6 52.0 %copy-start.49 = (f32[512]{0:T(512)S(1)}, f32[512]{0:T(512)}, u32[]{:S(2)}) copy-start(f32[512]{0:T(512)} %copy-done.48) | copy-start | bytes 6148
  459.9 473.2 %copy-start.1 = (bf16[768,768]{1,0:T(8,128)(2,1)S(1)}, bf16[768,768]{1,0:T(8,128)(2,1)}, u32[]{:S(2)}) copy-start(bf16[768,768]{1,0:T(8,128)(2,1)} %param.23) | copy-start | bytes 3538948
  (77 other events, 575.3 us)
Sparse Core Ops, SparseCore 0:
  48.0 24.2 all-gather.1
  203.7 28.1 reduce-scatter.14
  238.6 99.0 reduce-scatter.16
  343.5 98.0 reduce-scatter.22
  448.1 98.0 reduce-scatter.26
  551.9 97.9 reduce-scatter.24
  657.4 134.4 reduce-scatter.18
  798.3 134.7 reduce-scatter.20
where the time goes:
time: 948 us; the launch traced here: 940 us
  waiting for transfers between devices  473 us (50%)
  matrix products  156 us (16%)
  other arithmetic  155 us (16%)
  local copies, waits for them, and re-layouts  89.7 us (9%)
  blocking collectives  42.9 us (5%)
  between operations  15.6 us (2%)
    unnamed x11, waiting for transfers between devices  184 us
    reduce_scatter x1, waiting for transfers between devices, per_device(): lax.psum_scatter(grad_in_weight, ('seq', 'dp'), scatter_dimension=0, tile...  142 us
    reduce_scatter x1, waiting for transfers between devices, per_device(): lax.psum_scatter(grad_back_weight, ('seq', 'dp'), scatter_dimension=0, ti...  141 us
    scatter-add x5, other arithmetic, per_device(): halo_grad.at[:, :, begin:begin + tok_count:4]  89.7 us
    unnamed x1, blocking collectives  42.9 us
    unnamed x186, local copies, waits for them, and re-layouts  25.5 us
    dot_general x1, matrix products, per_device(): inner = jnp.dot(first_low, w_in, preferred_element_type=jnp.float32)  20.2 us
  transfers between devices with their start and end apart: 12, of which 6 were waited for; matrix products, arithmetic and copies ran while one was open for 26% of the time, Pallas kernels for 0%

commit v1 on v0

--- a/solution.py
+++ b/solution.py
@@ -32,6 +32,35 @@
     size = lax.axis_size(axis)
     pairs = [(i, i + by) for i in range(size) if 0 <= i + by < size]
     return lax.ppermute(shard, axis, pairs)
+
+
+def swap_stage(parts, dim, axis, count, stride):
+    size = lax.axis_size(axis)
+    me = lax.axis_index(axis)
+    mine = (me // stride) % count
+    total = lax.dynamic_index_in_dim(parts, mine, dim, keepdims=False)
+    for hop in range(1, count):
+        pairs = []
+        for device in range(size):
+            place = (device // stride) % count
+            pairs.append((device, device + ((place + hop) % count - place) * stride))
+        block = lax.dynamic_index_in_dim(parts, (mine + hop) % count, dim, keepdims=False)
+        total = total + lax.ppermute(block.astype(jnp.bfloat16), axis, pairs).astype(jnp.float32)
+    return total
+
+
+def scatter_sum(grad, seq_first):
+    seq, dp = lax.axis_size("seq"), lax.axis_size("dp")
+    rows = grad.shape[0] // (seq * dp)
+    parts = grad.reshape(seq // 2, 2, dp // 2, 2, rows, grad.shape[1])
+    parts = swap_stage(parts, 1, "seq", 2, 1)
+    if seq_first:
+        parts = swap_stage(parts, 0, "seq", seq // 2, 2)
+        parts = swap_stage(parts, 1, "dp", 2, 1)
+    else:
+        parts = swap_stage(parts, 2, "dp", 2, 1)
+        parts = swap_stage(parts, 0, "seq", seq // 2, 2)
+    return swap_stage(parts, 0, "dp", dp // 2, 2)
 
 
 def layer_norm(values, gain, offset):
@@ -310,18 +339,33 @@
         "ne,de->nd", value_grad, w_value, preferred_element_type=jnp.float32
     )
     tokens_grad = input_grad.astype(jnp.bfloat16).reshape(row_count, tok_count, model_width)
+    small = jnp.concatenate(
+        [
+            jnp.stack([grad_gain_one, grad_bias_one, grad_gain_two, grad_bias_two], axis=1),
+            grad_pool,
+            jnp.zeros((model_width, 128 - 9), jnp.float32),
+        ],
+        axis=1,
+    )
+    sum_in = scatter_sum(grad_in_weight, True)
+    sum_back = scatter_sum(grad_back_weight, False)
+    sum_out = scatter_sum(jnp.concatenate([grad_out_weight, small], axis=1), True)
+    sum_value = scatter_sum(grad_value_weight, False)
+    sum_query = scatter_sum(grad_query_weight, False)
+    sum_key = scatter_sum(grad_key_weight, True)
+    vectors = sum_out[:, model_width:]
     summed = (
-        lax.psum_scatter(grad_query_weight, ("seq", "dp"), scatter_dimension=0, tiled=True),
-        lax.psum_scatter(grad_key_weight, ("seq", "dp"), scatter_dimension=0, tiled=True),
-        lax.psum_scatter(grad_value_weight, ("seq", "dp"), scatter_dimension=0, tiled=True),
-        lax.psum_scatter(grad_out_weight, ("seq", "dp"), scatter_dimension=0, tiled=True),
-        lax.psum_scatter(grad_in_weight, ("seq", "dp"), scatter_dimension=0, tiled=True),
-        lax.psum_scatter(grad_back_weight, ("seq", "dp"), scatter_dimension=0, tiled=True),
-        lax.psum_scatter(grad_gain_one, ("seq", "dp"), scatter_dimension=0, tiled=True),
-        lax.psum_scatter(grad_bias_one, ("seq", "dp"), scatter_dimension=0, tiled=True),
-        lax.psum_scatter(grad_gain_two, ("seq", "dp"), scatter_dimension=0, tiled=True),
-        lax.psum_scatter(grad_bias_two, ("seq", "dp"), scatter_dimension=0, tiled=True),
-        lax.psum_scatter(grad_pool, ("seq", "dp"), scatter_dimension=0, tiled=True),
+        sum_query,
+        sum_key,
+        sum_value,
+        sum_out[:, :model_width],
+        sum_in,
+        sum_back,
+        vectors[:, 0],
+        vectors[:, 1],
+        vectors[:, 2],
+        vectors[:, 3],
+        vectors[:, 4:9],
     )
     return (
         mixed,

time: 948 us -> 545 us (0.57)
  waiting for transfers between devices: 473 us -> 38.6 us
  starting transfers between devices: 8.1 us -> 56 us
  blocking collectives: 42.9 us -> 0 us
  local copies, waits for them, and re-layouts: 89.7 us -> 114 us
  matrix products: 156 us -> 140 us
  other arithmetic: 155 us -> 171 us
    reduce_scatter x3 -> x0, waiting for transfers between devices: 283 us -> none  [the longest x1 142 us: per_device(): lax.psum_scatter(grad_in_weight, ('seq', 'dp'), scatter_dimension=0, tile...]
    unnamed x11 -> x2, waiting for transfers between devices: 184 us -> 0.03 us
    ppermute x0 -> x36, starting transfers between devices: none -> 48.2 us  [swap_stage(): lax.ppermute(block.astype(jnp.bfloat16), axis, pairs).astype(jnp.float32)]
    unnamed x1 -> x0, blocking collectives: 42.9 us -> none
    ppermute x0 -> x36, waiting for transfers between devices: none -> 35.6 us  [swap_stage(): lax.ppermute(block.astype(jnp.bfloat16), axis, pairs).astype(jnp.float32)]
    add x0 -> x24, other arithmetic: none -> 19.2 us  [swap_stage(): total + lax.ppermute(block.astype(jnp.bfloat16), axis, pairs).astype(jnp....]
    unnamed x186 -> x173, local copies, waits for them, and re-layouts: 25.5 us -> 8.1 us
    concatenate x0 -> x10, local copies, waits for them, and re-layouts: none -> 14.9 us  [per_device(): jnp.concatenate([grad_out_weight, small], axis=1)]
  transfers between devices with their start and end apart: 12 -> 42, of which waited for: 6 -> 14; matrix products, arithmetic and copies ran while one was open for 26% -> 48% of each run, Pallas kernels for 0% -> 0%
where the time goes in v1:
time: 545 us; the launch traced here: 536 us
  other arithmetic  171 us (31%)
  matrix products  140 us (26%)
  local copies, waits for them, and re-layouts  114 us (21%)
  starting transfers between devices  56 us (10%)
  waiting for transfers between devices  38.6 us (7%)
  between operations  15.7 us (3%)
    scatter-add x5, other arithmetic, per_device(): halo_grad.at[:, :, begin:begin + tok_count:4]  87.6 us
    ppermute x36, starting transfers between devices, swap_stage(): lax.ppermute(block.astype(jnp.bfloat16), axis, pairs).astype(jnp.float32)  48.2 us
    ppermute x36, waiting for transfers between devices, swap_stage(): lax.ppermute(block.astype(jnp.bfloat16), axis, pairs).astype(jnp.float32)  35.6 us
    slice x5, local copies, waits for them, and re-layouts, per_device(): taken = pair_halo[:, :, begin:begin + tok_count:4].astype(jnp.float32)  25.6 us
    add x24, other arithmetic, swap_stage(): total + lax.ppermute(block.astype(jnp.bfloat16), axis, pairs).astype(jnp....  19.2 us
    dot_general x1, matrix products, per_device(): inner = jnp.dot(first_low, w_in, preferred_element_type=jnp.float32)  18 us
    concatenate x10, local copies, waits for them, and re-layouts, per_device(): jnp.concatenate([grad_out_weight, small], axis=1)  14.9 us
    dot_general x1, matrix products, attend_backward(): jnp.einsum('gthe,gkhe->ghtk', grad_heads, value_heads, preferred_element_...  14.4 us
  transfers between devices with their start and end apart: 42, of which 14 were waited for; matrix products, arithmetic and copies ran while one was open for 48% of the time, Pallas kernels for 0%

profile of v1, /device:TPU:0, one launch (start us, length us, event | category | flops | bytes accessed | tf_op | source)
XLA Modules:
  0.0 536.3 jit_solution(7189669277972914637)
XLA Ops:
  75.3 7.7 %fusion.157 = (f32[12,512]{1,0:T(8,128)}, f32[12,512,640]{2,1,0:T(8,128)}) fusion(bf16[512,12,64]{0,2,1:T(8,128)(2,1)S(1)} %bitcast.341, bf16[640,12,64]{0,2,1:T(8,128)(2,1)S(1)} %bitcast.356, pred[512,640]{1,0:T(8,128)(4,1)S(1)} %fusion.30), kind=kOutput, calls=%fused_computation.338 | convolution fusion | flops 515106816 | bytes 17850368 | tf_op jit(solution)/shard_map/while/body/eval_jaxpr/gthe,gkhe->ghtk/dot_general | solution.py:80
  96.0 7.4 %fusion = f32[12,512]{1,0:T(8,128)S(1)} fusion(f32[12,512,640]{2,1,0:T(8,128)} %get-tuple-element.202, f32[12,512]{1,0:T(8,128)S(1)} %max.14), kind=kLoop, calls=%fused_computation.11 | loop fusion | flops 7858176 | bytes 15777792 | tf_op jit(solution)/shard_map/while/body/eval_jaxpr/reduce_sum | solution.py:102
  104.4 6.5 %fusion.17 = f32[12,64,512]{2,1,0:T(8,128)S(1)} fusion(bf16[512,12,64]{0,2,1:T(8,128)(2,1)S(1)} %bitcast.371, f32[12,512]{1,0:T(8,128)S(1)} %get-tuple-element.153, f32[12,512]{1,0:T(8,128)S(1)} %max.14, f32[12,512,512]{1,2,0:T(8,128)} %copy-done.2, pred[512,512]{0,1:T(8,128)(4,1)S(1)} %fusion.37), kind=kOutput, calls=%fused_computation.43 | convolution fusion | flops 418381824 | bytes 15253504 | tf_op jit(solution)/shard_map/while/body/eval_jaxpr/ghtk,gkhe->gthe/dot_general | solution.py:108
  111.0 7.8 %add_convert_fusion.3 = bf16[12,64,512]{2,1,0:T(8,128)(2,1)S(1)} fusion(f32[12,64,512]{2,1,0:T(8,128)S(1)} %fusion.17, bf16[640,12,64]{0,2,1:T(8,128)(2,1)S(1)} %bitcast.369, f32[12,512,640]{2,1,0:T(8,128)} %get-tuple-element.202, f32[12,512]{1,0:T(8,128)S(1)} %get-tuple-element.153, f32[12,512]{1,0:T(8,128)S(1)} %max.14), kind=kOutput, calls=%fused_computation.90 | convolution fusion | flops 515899392 | bytes 19120128 | tf_op jit(solution)/shard_map/while/body/eval_jaxpr/ghtk,gkhe->gthe/dot_general | solution.py:105
  120.2 18.0 %multiply_convert_fusion.2 = (bf16[512,3072]{1,0:T(8,128)(2,1)S(1)}, f32[512,3072]{1,0:T(8,128)}, f32[512,3072]{1,0:T(8,128)}) fusion(bf16[768,3072]{1,0:T(8,128)(2,1)S(1)} %bitcast.389, f32[512,768]{1,0:T(8,128)S(1)} %get-tuple-element.206, f32[768]{0:T(1024)S(1)} %copy-done.72, f32[768]{0:T(1024)S(1)} %copy-done.64, f32[512]{0:T(512)S(1)} %fusion.132, ...), kind=kOutput, calls=%fused_computation.29 | convolution fusion | flops 2520121344 | bytes 22030336 | tf_op jit(solution)/shard_map/dot_general | solution.py:263
  148.9 8.5 %add_convert_fusion = bf16[512,3072]{1,0:T(8,128)(2,1)} fusion(f32[512,3072]{1,0:T(8,128)} %get-tuple-element.159, f32[512,3072]{1,0:T(8,128)} %get-tuple-element.207, bf16[3072,768]{1,0:T(8,128)(2,1)S(1)} %bitcast.387, f32[512,768]{1,0:T(8,128)S(1)} %get-tuple-element.157, f32[512]{0:T(512)S(1)} %negate_multiply_fusion.2), kind=kOutput, calls=%fused_computation.28 | convolution fusion | flops 2438725632 | bytes 22022144 | tf_op jit(solution)/shard_map/nd,fd->nf/dot_general | solution.py:275
  157.4 7.3 %fusion.145 = f32[768,3072]{1,0:T(8,128)} fusion(bf16[512,3072]{1,0:T(8,128)(2,1)} %add_convert_fusion, f32[512,768]{1,0:T(8,128)S(1)} %get-tuple-element.206, f32[768]{0:T(1024)S(1)} %copy-done.72, f32[768]{0:T(1024)S(1)} %copy-done.64, f32[512]{0:T(512)S(1)} %fusion.132, f32[512]{0:T(512)S(1)} %broadcast_multiply_fusion.1), kind=kOutput, calls=%fused_computation.329 | convolution fusion | flops 2417885184 | bytes 14166016 | tf_op jit(solution)/shard_map/nd,nf->df/dot_general | solution.py:278
  171.7 11.4 %multiply_reduce_fusion.1 = (f32[12,512]{1,0:T(8,128)S(1)}, f32[12,512,512]{1,2,0:T(8,128)}) fusion(f32[12,512]{1,0:T(8,128)} %get-tuple-element.152, f32[12,512,512]{1,2,0:T(8,128)} %copy-done.2, pred[512,512]{0,1:T(8,128)(4,1)} %copy-done.20, bf16[512,12,64]{0,2,1:T(8,128)(2,1)S(1)} %bitcast.349, bf16[512,12,64]{0,2,1:T(8,128)(2,1)} %bitcast.372), kind=kOutput, calls=%fused_computation.13 | convolution fusion | flops 418375680 | bytes 27049984 | tf_op jit(solution)/shard_map/while/body/eval_jaxpr/gthe,gkhe->ghtk/dot_general | solution.py:129
  183.2 14.4 %multiply_reduce_fusion = (f32[12,512]{1,0:T(8,128)S(1)}, f32[12,512,640]{2,1,0:T(8,128)}) fusion(f32[12,512,640]{2,1,0:T(8,128)} %get-tuple-element.202, f32[12,512]{1,0:T(8,128)S(1)} %copy-done.42, bf16[512,12,64]{0,2,1:T(8,128)(2,1)S(1)} %bitcast.350, bf16[640,12,64]{0,2,1:T(8,128)(2,1)S(1)} %bitcast.370), kind=kOutput, calls=%fused_computation.6 | convolution fusion | flops 515106816 | bytes 33275904 | tf_op jit(solution)/shard_map/while/body/eval_jaxpr/gthe,gkhe->ghtk/dot_general | solution.py:126
  201.7 7.1 %multiply_convert_fusion.1 = bf16[12,512,512]{1,2,0:T(8,128)(2,1)S(1)} fusion(f32[12,512,512]{1,2,0:T(8,128)} %get-tuple-element.214, f32[12,512]{1,0:T(8,128)S(1)} %add.592, f32[12,512]{1,0:T(8,128)S(1)} %copy-done.42, f32[12,512,512]{1,2,0:T(8,128)S(1)} %bitcast.338, pred[512,512]{0,1:T(8,128)(4,1)S(1)} %copy-done.21), kind=kLoop, calls=%fused_computation.12 | loop fusion | flops 18874368 | bytes 31768576 | tf_op jit(solution)/shard_map/while/body/eval_jaxpr/convert_element_type | solution.py:134
  230.0 11.8 %multiply_convert_fusion = bf16[12,512,640]{2,1,0:T(8,128)(2,1)S(1)} fusion(f32[12,512,640]{2,1,0:T(8,128)} %get-tuple-element.212, f32[12,512,640]{2,1,0:T(8,128)} %get-tuple-element.202, f32[12,512]{1,0:T(8,128)S(1)} %add.592, f32[12,512]{1,0:T(8,128)S(1)} %copy-done.42), kind=kLoop, calls=%fused_computation.5 | loop fusion | flops 15728640 | bytes 39370752 | tf_op jit(solution)/shard_map/while/body/eval_jaxpr/convert_element_type | solution.py:133
  250.8 6.3 %multiply_convert_fusion.4 = bf16[12,64,512]{2,1,0:T(8,128)(2,1)S(1)} fusion(f32[12,64,512]{2,1,0:T(8,128)} %fusion.160, bf16[640,12,64]{0,2,1:T(8,128)(2,1)S(1)} %bitcast.357, bf16[12,512,640]{2,1,0:T(8,128)(2,1)} %copy-done.3), kind=kOutput, calls=%fused_computation.84 | convolution fusion | flops 504496128 | bytes 11206656 | tf_op jit(solution)/shard_map/while/body/eval_jaxpr/ghtk,gkhe->gthe/dot_general | solution.py:135
  259.8 8.2 %fusion.4 = f32[12,64,640]{2,1,0:T(8,128)} fusion(bf16[512,12,64]{0,2,1:T(8,128)(2,1)S(1)} %bitcast.352, f32[12,512,640]{2,1,0:T(8,128)} %get-tuple-element.202, f32[12,512]{1,0:T(8,128)S(1)} %copy-done.42), kind=kOutput, calls=%fused_computation.22 | convolution fusion | flops 511180800 | bytes 18505728 | tf_op jit(solution)/shard_map/while/body/eval_jaxpr/ghtk,gthe->gkhe/dot_general | solution.py:146
  276.4 7.1 %maximum_bitcast_fusion = f32[2,640,768]{2,0,1:T(2,128)} fusion(f32[1,1,640,768]{3,1,2,0:T(1,128)} %copy.115, f32[1,1,640,768]{3,1,2,0:T(1,128)S(1)} %copy-done.12), kind=kLoop, calls=%fused_computation.49 | loop fusion | flops 983040 | bytes 7864320 | tf_op jit(solution)/shard_map/while/body/eval_jaxpr/stack | solution.py:157
  310.2 6.2 %bitcast_add_fusion.1 = f32[2,4,2,24,3072]{4,3,1,2,0:T(8,128)} fusion(bf16[2,4,2,24,3072]{4,3,1,2,0:T(8,128)(2,1)} %collective-permute-done.28, f32[2,2,4,2,24,3072]{5,4,3,2,1,0:T(8,128)} %bitcast.366, s32[]{:T(128)S(6)} %select_n.293), kind=kLoop, calls=%fused_computation.47 | loop fusion | flops 2359296 | bytes 11796484 | tf_op jit(solution)/shard_map/add | solution.py:48
  324.7 18.2 %scatter_fusion = f32[2,640,768]{2,0,1:T(2,128)} fusion(f32[2,640,768]{2,0,1:T(2,128)} %maximum_bitcast_fusion, s32[128]{0:T(128)S(1)} %copy-done.69, f32[128,2,768]{2,1,0:T(2,128)} %copy.120), kind=kCustom, calls=%fused_computation | custom fusion | flops 196608 | bytes 2359808 | tf_op jit(solution)/shard_map/scatter-add | solution.py:307
  342.9 18.2 %scatter_fusion.1 = f32[2,640,768]{2,0,1:T(2,128)} fusion(f32[2,640,768]{2,0,1:T(2,128)} %scatter_fusion, s32[128]{0:T(128)S(1)} %copy-done.68, f32[128,2,768]{2,1,0:T(2,128)} %copy.121), kind=kCustom, calls=%fused_computation.1 | custom fusion | flops 196608 | bytes 2359808 | tf_op jit(solution)/shard_map/scatter-add | solution.py:307
  361.1 18.2 %scatter_fusion.2 = f32[2,640,768]{2,0,1:T(2,128)} fusion(f32[2,640,768]{2,0,1:T(2,128)} %scatter_fusion.1, s32[128]{0:T(128)S(1)} %copy-done.67, f32[128,2,768]{2,1,0:T(2,128)} %copy.122), kind=kCustom, calls=%fused_computation.2 | custom fusion | flops 196608 | bytes 2359808 | tf_op jit(solution)/shard_map/scatter-add | solution.py:307
  379.3 16.5 %scatter_fusion.3 = f32[2,640,768]{2,0,1:T(2,128)} fusion(f32[2,640,768]{2,0,1:T(2,128)} %scatter_fusion.2, s32[128]{0:T(128)S(1)} %copy-done.66, f32[128,2,768]{2,1,0:T(2,128)S(1)} %copy.123), kind=kCustom, calls=%fused_computation.3 | custom fusion | flops 196608 | bytes 2359808 | tf_op jit(solution)/shard_map/scatter-add | solution.py:307
  395.8 16.5 %scatter_fusion.4 = f32[2,640,768]{2,0,1:T(2,128)} fusion(f32[2,640,768]{2,0,1:T(2,128)} %scatter_fusion.3, s32[128]{0:T(128)S(1)} %copy-done.65, f32[128,2,768]{2,1,0:T(2,128)S(1)} %copy.124), kind=kCustom, calls=%fused_computation.4 | custom fusion | flops 196608 | bytes 2359808 | tf_op jit(solution)/shard_map/scatter-add | solution.py:307
  429.4 5.8 %concatenate.46 = f32[2,2,4,2,24,896]{5,4,3,2,1,0:T(8,128)} concatenate(f32[2,2,4,2,24,768]{5,4,3,2,1,0:T(8,128)} %fusion.71, f32[2,2,4,2,24,1]{5,4,3,2,1,0:T(8,128)S(1)} %copy-done.36, f32[2,2,4,2,24,1]{5,4,3,2,1,0:T(8,128)S(1)} %copy-done.37, f32[2,2,4,2,24,1]{5,4,3,2,1,0:T(8,128)S(1)} %copy-done.38, f32[2,2,4,2,24,1]{5,4,3,2,1,0:T(8,128)S(1)} %copy-done.35, ...), dimensions={5} | concatenate | bytes 5505024 | tf_op jit(solution)/shard_map/concatenate | solution.py:352
  446.6 9.8 %collective-permute-start.16 = (bf16[2,4,2,24,768]{4,3,1,0,2:T(8,128)(2,1)S(1)}, bf16[2,4,2,24,768]{4,3,1,0,2:T(8,128)(2,1)S(1)}, u32[]{:S(2)}, u32[]{:S(2)}) collective-permute-start(bf16[2,4,2,24,768]{4,3,1,0,2:T(8,128)(2,1)S(1)} %fusion.85), channel_id=1, source_target_pairs={{0,8},{8,0},{16,24},{24,16},{1,9},{9,1},{17,25},{25,17},{2,10},{10... | collective-permute-start | bytes 1769480 | tf_op jit(solution)/shard_map/ppermute | solution.py:48
  469.6 9.5 %collective-permute-done.36 = bf16[4,96,768]{2,1,0:T(8,128)(2,1)S(1)} collective-permute-done((bf16[4,96,768]{2,1,0:T(8,128)(2,1)S(1)}, bf16[4,96,768]{2,1,0:T(8,128)(2,1)S(1)}, u32[]{:S(2)}, u32[]{:S(2)}) %collective-permute-start.36) | collective-permute-done | bytes 589856 | tf_op jit(solution)/shard_map/ppermute | solution.py:48
  494.6 6.6 %collective-permute-done.32 = bf16[24,3072]{1,0:T(8,128)(2,1)S(1)} collective-permute-done((bf16[24,3072]{1,0:T(8,128)(2,1)S(1)}, bf16[24,3072]{1,0:T(8,128)(2,1)S(1)}, u32[]{:S(2)}, u32[]{:S(2)}) %collective-permute-start.32) | collective-permute-done | bytes 147488 | tf_op jit(solution)/shard_map/ppermute | solution.py:48
  (415 shorter events, 265.7 us)
Async XLA Ops:
  7.2 78.1 %all-gather.2.cloned.1.call-start = ((), (), s32[]{:S(2)}) async-start(), calls=%async_computation.1 | async-start | bytes 1966080 | tf_op jit(solution)/shard_map/all_gather | solution.py:241
  11.3 24.8 %collective-permute-start = (bf16[1,2,64,768]{3,2,1,0:T(8,128)(2,1)}, bf16[1,2,64,768]{3,2,1,0:T(8,128)(2,1)}, u32[]{:S(2)}, u32[]{:S(2)}) collective-permute-start(bf16[1,2,64,768]{3,2,1,0:T(8,128)(2,1)} %get-tuple-element.171), channel_id=1, source_target_pairs={{0,8},{8,16},{16,24},{1,9},{9,17},{17,25},{2,10},{10,18},{18,26},{... | collective-permute-start | bytes 589832 | tf_op jit(solution)/shard_map/ppermute | solution.py:22
  14.3 21.8 %collective-permute-start.1 = (bf16[1,2,64,768]{3,2,1,0:T(8,128)(2,1)}, bf16[1,2,64,768]{3,2,1,0:T(8,128)(2,1)}, u32[]{:S(2)}, u32[]{:S(2)}) collective-permute-start(bf16[1,2,64,768]{3,2,1,0:T(8,128)(2,1)} %get-tuple-element.172), channel_id=1, source_target_pairs={{8,0},{16,8},{24,16},{9,1},{17,9},{25,17},{10,2},{18,10},{26,18},{... | collective-permute-start | bytes 589832 | tf_op jit(solution)/shard_map/ppermute | solution.py:24
  61.5 254.9 %reduce-scatter.2.cloned.1.call-start = ((), (), s32[]{:S(2)}) async-start(), calls=%async_computation.2 | async-start | bytes 1966080 | tf_op jit(solution)/shard_map/reduce_scatter | solution.py:297
  218.1 83.6 %collective-permute-start.34 = (bf16[2,4,2,96,768]{4,3,1,0,2:T(8,128)(2,1)}, bf16[2,4,2,96,768]{4,3,1,0,2:T(8,128)(2,1)}, u32[]{:S(2)}, u32[]{:S(2)}) collective-permute-start(bf16[2,4,2,96,768]{4,3,1,0,2:T(8,128)(2,1)} %fusion.20), channel_id=1, source_target_pairs={{0,8},{8,0},{16,24},{24,16},{1,9},{9,1},{17,25},{25,17},{2,10},{10... | collective-permute-start | bytes 7077896 | tf_op jit(solution)/shard_map/ppermute | solution.py:48
  222.5 87.7 %collective-permute-start.28 = (bf16[2,4,2,24,3072]{4,3,1,2,0:T(8,128)(2,1)}, bf16[2,4,2,24,3072]{4,3,1,2,0:T(8,128)(2,1)}, u32[]{:S(2)}, u32[]{:S(2)}) collective-permute-start(bf16[2,4,2,24,3072]{4,3,1,2,0:T(8,128)(2,1)} %fusion.19), channel_id=1, source_target_pairs={{0,8},{8,0},{16,24},{24,16},{1,9},{9,1},{17,25},{25,17},{2,10},{10... | collective-permute-start | bytes 7077896 | tf_op jit(solution)/shard_map/ppermute | solution.py:48
  259.4 13.7 %collective-permute-start.4 = (bf16[2,4,2,24,768]{4,3,1,0,2:T(8,128)(2,1)S(1)}, bf16[2,4,2,24,768]{4,3,1,0,2:T(8,128)(2,1)}, u32[]{:S(2)}, u32[]{:S(2)}) collective-permute-start(bf16[2,4,2,24,768]{4,3,1,0,2:T(8,128)(2,1)S(1)} %fusion.83), channel_id=1, source_target_pairs={{0,8},{8,0},{16,24},{24,16},{1,9},{9,1},{17,25},{25,17},{2,10},{10... | collective-permute-start | bytes 1769480 | tf_op jit(solution)/shard_map/ppermute | solution.py:48
  308.7 152.5 %collective-permute-start.35 = (bf16[2,4,96,768]{3,2,1,0:T(8,128)(2,1)}, bf16[2,4,96,768]{3,2,1,0:T(8,128)(2,1)}, u32[]{:S(2)}, u32[]{:S(2)}) collective-permute-start(bf16[2,4,96,768]{3,2,1,0:T(8,128)(2,1)} %fusion.36), channel_id=1, source_target_pairs={{0,1},{1,0},{2,3},{3,2},{4,5},{5,4},{6,7},{7,6},{8,9},{9,8},{10,11... | collective-permute-start | bytes 3538952 | tf_op jit(solution)/shard_map/ppermute | solution.py:48
  416.9 24.2 %collective-permute-start.2 = (bf16[1,2,64,768]{3,1,2,0:T(2,128)(2,1)}, bf16[1,2,64,768]{3,1,2,0:T(2,128)(2,1)}, u32[]{:S(2)}, u32[]{:S(2)}) collective-permute-start(bf16[1,2,64,768]{3,1,2,0:T(2,128)(2,1)} %get-tuple-element.165), channel_id=1, source_target_pairs={{0,8},{8,16},{16,24},{1,9},{9,17},{17,25},{2,10},{10,18},{18,26},{... | collective-permute-start | bytes 589832 | tf_op jit(solution)/shard_map/ppermute | solution.py:34
  421.9 41.1 %collective-permute-start.29 = (bf16[4,2,24,3072]{3,2,0,1:T(8,128)(2,1)}, bf16[4,2,24,3072]{3,2,0,1:T(8,128)(2,1)}, u32[]{:S(2)}, u32[]{:S(2)}) collective-permute-start(bf16[4,2,24,3072]{3,2,0,1:T(8,128)(2,1)} %fusion.35), channel_id=1, source_target_pairs={{0,16},{8,24},{16,0},{24,8},{1,17},{9,25},{17,1},{25,9},{2,18},{10... | collective-permute-start | bytes 3538952 | tf_op jit(solution)/shard_map/ppermute | solution.py:48
  436.6 28.7 %collective-permute-start.22 = (bf16[2,4,2,24,896]{4,3,2,1,0:T(8,128)(2,1)S(1)}, bf16[2,4,2,24,896]{4,3,2,1,0:T(8,128)(2,1)S(1)}, u32[]{:S(2)}, u32[]{:S(2)}) collective-permute-start(bf16[2,4,2,24,896]{4,3,2,1,0:T(8,128)(2,1)S(1)} %fusion.80), channel_id=1, source_target_pairs={{0,8},{8,0},{16,24},{24,16},{1,9},{9,1},{17,25},{25,17},{2,10},{10... | collective-permute-start | bytes 2064392 | tf_op jit(solution)/shard_map/ppermute | solution.py:48
  446.6 20.9 %collective-permute-start.16 = (bf16[2,4,2,24,768]{4,3,1,0,2:T(8,128)(2,1)S(1)}, bf16[2,4,2,24,768]{4,3,1,0,2:T(8,128)(2,1)S(1)}, u32[]{:S(2)}, u32[]{:S(2)}) collective-permute-start(bf16[2,4,2,24,768]{4,3,1,0,2:T(8,128)(2,1)S(1)} %fusion.85), channel_id=1, source_target_pairs={{0,8},{8,0},{16,24},{24,16},{1,9},{9,1},{17,25},{25,17},{2,10},{10... | collective-permute-start | bytes 1769480 | tf_op jit(solution)/shard_map/ppermute | solution.py:48
  457.3 11.9 %collective-permute-start.10 = (bf16[2,4,2,24,768]{4,3,1,2,0:T(8,128)(2,1)S(1)}, bf16[2,4,2,24,768]{4,3,1,2,0:T(8,128)(2,1)S(1)}, u32[]{:S(2)}, u32[]{:S(2)}) collective-permute-start(bf16[2,4,2,24,768]{4,3,1,2,0:T(8,128)(2,1)S(1)} %fusion.84), channel_id=1, source_target_pairs={{0,8},{8,0},{16,24},{24,16},{1,9},{9,1},{17,25},{25,17},{2,10},{10... | collective-permute-start | bytes 1769480 | tf_op jit(solution)/shard_map/ppermute | solution.py:48
  462.9 16.2 %collective-permute-start.36 = (bf16[4,96,768]{2,1,0:T(8,128)(2,1)S(1)}, bf16[4,96,768]{2,1,0:T(8,128)(2,1)S(1)}, u32[]{:S(2)}, u32[]{:S(2)}) collective-permute-start(bf16[4,96,768]{2,1,0:T(8,128)(2,1)S(1)} %fusion.82), channel_id=1, source_target_pairs={{0,16},{8,24},{16,0},{24,8},{1,17},{9,25},{17,1},{25,9},{2,18},{10... | collective-permute-start | bytes 1769480 | tf_op jit(solution)/shard_map/ppermute | solution.py:48
  464.8 16.2 %collective-permute-start.30 = (bf16[4,24,3072]{2,1,0:T(8,128)(2,1)S(1)}, bf16[4,24,3072]{2,1,0:T(8,128)(2,1)S(1)}, u32[]{:S(2)}, u32[]{:S(2)}) collective-permute-start(bf16[4,24,3072]{2,1,0:T(8,128)(2,1)S(1)} %fusion.81), channel_id=1, source_target_pairs={{0,1},{1,0},{2,3},{3,2},{4,5},{5,4},{6,7},{7,6},{8,9},{9,8},{10,11... | collective-permute-start | bytes 1769480 | tf_op jit(solution)/shard_map/ppermute | solution.py:48
  465.6 20.9 %collective-permute-start.23 = (bf16[4,2,24,896]{3,2,1,0:T(8,128)(2,1)S(1)}, bf16[4,2,24,896]{3,2,1,0:T(8,128)(2,1)S(1)}, u32[]{:S(2)}, u32[]{:S(2)}) collective-permute-start(bf16[4,2,24,896]{3,2,1,0:T(8,128)(2,1)S(1)} %fusion.88), channel_id=1, source_target_pairs={{0,16},{8,24},{16,0},{24,8},{1,17},{9,25},{17,1},{25,9},{2,18},{10... | collective-permute-start | bytes 1032200 | tf_op jit(solution)/shard_map/ppermute | solution.py:48
  467.7 19.6 %collective-permute-start.17 = (bf16[2,4,24,768]{3,2,1,0:T(8,128)(2,1)S(1)}, bf16[2,4,24,768]{3,2,1,0:T(8,128)(2,1)S(1)}, u32[]{:S(2)}, u32[]{:S(2)}) collective-permute-start(bf16[2,4,24,768]{3,2,1,0:T(8,128)(2,1)S(1)} %fusion.95), channel_id=1, source_target_pairs={{0,1},{1,0},{2,3},{3,2},{4,5},{5,4},{6,7},{7,6},{8,9},{9,8},{10,11... | collective-permute-start | bytes 884744 | tf_op jit(solution)/shard_map/ppermute | solution.py:48
  469.4 22.5 %collective-permute-start.11 = (bf16[4,2,24,768]{3,2,0,1:T(8,128)(2,1)S(1)}, bf16[4,2,24,768]{3,2,0,1:T(8,128)(2,1)S(1)}, u32[]{:S(2)}, u32[]{:S(2)}) collective-permute-start(bf16[4,2,24,768]{3,2,0,1:T(8,128)(2,1)S(1)} %fusion.94), channel_id=1, source_target_pairs={{0,16},{8,24},{16,0},{24,8},{1,17},{9,25},{17,1},{25,9},{2,18},{10... | collective-permute-start | bytes 884744 | tf_op jit(solution)/shard_map/ppermute | solution.py:48
  479.3 25.2 %collective-permute-start.37 = (bf16[96,768]{1,0:T(8,128)(2,1)S(1)}, bf16[96,768]{1,0:T(8,128)(2,1)S(1)}, u32[]{:S(2)}, u32[]{:S(2)}) collective-permute-start(bf16[96,768]{1,0:T(8,128)(2,1)S(1)} %get-tuple-element.173), channel_id=1, source_target_pairs={{0,2},{1,3},{2,4},{3,5},{4,6},{5,7},{6,0},{7,1},{8,10},{9,11},{10,... | collective-permute-start | bytes 442376 | tf_op jit(solution)/shard_map/ppermute | solution.py:48
  481.0 24.0 %collective-permute-start.38 = (bf16[96,768]{1,0:T(8,128)(2,1)S(1)}, bf16[96,768]{1,0:T(8,128)(2,1)S(1)}, u32[]{:S(2)}, u32[]{:S(2)}) collective-permute-start(bf16[96,768]{1,0:T(8,128)(2,1)S(1)} %get-tuple-element.175), channel_id=1, source_target_pairs={{0,4},{1,5},{2,6},{3,7},{4,0},{5,1},{6,2},{7,3},{8,12},{9,13},{10,... | collective-permute-start | bytes 442376 | tf_op jit(solution)/shard_map/ppermute | solution.py:48
  487.3 13.9 %collective-permute-start.32 = (bf16[24,3072]{1,0:T(8,128)(2,1)S(1)}, bf16[24,3072]{1,0:T(8,128)(2,1)S(1)}, u32[]{:S(2)}, u32[]{:S(2)}) collective-permute-start(bf16[24,3072]{1,0:T(8,128)(2,1)S(1)} %get-tuple-element.178), channel_id=1, source_target_pairs={{0,4},{1,5},{2,6},{3,7},{4,0},{5,1},{6,2},{7,3},{8,12},{9,13},{10,... | collective-permute-start | bytes 442376 | tf_op jit(solution)/shard_map/ppermute | solution.py:48
  494.6 11.5 %collective-permute-start.39 = (bf16[96,768]{1,0:T(8,128)(2,1)S(1)}, bf16[96,768]{1,0:T(8,128)(2,1)S(1)}, u32[]{:S(2)}, u32[]{:S(2)}) collective-permute-start(bf16[96,768]{1,0:T(8,128)(2,1)S(1)} %get-tuple-element.174), channel_id=1, source_target_pairs={{0,6},{1,7},{2,0},{3,1},{4,2},{5,3},{6,4},{7,5},{8,14},{9,15},{10,... | collective-permute-start | bytes 442376 | tf_op jit(solution)/shard_map/ppermute | solution.py:48
  503.2 12.0 %collective-permute-start.18 = (bf16[4,24,768]{2,1,0:T(8,128)(2,1)S(1)}, bf16[4,24,768]{2,1,0:T(8,128)(2,1)S(1)}, u32[]{:S(2)}, u32[]{:S(2)}) collective-permute-start(bf16[4,24,768]{2,1,0:T(8,128)(2,1)S(1)} %fusion.105), channel_id=1, source_target_pairs={{0,16},{8,24},{16,0},{24,8},{1,17},{9,25},{17,1},{25,9},{2,18},{10... | collective-permute-start | bytes 442376 | tf_op jit(solution)/shard_map/ppermute | solution.py:48
  504.5 12.9 %collective-permute-start.12 = (bf16[4,24,768]{2,1,0:T(8,128)(2,1)S(1)}, bf16[4,24,768]{2,1,0:T(8,128)(2,1)S(1)}, u32[]{:S(2)}, u32[]{:S(2)}) collective-permute-start(bf16[4,24,768]{2,1,0:T(8,128)(2,1)S(1)} %fusion.104), channel_id=1, source_target_pairs={{0,1},{1,0},{2,3},{3,2},{4,5},{5,4},{6,7},{7,6},{8,9},{9,8},{10,11... | collective-permute-start | bytes 442376 | tf_op jit(solution)/shard_map/ppermute | solution.py:48
  (104 other events, 1380.8 us)
Sparse Core Ops, SparseCore 0:
  61.6 23.6 all-gather.1
  230.1 29.8 reduce-scatter.1

commit v2 on v0

v2 whole, which is shorter than its diff:
```python
from functools import partial

import jax
import jax.numpy as jnp
from jax import lax
from jax.experimental import pallas as pl
from jax.experimental.pallas import tpu as pltpu
from jax.sharding import PartitionSpec as P

D = 768
FF = 3072
H = 12
PAIRS = H // 2
HALF = 64
PWIN = 512
QB = 128
EXTRA = 16
LANES = 128
BF16 = jnp.bfloat16
F32 = jnp.float32
MB = 1 << 20


def nn(left, right):
    return jnp.dot(left, right, preferred_element_type=F32)


def nt(left, right, precision=None):
    return lax.dot_general(
        left, right, (((1,), (1,)), ((), ())), preferred_element_type=F32, precision=precision
    )


def iota(shape, dim):
    return lax.broadcasted_iota(jnp.int32, shape, dim)


def segment_of(info, place, row_len):
    item = jnp.zeros_like(place)
    for m in range(4):
        item = item + (place >= info[m]).astype(jnp.int32)
    return jnp.where((place >= 0) & (place < row_len), item, -2)


def head_half(block, head):
    lane = iota(block.shape, 1)
    return jnp.where((lane < 64) == (head == 0), block, jnp.zeros_like(block))


def tap_mask(info, tap, shift, count, row_len):
    center = info[4] + 4 * (iota((count, 1), 0) + shift)
    same = segment_of(info, center + tap - 2, row_len) == segment_of(info, center, row_len)
    return (same & (center < row_len)).astype(F32)


def project_kernel(info, tok, left, right, wq, wk, wv, taps, q_out, k_out, v_out, pool_out, tt_out, x, cells, *, row_len):
    count = tok.shape[0]
    x[0:HALF] = left[...]
    x[HALF : HALF + count] = tok[...]
    x[HALF + count :] = right[...]
    k_low = nn(x[...], wk[...]).astype(BF16)
    k_out[...] = k_low
    v_low = nn(x[...], wv[...]).astype(BF16)
    v_out[...] = v_low
    masks = [tap_mask(info, tap, 0, count // 4, row_len) for tap in range(5)]
    for which, low in ((0, k_low), (1, v_low)):
        wide = low.astype(F32)
        for c in range(D // LANES):
            lanes = slice(c * LANES, (c + 1) * LANES)
            cells[c] = wide[:, lanes]
            total = jnp.zeros((count // 4, LANES), F32)
            for tap in range(5):
                taken = cells.at[c][pl.ds(HALF + tap - 2, count // 4, stride=4), :]
                total = total + taken * masks[tap] * taps[tap : tap + 1, lanes]
            pool_out[which, :, lanes] = total.astype(BF16)
    q_out[...] = (nn(tok[...], wq[...]).astype(BF16).astype(F32) * 0.125).astype(BF16)
    tt_out[...] = tok[...].T


def near_forward_kernel(info, q, k, v, e_out, o_out, st_out, bias, *, row_len):
    count, span = q.shape[0], k.shape[0]
    blocks = count // QB

    @pl.when(pl.program_id(0) == 0)
    def _():
        for b in range(blocks):
            query_place = info[4] + b * QB + iota((1, QB), 1)
            key_place = info[4] - HALF + b * QB + iota((2 * QB, 1), 0)
            same = segment_of(info, key_place, row_len) == segment_of(info, query_place, row_len)
            near = jnp.abs(key_place - query_place) <= HALF
            bias[b] = jnp.where(same & near, 0.0, -1e30)

    vt = v[...].T
    ones = jnp.ones((16, span), BF16)
    st_out[...] = jnp.zeros_like(st_out)
    for head in range(2):
        qh = head_half(q[...], head)
        va = jnp.concatenate([vt[head * 64 : head * 64 + 64], ones], axis=0)
        for b in range(blocks):
            cols = slice(b * QB, (b + 1) * QB)
            keys = slice(b * QB, (b + 2) * QB)
            s = nt(k[keys, :], qh[cols]) + bias[b]
            top = jnp.max(s, axis=0, keepdims=True)
            e = jnp.exp(s - top).astype(BF16)
            e_out[head, b] = e
            oa = nn(va[:, keys], e)
            o_out[head * 64 : head * 64 + 64, cols] = oa[:64]
            st_out[0, head : head + 1, cols] = top
            st_out[0, 2 + head : 3 + head, cols] = oa[64:65]


def pool_forward_kernel(info, q, o_near, st, *rest, row_len, pieces):
    kv = rest[:pieces]
    e_out, o_out, rn_out, rp_out, bias = rest[pieces:]
    count = q.shape[0]
    size = kv[0].shape[1]

    @pl.when(pl.program_id(0) == 0)
    def _():
        query_place = info[4] + iota((1, count), 1)
        query_item = segment_of(info, query_place, row_len)
        for i in range(pieces):
            key_place = 4 * (info[8 + i] * size + iota((size, 1), 0))
            same = segment_of(info, key_place, row_len) == query_item
            near = jnp.abs(key_place - query_place) <= 2 * PWIN
            bias[i * size : (i + 1) * size] = jnp.where(same & near, 0.0, -1e30)

    kp = jnp.concatenate([piece[0] for piece in kv], axis=0)
    vt = jnp.concatenate([piece[1] for piece in kv], axis=0).T
    ones = jnp.ones((16, pieces * size), BF16)
    wide = min(256, count)
    for b in range(count // wide):
        cols = slice(b * wide, (b + 1) * wide)
        outs, near_scale, pool_scale = [], [], []
        for head in range(2):
            qh = head_half(q[cols, :], head)
            va = jnp.concatenate([vt[head * 64 : head * 64 + 64], ones], axis=0)
            s = nt(kp, qh) + bias[:, cols]
            near_top = st[0, head : head + 1, cols]
            top = jnp.maximum(jnp.max(s, axis=0, keepdims=True), near_top)
            e = jnp.exp(s - top).astype(BF16)
            e_out[head, :, cols] = e
            oa = nn(va, e)
            fade = jnp.exp(near_top - top)
            inverse = 1.0 / (fade * st[0, 2 + head : 3 + head, cols] + oa[64:65])
            outs.append((fade * o_near[head * 64 : head * 64 + 64, cols] + oa[:64]) * inverse)
            near_scale.append(jnp.broadcast_to(fade * inverse, (64, wide)))
            pool_scale.append(jnp.broadcast_to(inverse, (64, wide)))
        o_out[cols, :] = jnp.concatenate(outs, axis=0).T
        rn_out[cols, :] = jnp.concatenate(near_scale, axis=0).T
        rp_out[cols, :] = jnp.concatenate(pool_scale, axis=0).T


def normal_parts(v):
    bell = jnp.exp(v * v * -0.5)
    t = 1.0 / (1.0 + jnp.abs(v) * (0.3275911 * 0.7071067811865476))
    poly = t * (
        0.127414796 + t * (-0.142248368 + t * (0.7107068705 + t * (-0.7265760135 + t * 0.5307027145)))
    )
    tail = poly * bell
    return jnp.where(v < 0, tail, 1.0 - tail), v * bell * 0.3989422804014327


def normalized(values):
    shifted = values - jnp.mean(values, axis=1, keepdims=True)
    inverse = lax.rsqrt(jnp.mean(shifted * shifted, axis=1, keepdims=True) + 1e-05)
    return shifted * inverse, inverse


def norm_back(grad, gain, unit, inverse):
    e = grad * gain
    return inverse * (
        e
        - jnp.mean(e, axis=1, keepdims=True)
        - unit * jnp.mean(e * unit, axis=1, keepdims=True)
    )


def block_of(step, info, parts):
    ny = parts // 2
    back = step - parts
    mine = info[5]
    going_back = jnp.where(
        back < ny, 2 * back + 1 - mine, 2 * (back - ny) + mine
    )
    return jnp.where(step < parts, step, going_back)


def dense_kernel(
    info, o, rn, rp, tok, og, vecs, w_out, w_in, w_back,
    mixed, sum_grad, don, dop, in_keep, in_send, back_keep, back_send, out_keep, out_send, sums,
    att, first, unit_one, inv_one, low, low_t, act, slope, feed, feed_grad,
    *, parts,
):
    ny = parts // 2
    step = pl.program_id(0)
    width = w_in.shape[1]
    rc = in_keep.shape[1]
    mine = info[5]
    hidden = pl.ds(pl.multiple_of(block_of(step, info, parts) * width, width), width)
    gain_one, bias_one = vecs[0:1, :], vecs[1:2, :]
    gain_two, bias_two = vecs[2:3, :], vecs[3:4, :]

    def rows_of(y, core):
        return pl.ds(pl.multiple_of((2 * y + core) * rc, rc), rc)

    @pl.when(step == 0)
    def _():
        att[...] = o[...].astype(BF16)
        unit, inverse = normalized(tok[...].astype(F32) + nn(att[...], w_out[...]))
        unit_one[...] = unit
        inv_one[...] = jnp.broadcast_to(inverse, inv_one.shape)
        first[...] = unit * gain_one + bias_one
        low[...] = first[...].astype(BF16)
        low_t[...] = low[...].T
        feed[...] = jnp.zeros_like(feed)
        sums[...] = jnp.zeros_like(sums)

    @pl.when(step < parts)
    def _():
        inner = nn(low[...], w_in[...])
        phi, bell = normal_parts(inner)
        act[:, hidden] = (inner * phi).astype(BF16)
        slope[:, hidden] = (phi + bell).astype(slope.dtype)
        feed[...] += nn(act[:, hidden], w_back[...])

    @pl.when(step == parts - 1)
    def _():
        unit, inverse = normalized(first[...] + feed[...])
        mixed[...] = (unit * gain_two + bias_two).astype(BF16)
        upstream = og[...].astype(F32)
        sums[2:3] = jnp.sum(upstream * unit, axis=0, keepdims=True)
        sums[3:4] = jnp.sum(upstream, axis=0, keepdims=True)
        z_grad = norm_back(upstream, gain_two, unit, inverse)
        feed[...] = z_grad
        feed_grad[...] = z_grad.astype(BF16)

    @pl.when(step >= parts)
    def _():
        inner_grad = (nt(feed_grad[...], w_back[...]) * slope[:, hidden].astype(F32)).astype(BF16)
        act_t = act[:, hidden].T
        back = nn(act_t, feed_grad[...]).astype(BF16)

        @pl.when(step < parts + ny)
        def _():
            back_send[0] = back

        @pl.when(step >= parts + ny)
        def _():
            back_keep[0] = back

        for y in range(ny):
            in_send[y] = nn(low_t[rows_of(y, 1 - mine), :], inner_grad).astype(BF16)
            in_keep[y] = nn(low_t[rows_of(y, mine), :], inner_grad).astype(BF16)
        feed[...] += nt(inner_grad, w_in[...])

    @pl.when(step == 2 * parts - 1)
    def _():
        first_grad = feed[...]
        unit = unit_one[...]
        sums[0:1] = jnp.sum(first_grad * unit, axis=0, keepdims=True)
        sums[1:2] = jnp.sum(first_grad, axis=0, keepdims=True)
        total = norm_back(first_grad, gain_one, unit, inv_one[:, 0:1])
        sum_grad[...] = total
        branch_grad = total.astype(BF16)
        attended_grad = nt(branch_grad, w_out[...])
        don[...] = (attended_grad * rn[...]).astype(BF16)
        dop[...] = (attended_grad * rp[...]).astype(BF16)
        low_t[...] = att[...].T
        for y in range(ny):
            out_send[y] = nn(low_t[rows_of(y, 1 - mine), :], branch_grad).astype(BF16)
            out_keep[y] = nn(low_t[rows_of(y, mine), :], branch_grad).astype(BF16)


def score_delta(grad, attended):
    pick = ((iota((8, LANES), 1) // 64) == iota((8, LANES), 0)).astype(F32)
    return nt(pick, grad.astype(F32) * attended, precision=lax.Precision.HIGHEST)


def pool_backward_kernel(info, q, grad, o, e, *rest, pieces):
    kv = rest[:pieces]
    keep, send, dq_out, dk, dv = rest[pieces:]
    ny = pieces // 2
    count = q.shape[0]
    size = kv[0].shape[1]
    delta = score_delta(grad[...], o[...])
    kp = jnp.concatenate([piece[0] for piece in kv], axis=0)
    kt = kp.T
    vp = jnp.concatenate([piece[1] for piece in kv], axis=0)
    wide = min(256, count)
    for head in range(2):
        for b in range(count // wide):
            cols = slice(b * wide, (b + 1) * wide)
            gh = head_half(grad[cols, :], head)
            qh = head_half(q[cols, :], head)
            low = e[head, :, cols]
            dp = nt(vp, gh) - delta[head : head + 1, cols]
            ds = (low.astype(F32) * dp).astype(BF16)
            key_part = nn(ds, qh)
            value_part = nn(low, gh)
            if head == 0 and b == 0:
                dk[...] = key_part
                dv[...] = value_part
            else:
                dk[...] += key_part
                dv[...] += value_part
            dq_out[head * 64 : head * 64 + 64, cols] = nn(kt[head * 64 : head * 64 + 64], ds)
    for i in range(pieces):
        target = keep if i < ny else send
        after = pl.ds(pl.multiple_of(info[8 + pieces + i] * size, size), EXTRA)
        for which, total in ((0, dk), (1, dv)):
            target[i % ny, which, 0:size] = total[i * size : (i + 1) * size].astype(BF16)
            target[i % ny, which, size:] = total[after, :].astype(BF16)


def near_backward_kernel(q, grad, o, e, k, v, dq_pool, own, before, behind, dq_out, dk, dv):
    count = q.shape[0]
    delta = score_delta(grad[...], o[...])
    kt = k[...].T
    dk[...] = jnp.zeros_like(dk)
    dv[...] = jnp.zeros_like(dv)
    for b in range(count // QB):
        cols = slice(b * QB, (b + 1) * QB)
        keys = slice(b * QB, (b + 2) * QB)
        lows, scores, grads, queries, dqs = [], [], [], [], []
        for head in range(2):
            gh = head_half(grad[cols, :], head)
            low = e[head, b]
            dp = nt(v[keys, :], gh) - delta[head : head + 1, cols]
            ds = (low.astype(F32) * dp).astype(BF16)
            dqs.append(nn(kt[head * 64 : head * 64 + 64, keys], ds))
            lows.append(low)
            scores.append(ds)
            grads.append(gh)
            queries.append(head_half(q[cols, :], head))
        dk[keys, :] += nn(jnp.concatenate(scores, axis=1), jnp.concatenate(queries, axis=0))
        dv[keys, :] += nn(jnp.concatenate(lows, axis=1), jnp.concatenate(grads, axis=0))
        total = (jnp.concatenate(dqs, axis=0) + dq_pool[:, cols]) * 0.125
        dq_out[cols, :] = total.T.astype(BF16)
    for which, total in ((0, dk), (1, dv)):
        before[which] = total[0:HALF].astype(BF16)
        own[which] = total[HALF : HALF + count]
        behind[which] = total[HALF + count :].astype(BF16)


def query_grad_kernel(info, tt, dq, wq, sum_grad, keep, send, part):
    ny, rc = keep.shape[0], keep.shape[1]
    mine = info[5]
    for y in range(ny):
        for target, core in ((send, 1 - mine), (keep, mine)):
            rows = pl.ds(pl.multiple_of((2 * y + core) * rc, rc), rc)
            target[y] = nn(tt[rows, :], dq[...]).astype(BF16)
    part[...] = sum_grad[...] + nt(dq[...], wq[...])


def key_grad_kernel(info, tt, own, above, below, k, v, wk, wv, part, sums, taps, *rest, row_len, pieces):
    pooled = rest[:pieces]
    keep, send, tokens_grad, acc, cells, g, small, small_t, k_low, v_low = rest[pieces:]
    ny, rc = keep.shape[0], keep.shape[1]
    count = part.shape[0]
    size = count // 4
    mine = info[5]
    small[...] = jnp.zeros_like(small)
    small[0:8] = sums[...]
    masks = [tap_mask(info, tap, 0, size, row_len) for tap in range(5)]
    next_masks = [tap_mask(info, tap, 1, size, row_len) for tap in range(2)]
    moves = ((2, 0, 0), (3, 1, 0), (4, 2, 0), (0, 2, 1), (1, 3, 1))
    for which, source, low in ((0, k, k_low), (1, v, v_low)):
        for c in range(D // LANES):
            lanes = slice(c * LANES, (c + 1) * LANES)
            grad = acc.at[c]
            grad[...] = own[which, :, lanes]
            grad[0:HALF, :] += below[which, :, lanes].astype(F32)
            grad[count - HALF :, :] += above[which, :, lanes].astype(F32)
            cells[...] = source[:, lanes].astype(F32)
            total = pooled[0][0, which, :, lanes].astype(F32)
            for piece in pooled[1:]:
                total = total + piece[0, which, :, lanes].astype(F32)
            g[...] = total
            for tap, place, shift in moves:
                mask = next_masks[tap] if shift else masks[tap]
                spread = g[shift : shift + size, :] * mask * taps[tap : tap + 1, lanes]
                grad[pl.ds(place, size, stride=4), :] += spread
            for tap in range(5):
                taken = cells[pl.ds(HALF + tap - 2, size, stride=4), :]
                product = g[0:size, :] * masks[tap] * taken
                small[8 + tap : 9 + tap, lanes] += jnp.sum(product, axis=0, keepdims=True)
            low[:, lanes] = grad[...].astype(BF16)
    small_t[...] = small[...].T.astype(BF16)
    for y in range(ny):
        for target, core in ((send, 1 - mine), (keep, mine)):
            rows = pl.ds(pl.multiple_of((2 * y + core) * rc, rc), rc)
            target[y, :, 0:D] = nn(tt[rows, :], k_low[...]).astype(BF16)
            target[y, :, D : 2 * D] = nn(tt[rows, :], v_low[...]).astype(BF16)
            target[y, :, 2 * D :] = small_t[rows, :]
    total = part[...] + nt(k_low[...], wk[...])
    tokens_grad[...] = (total + nt(v_low[...], wv[...])).astype(BF16)


def hop_pairs(axis, count, stride, hop):
    pairs = []
    for device in range(lax.axis_size(axis)):
        place = (device // stride) % count
        pairs.append((device, device + ((place + hop) % count - place) * stride))
    return pairs


def swap_stage(parts, dim, axis, count, stride):
    mine = (lax.axis_index(axis) // stride) % count
    total = lax.dynamic_index_in_dim(parts, mine, dim, keepdims=False)
    for hop in range(1, count):
        block = lax.dynamic_index_in_dim(parts, (mine + hop) % count, dim, keepdims=False)
        moved = lax.ppermute(block.astype(BF16), axis, hop_pairs(axis, count, stride, hop))
        total = total + moved.astype(F32)
    return total


def scatter_sum(keep, send, seq_first):
    seq, dp = lax.axis_size("seq"), lax.axis_size("dp")
    moved = lax.ppermute(send, "seq", hop_pairs("seq", 2, 1, 1))
    parts = keep.astype(F32) + moved.astype(F32)
    near = 2 if dp % 2 == 0 else 1
    parts = parts.reshape(seq // 2, dp // near, near, parts.shape[1] // dp, parts.shape[2])
    if seq_first:
        parts = swap_stage(parts, 0, "seq", seq // 2, 2)
        parts = swap_stage(parts, 1, "dp", near, 1)
    else:
        parts = swap_stage(parts, 2, "dp", near, 1)
        parts = swap_stage(parts, 0, "seq", seq // 2, 2)
    return swap_stage(parts, 0, "dp", dp // near, near)


def shifted(block, by):
    size = lax.axis_size("seq")
    return lax.ppermute(block, "seq", [(i, i + by) for i in range(size) if 0 <= i + by < size])


def call(kernel, info, args, in_specs, outs, out_specs, grid, scratch, flops, vmem, name):
    moved = sum(a.size * a.dtype.itemsize for a in list(args) + list(outs))
    return pl.pallas_call(
        kernel,
        grid_spec=pltpu.PrefetchScalarGridSpec(
            num_scalar_prefetch=1,
            grid=grid,
            in_specs=in_specs,
            out_specs=out_specs,
            scratch_shapes=scratch,
        ),
        out_shape=outs,
        compiler_params=pltpu.CompilerParams(
            vmem_limit_bytes=vmem * MB, dimension_semantics=("arbitrary",) * len(grid)
        ),
        cost_estimate=pl.CostEstimate(flops=flops, bytes_accessed=moved, transcendentals=0),
        name=name,
    )(info, *args)


def whole(array):
    rank = len(array.shape)
    return pl.BlockSpec(array.shape, lambda i, info: (0,) * rank)


def columns(array, width=LANES):
    rank = len(array.shape)
    return pl.BlockSpec(array.shape[:-1] + (width,), lambda i, info: (0,) * (rank - 1) + (i,))


def leading(array, size):
    rank = len(array.shape)
    return pl.BlockSpec((size,) + array.shape[1:], lambda i, info: (i,) + (0,) * (rank - 1))


def per_device(
    tokens,
    item_lengths,
    w_query,
    w_key,
    w_value,
    w_out,
    w_in,
    w_back,
    norm1_gain,
    norm1_bias,
    norm2_gain,
    norm2_bias,
    pool_weight,
    out_grad,
):
    _, count, _ = tokens.shape
    seq = lax.axis_size("seq")
    ny = seq // 2
    row_len = count * seq
    span = count + 2 * HALF
    size = count // 4
    rc = D // seq
    here = lax.axis_index("seq")
    core, y = here % 2, here // 2
    owners = []
    for other in range(2):
        for hop in range(ny):
            owners.append(((y + hop) % ny) * 2 + jnp.bitwise_xor(core, other))
    afters = []
    for owner in owners:
        after = jnp.minimum(owner + 1, seq - 1)
        afters.append(jnp.bitwise_xor(after % 2, core) * ny + (after // 2 - y) % ny)
    zero = jnp.zeros((), jnp.int32)
    info = jnp.concatenate(
        [
            jnp.cumsum(item_lengths[0]).astype(jnp.int32),
            jnp.stack([here * count, core, y, zero] + owners + afters).astype(jnp.int32),
        ]
    )
    tok = tokens[0]
    og = out_grad[0]
    left = shifted(tok[count - HALF :], 1)
    right = shifted(tok[:HALF], -1)
    taps = jnp.pad(pool_weight.T, ((0, 3), (0, 0)))
    vecs = jnp.concatenate(
        [jnp.stack([norm1_gain, norm1_bias, norm2_gain, norm2_bias]), jnp.zeros((4, D), F32)]
    )

    def shape(dims, kind):
        return jax.ShapeDtypeStruct(dims, kind)

    args = (tok, left, right, w_query, w_key, w_value, taps)
    outs = (
        shape((count, D), BF16),
        shape((span, D), BF16),
        shape((span, D), BF16),
        shape((2, size, D), BF16),
        shape((D, count), BF16),
    )
    queries, keys, values, pool_own, tok_t = call(
        partial(project_kernel, row_len=row_len),
        info,
        args,
        [whole(a) for a in args],
        outs,
        [whole(a) for a in outs],
        (1,),
        [
            pltpu.VMEM((span, D), BF16),
            pltpu.VMEM((D // LANES, span, LANES), F32),
        ],
        2 * D * D * (count + 2 * span),
        40,
        "project",
    )

    pieces = [pool_own]
    for hop in range(1, ny):
        pieces.append(lax.ppermute(pool_own, "seq", hop_pairs("seq", ny, 2, ny - hop)))
    pieces = pieces + [lax.ppermute(piece, "seq", hop_pairs("seq", 2, 1, 1)) for piece in pieces]

    blocks = count // QB
    args = (queries, keys, values)
    outs = (
        shape((H, blocks, 2 * QB, QB), BF16),
        shape((D, count), F32),
        shape((PAIRS, 8, count), F32),
    )
    near_e, o_near, stats = call(
        partial(near_forward_kernel, row_len=row_len),
        info,
        args,
        [columns(a) for a in args],
        outs,
        [leading(outs[0], 2), leading(outs[1], LANES), leading(outs[2], 1)],
        (PAIRS,),
        [pltpu.VMEM((blocks, 2 * QB, QB), F32)],
        4 * H * 256 * 256 * count,
        32,
        "near_forward",
    )

    pool_all = seq * size
    args = (queries, o_near, stats) + tuple(pieces)
    outs = (
        shape((H, pool_all, count), BF16),
        shape((count, D), F32),
        shape((count, D), F32),
        shape((count, D), F32),
    )
    pool_e, attention, near_scale, pool_scale = call(
        partial(pool_forward_kernel, row_len=row_len, pieces=seq),
        info,
        args,
        [columns(queries), leading(o_near, LANES), leading(stats, 1)] + [columns(p) for p in pieces],
        outs,
        [leading(outs[0], 2)] + [columns(a) for a in outs[1:]],
        (PAIRS,),
        [pltpu.VMEM((pool_all, count), F32)],
        4 * H * 512 * 256 * count,
        32,
        "pool_forward",
    )

    width = FF // seq
    args = (attention, near_scale, pool_scale, tok, og, vecs, w_out, w_in, w_back)
    half_in = shape((ny, rc, FF), BF16)
    half_back = shape((ny, width, D), BF16)
    half_out = shape((ny, rc, D), BF16)
    outs = (
        shape((count, D), BF16),
        shape((count, D), F32),
        shape((count, D), BF16),
        shape((count, D), BF16),
        half_in,
        half_in,
        half_back,
        half_back,
        half_out,
        half_out,
        shape((8, D), F32),
    )
    in_columns = pl.BlockSpec(
        (ny, rc, width),
        lambda i, info: (0, 0, block_of(jnp.maximum(i, seq), info, seq)),
    )
    (
        mixed,
        sum_grad,
        near_grad,
        pool_grad,
        in_keep,
        in_send,
        back_keep,
        back_send,
        out_keep,
        out_send,
        sums,
    ) = call(
        partial(dense_kernel, parts=seq),
        info,
        args,
        [whole(a) for a in args[:7]]
        + [
            pl.BlockSpec((D, width), lambda i, info: (0, block_of(i, info, seq))),
            pl.BlockSpec((width, D), lambda i, info: (block_of(i, info, seq), 0)),
        ],
        outs,
        [whole(a) for a in outs[:4]]
        + [
            in_columns,
            in_columns,
            pl.BlockSpec(
                (1, width, D), lambda i, info: (jnp.maximum(i - seq - ny, 0), 0, 0)
            ),
            pl.BlockSpec(
                (1, width, D), lambda i, info: (jnp.clip(i - seq, 0, ny - 1), 0, 0)
            ),
        ]
        + [whole(a) for a in outs[8:]],
        (2 * seq,),
        [
            pltpu.VMEM((count, D), BF16),
            pltpu.VMEM((count, D), F32),
            pltpu.VMEM((count, D), F32),
            pltpu.VMEM((count, LANES), F32),
            pltpu.VMEM((count, D), BF16),
            pltpu.VMEM((D, count), BF16),
            pltpu.VMEM((count, FF), BF16),
            pltpu.VMEM((count, FF), BF16),
            pltpu.VMEM((count, D), F32),
            pltpu.VMEM((count, D), BF16),
        ],
        2 * count * (3 * D * D + 6 * D * FF),
        58,
        "dense",
    )
    sum_in = scatter_sum(in_keep, in_send, True)
    sum_back = scatter_sum(back_keep, back_send, False)
    sum_out = scatter_sum(out_keep, out_send, True)

    args = (queries, pool_grad, attention, pool_e) + tuple(pieces)
    half_pool = shape((ny, 2, size + EXTRA, D), BF16)
    outs = (half_pool, half_pool, shape((D, count), F32))
    pool_keep, pool_send, dq_pool = call(
        partial(pool_backward_kernel, pieces=seq),
        info,
        args,
        [columns(a) for a in args[:3]] + [leading(pool_e, 2)] + [columns(p) for p in pieces],
        outs,
        [columns(half_pool), columns(half_pool), leading(outs[2], LANES)],
        (PAIRS,),
        [pltpu.VMEM((pool_all, LANES), F32), pltpu.VMEM((pool_all, LANES), F32)],
        8 * H * 512 * 256 * count,
        32,
        "pool_backward",
    )
    pool_moved = lax.ppermute(pool_send, "seq", hop_pairs("seq", 2, 1, 1))
    pooled = [pool_keep[0:1], pool_moved[0:1]]
    for hop in range(1, ny):
        both = pool_keep[hop : hop + 1].astype(F32) + pool_moved[hop : hop + 1].astype(F32)
        pooled.append(lax.ppermute(both.astype(BF16), "seq", hop_pairs("seq", ny, 2, hop)))

    args = (queries, near_grad, attention, near_e, keys, values, dq_pool)
    outs = (
        shape((2, count, D), F32),
        shape((2, HALF, D), BF16),
        shape((2, HALF, D), BF16),
        shape((count, D), BF16),
    )
    own, before, behind, query_grad = call(
        lambda info, *refs: near_backward_kernel(*refs),
        info,
        args,
        [columns(a) for a in args[:3]]
        + [leading(near_e, 2), columns(keys), columns(values), leading(dq_pool, LANES)],
        outs,
        [columns(a) for a in outs],
        (PAIRS,),
        [pltpu.VMEM((span, LANES), F32), pltpu.VMEM((span, LANES), F32)],
        8 * H * 256 * 256 * count,
        32,
        "near_backward",
    )
    above = shifted(before, -1)
    below = shifted(behind, 1)

    args = (tok_t, query_grad, w_query, sum_grad)
    outs = (half_out, half_out, shape((count, D), F32))
    query_keep, query_send, part = call(
        query_grad_kernel,
        info,
        args,
        [whole(a) for a in args],
        outs,
        [whole(a) for a in outs],
        (1,),
        [],
        4 * count * D * D,
        32,
        "query_grad",
    )
    sum_query = scatter_sum(query_keep, query_send, False)

    args = (tok_t, own, above, below, keys, values, w_key, w_value, part, sums, taps) + tuple(pooled)
    half_both = shape((ny, rc, 2 * D + LANES), BF16)
    outs = (half_both, half_both, shape((count, D), BF16))
    both_keep, both_send, tokens_grad = call(
        partial(key_grad_kernel, row_len=row_len, pieces=len(pooled)),
        info,
        args,
        [whole(a) for a in args],
        outs,
        [whole(a) for a in outs],
        (1,),
        [
            pltpu.VMEM((D // LANES, count, LANES), F32),
            pltpu.VMEM((span, LANES), F32),
            pltpu.VMEM((size + EXTRA, LANES), F32),
            pltpu.VMEM((LANES, D), F32),
            pltpu.VMEM((D, LANES), BF16),
            pltpu.VMEM((count, D), BF16),
            pltpu.VMEM((count, D), BF16),
        ],
        8 * count * D * D,
        56,
        "key_grad",
    )
    sum_key = scatter_sum(both_keep[:, :, :D], both_send[:, :, :D], True)
    sum_rest = scatter_sum(both_keep[:, :, D:], both_send[:, :, D:], False)
    vectors = sum_rest[:, D:]
    return (
        mixed[None],
        tokens_grad[None],
        sum_query,
        sum_key,
        sum_rest[:, :D],
        sum_out,
        sum_in,
        sum_back,
        vectors[:, 0],
        vectors[:, 1],
        vectors[:, 2],
        vectors[:, 3],
        vectors[:, 8:13],
    )


def solution(mesh):
    shards, copied = P("dp", "seq", None), P()
    spread = P(("seq", "dp"), None)
    vector = P(("seq", "dp"))
    return jax.shard_map(
        per_device,
        mesh=mesh,
        in_specs=(shards, P("dp", None)) + (copied,) * 11 + (shards,),
        out_specs=(shards, shards) + (spread,) * 6 + (vector,) * 4 + (spread,),
        check_vma=False,
    )
```

time: 948 us -> 291 us (0.31)
  waiting for transfers between devices: 473 us -> 78.2 us
  matrix products: 156 us -> 0 us
  other arithmetic: 155 us -> 15.9 us
  Pallas kernels: 0 us -> 102 us
  local copies, waits for them, and re-layouts: 89.7 us -> 35.9 us
  starting transfers between devices: 8.1 us -> 56.1 us
  blocking collectives: 42.9 us -> 0 us
  between operations: 15.6 us -> 1.66 us
    reduce_scatter x4 -> x0, waiting for transfers between devices: 283 us -> none  [the longest x1 142 us: per_device(): lax.psum_scatter(grad_in_weight, ('seq', 'dp'), scatter_dimension=0, tile...]
    unnamed x11 -> x0, waiting for transfers between devices: 184 us -> none
    dot_general x30 -> x0, matrix products: 156 us -> none  [the longest x1 20.2 us: per_device(): inner = jnp.dot(first_low, w_in, preferred_element_type=jnp.float32)]
    pallas_call x0 -> x8, Pallas kernels: none -> 102 us  [call(): pl.pallas_call(kernel, grid_spec=pltpu.PrefetchScalarGridSpec(num_scalar_...]
    scatter-add x7 -> x0, other arithmetic: 90.2 us -> none  [the longest x5 89.7 us: per_device(): halo_grad.at[:, :, begin:begin + tok_count:4]]
    ppermute x4 -> x45, waiting for transfers between devices: 0.7 us -> 78.2 us  [the longest x30 60.1 us: swap_stage(): lax.ppermute(block.astype(BF16), axis, hop_pairs(axis, count, stride, hop))]
    ppermute x4 -> x45, starting transfers between devices: 7.15 us -> 56.1 us  [the longest x30 40.8 us: swap_stage(): lax.ppermute(block.astype(BF16), axis, hop_pairs(axis, count, stride, hop))]
    unnamed x1 -> x0, blocking collectives: 42.9 us -> none
  transfers between devices with their start and end apart: 12 -> 45, of which waited for: 6 -> 16; matrix products, arithmetic and copies ran while one was open for 26% -> 9% of each run, Pallas kernels for 0% -> 7%
where the time goes in v2:
time: 291 us; the launch traced here: 290 us
  Pallas kernels  102 us (35%)
  waiting for transfers between devices  78.2 us (27%)
  starting transfers between devices  56.1 us (19%)
  local copies, waits for them, and re-layouts  35.9 us (12%)
  other arithmetic  15.9 us (5%)
    pallas_call x8, Pallas kernels, call(): pl.pallas_call(kernel, grid_spec=pltpu.PrefetchScalarGridSpec(num_scalar_...  102 us
    ppermute x30, waiting for transfers between devices, swap_stage(): lax.ppermute(block.astype(BF16), axis, hop_pairs(axis, count, stride, hop))  60.1 us
    ppermute x30, starting transfers between devices, swap_stage(): lax.ppermute(block.astype(BF16), axis, hop_pairs(axis, count, stride, hop))  40.8 us
    unnamed x95, local copies, waits for them, and re-layouts  23.9 us
    ppermute x1, waiting for transfers between devices, per_device(): lax.ppermute(pool_own, 'seq', hop_pairs('seq', ny, 2, ny - hop))  8.82 us
    ppermute x4, starting transfers between devices, shifted(): lax.ppermute(block, 'seq', [(i, i + by) for i in range(size) if 0 <= i +...  7.98 us
    add x18, other arithmetic, swap_stage(): total = total + moved.astype(F32)  7.72 us
    ppermute x1, waiting for transfers between devices, per_device(): lax.ppermute(both.astype(BF16), 'seq', hop_pairs('seq', ny, 2, hop))  7.16 us
  transfers between devices with their start and end apart: 45, of which 16 were waited for; matrix products, arithmetic and copies ran while one was open for 9% of the time, Pallas kernels for 7%

profile of v2, /device:TPU:0, one launch (start us, length us, event | category | flops | bytes accessed | tf_op | source)
XLA Modules:
  0.0 290.3 jit_solution(8240881265212880981)
XLA Ops:
  14.3 3.1 %project.1 = (bf16[512,768]{1,0:T(8,128)(2,1)S(1)}, bf16[640,768]{1,0:T(8,128)(2,1)S(1)}, bf16[640,768]{1,0:T(8,128)(2,1)S(1)}, bf16[2,128,768]{2,1,0:T(8,128)(2,1)S(1)}, bf16[768,512]{1,0:T(8,128)(2,1)S(1)}) custom-call(s32[16]{0:T(128)S(1)} %concatenate.6.info, bf16[512,768]{1,0:T(8,128)(2,1)S(1)} %bitcast.161, ...), custom_call_target="tpu_custom_call" | custom-call | flops 2113929216 | bytes 8478720 | tf_op jit(solution)/shard_map/project/pallas_call | solution.py:440
  19.1 3.0 %collective-permute-start.2 = (bf16[2,128,768]{2,1,0:T(8,128)(2,1)S(1)}, bf16[2,128,768]{2,1,0:T(8,128)(2,1)S(1)}, u32[]{:S(2)}, u32[]{:S(2)}) collective-permute-start(bf16[2,128,768]{2,1,0:T(8,128)(2,1)S(1)} %get-tuple-element.54.rest_0_), channel_id=1, source_target_pairs={{0,16},{8,24},{16,0},{24,8},{1,17},{9,25},{17,1},{25,9},{2,18},{10... | collective-permute-start | bytes 1179656 | tf_op jit(solution)/shard_map/ppermute | solution.py:552
  22.4 8.8 %collective-permute-done.2.rest_1_ = bf16[2,128,768]{2,1,0:T(8,128)(2,1)S(1)} collective-permute-done((bf16[2,128,768]{2,1,0:T(8,128)(2,1)S(1)}, bf16[2,128,768]{2,1,0:T(8,128)(2,1)S(1)}, u32[]{:S(2)}, u32[]{:S(2)}) %collective-permute-start.2) | collective-permute-done | bytes 393248 | tf_op jit(solution)/shard_map/ppermute | solution.py:552
  33.8 8.9 %near_forward.1 = (bf16[12,4,256,128]{3,2,1,0:T(8,128)(2,1)S(1)}, f32[768,512]{1,0:T(8,128)S(1)}, f32[6,8,512]{2,1,0:T(8,128)S(1)}) custom-call(s32[16]{0:T(128)S(1)} %concatenate.6.info, bf16[512,768]{1,0:T(8,128)(2,1)S(1)} %copy-done.24, bf16[640,768]{1,0:T(8,128)(2,1)S(1)} %get-tuple-element.50.k.refs_4_, bf16[640,768]{1,0:T(8,128)(2,1)S(1)} %get-tuple-element.51.v.refs_5_), custom_call_target="tpu_custom_call" | custom-call | flops 1610612736 | bytes 7569408 | tf_op jit(solution)/shard_map/near_forward/pallas_call | solution.py:440
  44.5 14.2 %pool_forward.1 = (bf16[12,512,512]{2,1,0:T(8,128)(2,1)S(1)}, f32[512,768]{1,0:T(8,128)S(1)}, f32[512,768]{1,0:T(8,128)S(1)}, f32[512,768]{1,0:T(8,128)S(1)}) custom-call(s32[16]{0:T(128)S(1)} %concatenate.6.info, bf16[512,768]{1,0:T(8,128)(2,1)S(1)} %copy-done.24, f32[768,512]{1,0:T(8,128)S(1)} %get-tuple-element.52.o_near, ...), custom_call_target="tpu_custom_call" | custom-call | flops 3221225472 | bytes 15040512 | tf_op jit(solution)/shard_map/pool_forward/pallas_call | solution.py:440
  65.0 38.5 %dense.1 = (bf16[512,768]{1,0:T(8,128)(2,1)}, f32[512,768]{1,0:T(8,128)}, bf16[512,768]{1,0:T(8,128)(2,1)}, bf16[512,768]{1,0:T(8,128)(2,1)}, bf16[2,192,3072]{2...) custom-call(s32[16]{0:T(128)} %copy-done.10, ...), custom_call_target="tpu_custom_call" | custom-call | flops 16307453952 | bytes 31506432 | tf_op jit(solution)/shard_map/dense/pallas_call | solution.py:440
  108.6 12.8 %pool_backward.1 = (bf16[2,2,144,768]{3,2,1,0:T(8,128)(2,1)S(1)}, bf16[2,2,144,768]{3,2,1,0:T(8,128)(2,1)}, f32[768,512]{1,0:T(8,128)S(1)}) custom-call(s32[16]{0:T(128)S(1)} %copy-done.11, bf16[512,768]{1,0:T(8,128)(2,1)S(1)} %copy-done.25, bf16[512,768]{1,0:T(8,128)(2,1)S(1)} %copy-done.32, f32[512,768]{1,0:T(8,128)S(1)} %copy-done.22, ...), custom_call_target="tpu_custom_call" | custom-call | flops 6442450944 | bytes 14352384 | tf_op jit(solution)/shard_map/pool_backward/pallas_call | solution.py:440
  121.5 11.6 %near_backward.1 = (f32[2,512,768]{2,1,0:T(8,128)S(1)}, bf16[2,64,768]{2,1,0:T(8,128)(2,1)S(1)}, bf16[2,64,768]{2,1,0:T(8,128)(2,1)S(1)}, bf16[512,768]{1,0:T(8,128)(2,1)S(1)}) custom-call(s32[16]{0:T(128)S(1)} %copy-done.11, bf16[512,768]{1,0:T(8,128)(2,1)S(1)} %copy-done.26, bf16[512,768]{1,0:T(8,128)(2,1)S(1)} %copy-done.27, f32[512,768]{1,0:T(8,128)S(1)} %copy-done.22, ...), custom_call_target="tpu_custom_call" | custom-call | flops 3221225472 | bytes 14155776 | tf_op jit(solution)/shard_map/near_backward/pallas_call | solution.py:440
  138.1 3.0 %collective-permute-start.6 = (bf16[2,64,768]{2,1,0:T(8,128)(2,1)S(1)}, bf16[2,64,768]{2,1,0:T(8,128)(2,1)S(1)}, u32[]{:S(2)}, u32[]{:S(2)}) collective-permute-start(bf16[2,64,768]{2,1,0:T(8,128)(2,1)S(1)} %get-tuple-element.67), channel_id=1, source_target_pairs={{0,8},{8,16},{16,24},{1,9},{9,17},{17,25},{2,10},{10,18},{18,26},{... | collective-permute-start | bytes 589832 | tf_op jit(solution)/shard_map/ppermute | solution.py:435
  149.5 4.6 %collective-permute-done.10 = bf16[2,4,24,768]{3,2,1,0:T(8,128)(2,1)S(1)} collective-permute-done((bf16[2,4,24,768]{3,2,1,0:T(8,128)(2,1)S(1)}, bf16[2,4,24,768]{3,2,1,0:T(8,128)(2,1)S(1)}, u32[]{:S(2)}, u32[]{:S(2)}) %collective-permute-start.10) | collective-permute-done | bytes 294944 | tf_op jit(solution)/shard_map/ppermute | solution.py:413
  160.1 7.2 %collective-permute-done.8.rest_2_ = bf16[1,2,144,768]{3,2,1,0:T(8,128)(2,1)S(1)} collective-permute-done((bf16[1,2,144,768]{3,2,1,0:T(8,128)(2,1)S(1)}, bf16[1,2,144,768]{3,2,1,0:T(8,128)(2,1)S(1)}, u32[]{:S(2)}, u32[]{:S(2)}) %collective-permute-start.8) | collective-permute-done | bytes 442400 | tf_op jit(solution)/shard_map/ppermute | solution.py:695
  168.0 11.4 %key_grad.1 = (bf16[2,192,1664]{2,1,0:T(8,128)(2,1)}, bf16[2,192,1664]{2,1,0:T(8,128)(2,1)}, bf16[512,768]{1,0:T(8,128)(2,1)}) custom-call(s32[16]{0:T(128)} %copy-done.10, bf16[768,512]{1,0:T(8,128)(2,1)} %copy-done.6, f32[2,512,768]{2,1,0:T(8,128)} %copy-done, bf16[2,64,768]{2,1,0:T(8,128)(2,1)} %copy-done.40, bf16[2,64,768]{2,1,0:T(8,128)(2,1)} %copy-done.41, ...), custom_call_target="tpu_custom_call" | custom-call | flops 2415919104 | bytes 14942208 | tf_op jit(solution)/shard_map/key_grad/pallas_call | solution.py:440
  180.8 3.6 %collective-permute-start.14 = (bf16[24,768]{1,0:T(8,128)(2,1)S(1)}, bf16[24,768]{1,0:T(8,128)(2,1)S(1)}, u32[]{:S(2)}, u32[]{:S(2)}) collective-permute-start(bf16[24,768]{1,0:T(8,128)(2,1)S(1)} %get-tuple-element.146), channel_id=1, source_target_pairs={{0,6},{1,7},{2,0},{3,1},{4,2},{5,3},{6,4},{7,5},{8,14},{9,15},{10,... | collective-permute-start | bytes 110600 | tf_op jit(solution)/shard_map/ppermute | solution.py:413
  196.2 4.3 %collective-permute-done.16 = bf16[4,2,24,768]{3,2,0,1:T(8,128)(2,1)S(1)} collective-permute-done((bf16[4,2,24,768]{3,2,0,1:T(8,128)(2,1)S(1)}, bf16[4,2,24,768]{3,2,0,1:T(8,128)(2,1)S(1)}, u32[]{:S(2)}, u32[]{:S(2)}) %collective-permute-start.16) | collective-permute-done | bytes 294944 | tf_op jit(solution)/shard_map/ppermute | solution.py:413
  203.0 4.5 %collective-permute-done.17 = bf16[4,24,768]{2,1,0:T(8,128)(2,1)S(1)} collective-permute-done((bf16[4,24,768]{2,1,0:T(8,128)(2,1)S(1)}, bf16[4,24,768]{2,1,0:T(8,128)(2,1)S(1)}, u32[]{:S(2)}, u32[]{:S(2)}) %collective-permute-start.17) | collective-permute-done | bytes 147488 | tf_op jit(solution)/shard_map/ppermute | solution.py:413
  210.1 3.4 %collective-permute-done.22 = bf16[2,4,24,896]{3,2,1,0:T(8,128)(2,1)S(1)} collective-permute-done((bf16[2,4,24,896]{3,2,1,0:T(8,128)(2,1)S(1)}, bf16[2,4,24,896]{3,2,1,0:T(8,128)(2,1)S(1)}, u32[]{:S(2)}, u32[]{:S(2)}) %collective-permute-start.22) | collective-permute-done | bytes 344096 | tf_op jit(solution)/shard_map/ppermute | solution.py:413
  224.8 2.9 %collective-permute-start.26 = (bf16[24,896]{1,0:T(8,128)(2,1)S(1)}, bf16[24,896]{1,0:T(8,128)(2,1)S(1)}, u32[]{:S(2)}, u32[]{:S(2)}) collective-permute-start(bf16[24,896]{1,0:T(8,128)(2,1)S(1)} %get-tuple-element.137), channel_id=1, source_target_pairs={{0,6},{1,7},{2,0},{3,1},{4,2},{5,3},{6,4},{7,5},{8,14},{9,15},{10,... | collective-permute-start | bytes 129032 | tf_op jit(solution)/shard_map/ppermute | solution.py:413
  228.4 16.2 %collective-permute-done.34 = bf16[4,2,24,3072]{3,2,0,1:T(8,128)(2,1)S(1)} collective-permute-done((bf16[4,2,24,3072]{3,2,0,1:T(8,128)(2,1)S(1)}, bf16[4,2,24,3072]{3,2,0,1:T(8,128)(2,1)S(1)}, u32[]{:S(2)}, u32[]{:S(2)}) %collective-permute-start.34) | collective-permute-done | bytes 1179680 | tf_op jit(solution)/shard_map/ppermute | solution.py:413
  254.7 6.7 %collective-permute-done.35 = bf16[4,24,3072]{2,1,0:T(8,128)(2,1)} collective-permute-done((bf16[4,24,3072]{2,1,0:T(8,128)(2,1)}, bf16[4,24,3072]{2,1,0:T(8,128)(2,1)}, u32[]{:S(2)}, u32[]{:S(2)}) %collective-permute-start.35) | collective-permute-done | bytes 589856 | tf_op jit(solution)/shard_map/ppermute | solution.py:413
  262.6 3.0 %collective-permute-start.38 = (bf16[24,3072]{1,0:T(8,128)(2,1)S(1)}, bf16[24,3072]{1,0:T(8,128)(2,1)S(1)}, u32[]{:S(2)}, u32[]{:S(2)}) collective-permute-start(bf16[24,3072]{1,0:T(8,128)(2,1)S(1)} %get-tuple-element.132), channel_id=1, source_target_pairs={{0,6},{1,7},{2,0},{3,1},{4,2},{5,3},{6,4},{7,5},{8,14},{9,15},{10,... | collective-permute-start | bytes 442376 | tf_op jit(solution)/shard_map/ppermute | solution.py:413
  266.4 3.2 %collective-permute-start.44 = (bf16[96,768]{1,0:T(8,128)(2,1)S(1)}, bf16[96,768]{1,0:T(8,128)(2,1)S(1)}, u32[]{:S(2)}, u32[]{:S(2)}) collective-permute-start(bf16[96,768]{1,0:T(8,128)(2,1)S(1)} %get-tuple-element.129), channel_id=1, source_target_pairs={{0,6},{1,7},{2,0},{3,1},{4,2},{5,3},{6,4},{7,5},{8,14},{9,15},{10,... | collective-permute-start | bytes 442376 | tf_op jit(solution)/shard_map/ppermute | solution.py:413
  270.8 3.5 %collective-permute-start.42 = (bf16[96,768]{1,0:T(8,128)(2,1)S(1)}, bf16[96,768]{1,0:T(8,128)(2,1)S(1)}, u32[]{:S(2)}, u32[]{:S(2)}) collective-permute-start(bf16[96,768]{1,0:T(8,128)(2,1)S(1)} %get-tuple-element.128), channel_id=1, source_target_pairs={{0,2},{1,3},{2,4},{3,5},{4,6},{5,7},{6,0},{7,1},{8,10},{9,11},{10,... | collective-permute-start | bytes 442376 | tf_op jit(solution)/shard_map/ppermute | solution.py:413
  274.4 10.3 %collective-permute-done.37 = bf16[24,3072]{1,0:T(8,128)(2,1)S(1)} collective-permute-done((bf16[24,3072]{1,0:T(8,128)(2,1)S(1)}, bf16[24,3072]{1,0:T(8,128)(2,1)S(1)}, u32[]{:S(2)}, u32[]{:S(2)}) %collective-permute-start.37) | collective-permute-done | bytes 147488 | tf_op jit(solution)/shard_map/ppermute | solution.py:413
  285.5 4.0 %collective-permute-done.43 = bf16[96,768]{1,0:T(8,128)(2,1)S(1)} collective-permute-done((bf16[96,768]{1,0:T(8,128)(2,1)S(1)}, bf16[96,768]{1,0:T(8,128)(2,1)S(1)}, u32[]{:S(2)}, u32[]{:S(2)}) %collective-permute-start.43) | collective-permute-done | bytes 147488 | tf_op jit(solution)/shard_map/ppermute | solution.py:413
  (229 shorter events, 95.8 us)
Async XLA Ops:
  19.1 12.1 %collective-permute-start.2 = (bf16[2,128,768]{2,1,0:T(8,128)(2,1)S(1)}, bf16[2,128,768]{2,1,0:T(8,128)(2,1)S(1)}, u32[]{:S(2)}, u32[]{:S(2)}) collective-permute-start(bf16[2,128,768]{2,1,0:T(8,128)(2,1)S(1)} %get-tuple-element.54.rest_0_), channel_id=1, source_target_pairs={{0,16},{8,24},{16,0},{24,8},{1,17},{9,25},{17,1},{25,9},{2,18},{10... | collective-permute-start | bytes 1179656 | tf_op jit(solution)/shard_map/ppermute | solution.py:552
  22.2 22.3 %collective-permute-start.3 = (bf16[2,128,768]{2,1,0:T(8,128)(2,1)S(1)}, bf16[2,128,768]{2,1,0:T(8,128)(2,1)S(1)}, u32[]{:S(2)}, u32[]{:S(2)}) collective-permute-start(bf16[2,128,768]{2,1,0:T(8,128)(2,1)S(1)} %get-tuple-element.54.rest_0_), channel_id=1, source_target_pairs={{0,8},{8,0},{16,24},{24,16},{1,9},{9,1},{17,25},{25,17},{2,10},{10... | collective-permute-start | bytes 1179656 | tf_op jit(solution)/shard_map/ppermute | solution.py:553
  31.2 13.3 %collective-permute-start.4 = (bf16[2,128,768]{2,1,0:T(8,128)(2,1)S(1)}, bf16[2,128,768]{2,1,0:T(8,128)(2,1)}, u32[]{:S(2)}, u32[]{:S(2)}) collective-permute-start(bf16[2,128,768]{2,1,0:T(8,128)(2,1)S(1)} %collective-permute-done.2.rest_1_), channel_id=1, source_target_pairs={{0,8},{8,0},{16,24},{24,16},{1,9},{9,1},{17,25},{25,17},{2,10},{10... | collective-permute-start | bytes 1179656 | tf_op jit(solution)/shard_map/ppermute | solution.py:553
  136.8 22.7 %collective-permute-start.5 = (bf16[2,64,768]{2,1,0:T(8,128)(2,1)S(1)}, bf16[2,64,768]{2,1,0:T(8,128)(2,1)S(1)}, u32[]{:S(2)}, u32[]{:S(2)}) collective-permute-start(bf16[2,64,768]{2,1,0:T(8,128)(2,1)S(1)} %get-tuple-element.66), channel_id=1, source_target_pairs={{8,0},{16,8},{24,16},{9,1},{17,9},{25,17},{10,2},{18,10},{26,18},{... | collective-permute-start | bytes 589832 | tf_op jit(solution)/shard_map/ppermute | solution.py:435
  138.1 21.9 %collective-permute-start.6 = (bf16[2,64,768]{2,1,0:T(8,128)(2,1)S(1)}, bf16[2,64,768]{2,1,0:T(8,128)(2,1)S(1)}, u32[]{:S(2)}, u32[]{:S(2)}) collective-permute-start(bf16[2,64,768]{2,1,0:T(8,128)(2,1)S(1)} %get-tuple-element.67), channel_id=1, source_target_pairs={{0,8},{8,16},{16,24},{1,9},{9,17},{17,25},{2,10},{10,18},{18,26},{... | collective-permute-start | bytes 589832 | tf_op jit(solution)/shard_map/ppermute | solution.py:435
  142.0 72.5 %collective-permute-start.33 = (bf16[2,192,3072]{2,1,0:T(8,128)(2,1)}, bf16[2,192,3072]{2,1,0:T(8,128)(2,1)S(1)}, u32[]{:S(2)}, u32[]{:S(2)}) collective-permute-start(bf16[2,192,3072]{2,1,0:T(8,128)(2,1)} %get-tuple-element.82), channel_id=1, source_target_pairs={{0,8},{8,0},{16,24},{24,16},{1,9},{9,1},{17,25},{25,17},{2,10},{10... | collective-permute-start | bytes 7077896 | tf_op jit(solution)/shard_map/ppermute | solution.py:420
  154.1 13.1 %collective-permute-start.8 = (bf16[1,2,144,768]{3,2,1,0:T(8,128)(2,1)S(1)}, bf16[1,2,144,768]{3,2,1,0:T(8,128)(2,1)S(1)}, u32[]{:S(2)}, u32[]{:S(2)}) collective-permute-start(bf16[1,2,144,768]{3,2,1,0:T(8,128)(2,1)S(1)} %add_convert_fusion), channel_id=1, source_target_pairs={{0,16},{8,24},{16,0},{24,8},{1,17},{9,25},{17,1},{25,9},{2,18},{10... | collective-permute-start | bytes 1327112 | tf_op jit(solution)/shard_map/ppermute | solution.py:695
  157.3 23.4 %collective-permute-start.11 = (bf16[4,24,768]{2,1,0:T(8,128)(2,1)S(1)}, bf16[4,24,768]{2,1,0:T(8,128)(2,1)S(1)}, u32[]{:S(2)}, u32[]{:S(2)}) collective-permute-start(bf16[4,24,768]{2,1,0:T(8,128)(2,1)S(1)} %fusion.13), channel_id=1, source_target_pairs={{0,16},{8,24},{16,0},{24,8},{1,17},{9,25},{17,1},{25,9},{2,18},{10... | collective-permute-start | bytes 442376 | tf_op jit(solution)/shard_map/ppermute | solution.py:413
  159.6 24.8 %collective-permute-start.29 = (bf16[4,24,768]{2,1,0:T(8,128)(2,1)S(1)}, bf16[4,24,768]{2,1,0:T(8,128)(2,1)S(1)}, u32[]{:S(2)}, u32[]{:S(2)}) collective-permute-start(bf16[4,24,768]{2,1,0:T(8,128)(2,1)S(1)} %fusion.15), channel_id=1, source_target_pairs={{0,1},{1,0},{2,3},{3,2},{4,5},{5,4},{6,7},{7,6},{8,9},{9,8},{10,11... | collective-permute-start | bytes 442376 | tf_op jit(solution)/shard_map/ppermute | solution.py:413
  194.0 22.6 %collective-permute-start.39 = (bf16[2,768,768]{2,1,0:T(8,128)(2,1)S(1)}, bf16[2,768,768]{2,1,0:T(8,128)(2,1)S(1)}, u32[]{:S(2)}, u32[]{:S(2)}) collective-permute-start(bf16[2,768,768]{2,1,0:T(8,128)(2,1)S(1)} %copy-done.46), channel_id=1, source_target_pairs={{0,8},{8,0},{16,24},{24,16},{1,9},{9,1},{17,25},{25,17},{2,10},{10... | collective-permute-start | bytes 7077896 | tf_op jit(solution)/shard_map/ppermute | solution.py:420
  207.6 15.0 %collective-permute-start.20 = (bf16[24,768]{1,0:T(8,128)(2,1)S(1)}, bf16[24,768]{1,0:T(8,128)(2,1)S(1)}, u32[]{:S(2)}, u32[]{:S(2)}) collective-permute-start(bf16[24,768]{1,0:T(8,128)(2,1)S(1)} %get-tuple-element.143), channel_id=1, source_target_pairs={{0,6},{1,7},{2,0},{3,1},{4,2},{5,3},{6,4},{7,5},{8,14},{9,15},{10,... | collective-permute-start | bytes 110600 | tf_op jit(solution)/shard_map/ppermute | solution.py:413
  210.1 14.0 %collective-permute-start.19 = (bf16[24,768]{1,0:T(8,128)(2,1)S(1)}, bf16[24,768]{1,0:T(8,128)(2,1)S(1)}, u32[]{:S(2)}, u32[]{:S(2)}) collective-permute-start(bf16[24,768]{1,0:T(8,128)(2,1)S(1)} %get-tuple-element.144), channel_id=1, source_target_pairs={{0,4},{1,5},{2,6},{3,7},{4,0},{5,1},{6,2},{7,3},{8,12},{9,13},{10,... | collective-permute-start | bytes 110600 | tf_op jit(solution)/shard_map/ppermute | solution.py:413
  216.6 28.0 %collective-permute-start.34 = (bf16[4,2,24,3072]{3,2,0,1:T(8,128)(2,1)S(1)}, bf16[4,2,24,3072]{3,2,0,1:T(8,128)(2,1)S(1)}, u32[]{:S(2)}, u32[]{:S(2)}) collective-permute-start(bf16[4,2,24,3072]{3,2,0,1:T(8,128)(2,1)S(1)} %fusion), channel_id=1, source_target_pairs={{0,16},{8,24},{16,0},{24,8},{1,17},{9,25},{17,1},{25,9},{2,18},{10... | collective-permute-start | bytes 3538952 | tf_op jit(solution)/shard_map/ppermute | solution.py:413
  222.6 28.6 %collective-permute-start.40 = (bf16[2,4,96,768]{3,2,1,0:T(8,128)(2,1)S(1)}, bf16[2,4,96,768]{3,2,1,0:T(8,128)(2,1)}, u32[]{:S(2)}, u32[]{:S(2)}) collective-permute-start(bf16[2,4,96,768]{3,2,1,0:T(8,128)(2,1)S(1)} %fusion.1), channel_id=1, source_target_pairs={{0,1},{1,0},{2,3},{3,2},{4,5},{5,4},{6,7},{7,6},{8,9},{9,8},{10,11... | collective-permute-start | bytes 3538952 | tf_op jit(solution)/shard_map/ppermute | solution.py:413
  224.8 22.2 %collective-permute-start.26 = (bf16[24,896]{1,0:T(8,128)(2,1)S(1)}, bf16[24,896]{1,0:T(8,128)(2,1)S(1)}, u32[]{:S(2)}, u32[]{:S(2)}) collective-permute-start(bf16[24,896]{1,0:T(8,128)(2,1)S(1)} %get-tuple-element.137), channel_id=1, source_target_pairs={{0,6},{1,7},{2,0},{3,1},{4,2},{5,3},{6,4},{7,5},{8,14},{9,15},{10,... | collective-permute-start | bytes 129032 | tf_op jit(solution)/shard_map/ppermute | solution.py:413
  227.8 19.3 %collective-permute-start.25 = (bf16[24,896]{1,0:T(8,128)(2,1)S(1)}, bf16[24,896]{1,0:T(8,128)(2,1)S(1)}, u32[]{:S(2)}, u32[]{:S(2)}) collective-permute-start(bf16[24,896]{1,0:T(8,128)(2,1)S(1)} %get-tuple-element.138), channel_id=1, source_target_pairs={{0,4},{1,5},{2,6},{3,7},{4,0},{5,1},{6,2},{7,3},{8,12},{9,13},{10,... | collective-permute-start | bytes 129032 | tf_op jit(solution)/shard_map/ppermute | solution.py:413
  227.8 19.3 %collective-permute-start.24 = (bf16[24,896]{1,0:T(8,128)(2,1)S(1)}, bf16[24,896]{1,0:T(8,128)(2,1)S(1)}, u32[]{:S(2)}, u32[]{:S(2)}) collective-permute-start(bf16[24,896]{1,0:T(8,128)(2,1)S(1)} %get-tuple-element.136), channel_id=1, source_target_pairs={{0,2},{1,3},{2,4},{3,5},{4,6},{5,7},{6,0},{7,1},{8,10},{9,11},{10,... | collective-permute-start | bytes 129032 | tf_op jit(solution)/shard_map/ppermute | solution.py:413
  245.7 15.6 %collective-permute-start.35 = (bf16[4,24,3072]{2,1,0:T(8,128)(2,1)}, bf16[4,24,3072]{2,1,0:T(8,128)(2,1)}, u32[]{:S(2)}, u32[]{:S(2)}) collective-permute-start(bf16[4,24,3072]{2,1,0:T(8,128)(2,1)} %fusion.2), channel_id=1, source_target_pairs={{0,1},{1,0},{2,3},{3,2},{4,5},{5,4},{6,7},{7,6},{8,9},{9,8},{10,11... | collective-permute-start | bytes 1769480 | tf_op jit(solution)/shard_map/ppermute | solution.py:413
  253.5 12.7 %collective-permute-start.41 = (bf16[4,96,768]{2,1,0:T(8,128)(2,1)S(1)}, bf16[4,96,768]{2,1,0:T(8,128)(2,1)S(1)}, u32[]{:S(2)}, u32[]{:S(2)}) collective-permute-start(bf16[4,96,768]{2,1,0:T(8,128)(2,1)S(1)} %fusion.3), channel_id=1, source_target_pairs={{0,16},{8,24},{16,0},{24,8},{1,17},{9,25},{17,1},{25,9},{2,18},{10... | collective-permute-start | bytes 1769480 | tf_op jit(solution)/shard_map/ppermute | solution.py:413
  265.6 19.1 %collective-permute-start.37 = (bf16[24,3072]{1,0:T(8,128)(2,1)S(1)}, bf16[24,3072]{1,0:T(8,128)(2,1)S(1)}, u32[]{:S(2)}, u32[]{:S(2)}) collective-permute-start(bf16[24,3072]{1,0:T(8,128)(2,1)S(1)} %get-tuple-element.133), channel_id=1, source_target_pairs={{0,4},{1,5},{2,6},{3,7},{4,0},{5,1},{6,2},{7,3},{8,12},{9,13},{10,... | collective-permute-start | bytes 442376 | tf_op jit(solution)/shard_map/ppermute | solution.py:413
  265.6 19.1 %collective-permute-start.36 = (bf16[24,3072]{1,0:T(8,128)(2,1)S(1)}, bf16[24,3072]{1,0:T(8,128)(2,1)S(1)}, u32[]{:S(2)}, u32[]{:S(2)}) collective-permute-start(bf16[24,3072]{1,0:T(8,128)(2,1)S(1)} %get-tuple-element.131), channel_id=1, source_target_pairs={{0,2},{1,3},{2,4},{3,5},{4,6},{5,7},{6,0},{7,1},{8,10},{9,11},{10,... | collective-permute-start | bytes 442376 | tf_op jit(solution)/shard_map/ppermute | solution.py:413
  266.4 19.1 %collective-permute-start.44 = (bf16[96,768]{1,0:T(8,128)(2,1)S(1)}, bf16[96,768]{1,0:T(8,128)(2,1)S(1)}, u32[]{:S(2)}, u32[]{:S(2)}) collective-permute-start(bf16[96,768]{1,0:T(8,128)(2,1)S(1)} %get-tuple-element.129), channel_id=1, source_target_pairs={{0,6},{1,7},{2,0},{3,1},{4,2},{5,3},{6,4},{7,5},{8,14},{9,15},{10,... | collective-permute-start | bytes 442376 | tf_op jit(solution)/shard_map/ppermute | solution.py:413
  269.7 19.8 %collective-permute-start.43 = (bf16[96,768]{1,0:T(8,128)(2,1)S(1)}, bf16[96,768]{1,0:T(8,128)(2,1)S(1)}, u32[]{:S(2)}, u32[]{:S(2)}) collective-permute-start(bf16[96,768]{1,0:T(8,128)(2,1)S(1)} %get-tuple-element.130), channel_id=1, source_target_pairs={{0,4},{1,5},{2,6},{3,7},{4,0},{5,1},{6,2},{7,3},{8,12},{9,13},{10,... | collective-permute-start | bytes 442376 | tf_op jit(solution)/shard_map/ppermute | solution.py:413
  270.8 18.6 %collective-permute-start.42 = (bf16[96,768]{1,0:T(8,128)(2,1)S(1)}, bf16[96,768]{1,0:T(8,128)(2,1)S(1)}, u32[]{:S(2)}, u32[]{:S(2)}) collective-permute-start(bf16[96,768]{1,0:T(8,128)(2,1)S(1)} %get-tuple-element.128), channel_id=1, source_target_pairs={{0,2},{1,3},{2,4},{3,5},{4,6},{5,7},{6,0},{7,1},{8,10},{9,11},{10,... | collective-permute-start | bytes 442376 | tf_op jit(solution)/shard_map/ppermute | solution.py:413
  (68 other events, 819.9 us)

commit v3 on v2

--- a/solution.py
+++ b/solution.py
@@ -51,6 +51,36 @@
     center = info[4] + 4 * (iota((count, 1), 0) + shift)
     same = segment_of(info, center + tap - 2, row_len) == segment_of(info, center, row_len)
     return (same & (center < row_len)).astype(F32)
+
+
+def folds(rows, width):
+    return 2 if rows % 16 and rows % 8 == 0 and (width // 2) % LANES == 0 else 1
+
+
+def folded(rows, width):
+    fold = folds(rows, width)
+    return (rows * fold, width // fold)
+
+
+def fold_rows(block):
+    rows, width = block.shape
+    fold = folds(rows, width)
+    part = width // fold
+    return jnp.concatenate([block[:, i * part : (i + 1) * part] for i in range(fold)], axis=0)
+
+
+def unfold_rows(block, rows):
+    fold = block.shape[0] // rows
+    return jnp.concatenate([block[i * rows : (i + 1) * rows] for i in range(fold)], axis=1)
+
+
+def store_chunks(target, total, inner=()):
+    nz, nx = target.shape[0], target.shape[1]
+    rows = total.shape[0] // (nz * nx)
+    for z in range(nz):
+        for x in range(nx):
+            start = (z * nx + x) * rows
+            target[(z, x) + inner] = fold_rows(total[start : start + rows]).astype(BF16)
 
 
 def project_kernel(info, tok, left, right, wq, wk, wv, taps, q_out, k_out, v_out, pool_out, tt_out, x, cells, *, row_len):
@@ -195,7 +225,7 @@
     ny = parts // 2
     step = pl.program_id(0)
     width = w_in.shape[1]
-    rc = in_keep.shape[1]
+    rc = D // parts
     mine = info[5]
     hidden = pl.ds(pl.multiple_of(block_of(step, info, parts) * width, width), width)
     gain_one, bias_one = vecs[0:1, :], vecs[1:2, :]
@@ -239,19 +269,19 @@
     def _():
         inner_grad = (nt(feed_grad[...], w_back[...]) * slope[:, hidden].astype(F32)).astype(BF16)
         act_t = act[:, hidden].T
-        back = nn(act_t, feed_grad[...]).astype(BF16)
+        back = nn(act_t, feed_grad[...])
 
         @pl.when(step < parts + ny)
         def _():
-            back_send[0] = back
+            store_chunks(back_send.at[0], back)
 
         @pl.when(step >= parts + ny)
         def _():
-            back_keep[0] = back
+            store_chunks(back_keep.at[0], back)
 
         for y in range(ny):
-            in_send[y] = nn(low_t[rows_of(y, 1 - mine), :], inner_grad).astype(BF16)
-            in_keep[y] = nn(low_t[rows_of(y, mine), :], inner_grad).astype(BF16)
+            store_chunks(in_send.at[y], nn(low_t[rows_of(y, 1 - mine), :], inner_grad), (0,))
+            store_chunks(in_keep.at[y], nn(low_t[rows_of(y, mine), :], inner_grad), (0,))
         feed[...] += nt(inner_grad, w_in[...])
 
     @pl.when(step == 2 * parts - 1)
@@ -268,8 +298,8 @@
         dop[...] = (attended_grad * rp[...]).astype(BF16)
         low_t[...] = att[...].T
         for y in range(ny):
-            out_send[y] = nn(low_t[rows_of(y, 1 - mine), :], branch_grad).astype(BF16)
-            out_keep[y] = nn(low_t[rows_of(y, mine), :], branch_grad).astype(BF16)
+            store_chunks(out_send.at[y], nn(low_t[rows_of(y, 1 - mine), :], branch_grad))
+            store_chunks(out_keep.at[y], nn(low_t[rows_of(y, mine), :], branch_grad))
 
 
 def score_delta(grad, attended):
@@ -344,19 +374,23 @@
 
 
 def query_grad_kernel(info, tt, dq, wq, sum_grad, keep, send, part):
-    ny, rc = keep.shape[0], keep.shape[1]
+    ny = keep.shape[0]
+    rc = D // (2 * ny)
     mine = info[5]
     for y in range(ny):
         for target, core in ((send, 1 - mine), (keep, mine)):
             rows = pl.ds(pl.multiple_of((2 * y + core) * rc, rc), rc)
-            target[y] = nn(tt[rows, :], dq[...]).astype(BF16)
+            store_chunks(target.at[y], nn(tt[rows, :], dq[...]))
     part[...] = sum_grad[...] + nt(dq[...], wq[...])
 
 
 def key_grad_kernel(info, tt, own, above, below, k, v, wk, wv, part, sums, taps, *rest, row_len, pieces):
     pooled = rest[:pieces]
-    keep, send, tokens_grad, acc, cells, g, small, small_t, k_low, v_low = rest[pieces:]
-    ny, rc = keep.shape[0], keep.shape[1]
+    k_keep, k_send, v_keep, v_send, s_keep, s_send, tokens_grad = rest[pieces : pieces + 7]
+    acc, cells, g, small, small_t, k_low, v_low = rest[pieces + 7 :]
+    ny, nz, nx = k_keep.shape[:3]
+    rc = D // (2 * ny)
+    few = rc // (nz * nx)
     count = part.shape[0]
     size = count // 4
     mine = info[5]
@@ -386,13 +420,19 @@
                 product = g[0:size, :] * masks[tap] * taken
                 small[8 + tap : 9 + tap, lanes] += jnp.sum(product, axis=0, keepdims=True)
             low[:, lanes] = grad[...].astype(BF16)
-    small_t[...] = small[...].T.astype(BF16)
+    small_t[...] = small[...].T
     for y in range(ny):
-        for target, core in ((send, 1 - mine), (keep, mine)):
+        sides = ((k_send, v_send, s_send, 1 - mine), (k_keep, v_keep, s_keep, mine))
+        for k_part, v_part, s_part, core in sides:
             rows = pl.ds(pl.multiple_of((2 * y + core) * rc, rc), rc)
-            target[y, :, 0:D] = nn(tt[rows, :], k_low[...]).astype(BF16)
-            target[y, :, D : 2 * D] = nn(tt[rows, :], v_low[...]).astype(BF16)
-            target[y, :, 2 * D :] = small_t[rows, :]
+            store_chunks(k_part.at[y], nn(tt[rows, :], k_low[...]))
+            store_chunks(v_part.at[y], nn(tt[rows, :], v_low[...]))
+            vectors = small_t[rows, :]
+            for z in range(nz):
+                for x in range(nx):
+                    start = (z * nx + x) * few
+                    s_part[y, z, x] = jnp.zeros(s_part.shape[3:], BF16)
+                    s_part[y, z, x, 0:few] = vectors[start : start + few].astype(BF16)
     total = part[...] + nt(k_low[...], wk[...])
     tokens_grad[...] = (total + nt(v_low[...], wv[...])).astype(BF16)
 
@@ -405,29 +445,199 @@
     return pairs
 
 
-def swap_stage(parts, dim, axis, count, stride):
-    mine = (lax.axis_index(axis) // stride) % count
-    total = lax.dynamic_index_in_dim(parts, mine, dim, keepdims=False)
-    for hop in range(1, count):
-        block = lax.dynamic_index_in_dim(parts, (mine + hop) % count, dim, keepdims=False)
-        moved = lax.ppermute(block.astype(BF16), axis, hop_pairs(axis, count, stride, hop))
-        total = total + moved.astype(F32)
-    return total
-
-
-def scatter_sum(keep, send, seq_first):
-    seq, dp = lax.axis_size("seq"), lax.axis_size("dp")
-    moved = lax.ppermute(send, "seq", hop_pairs("seq", 2, 1, 1))
-    parts = keep.astype(F32) + moved.astype(F32)
-    near = 2 if dp % 2 == 0 else 1
-    parts = parts.reshape(seq // 2, dp // near, near, parts.shape[1] // dp, parts.shape[2])
-    if seq_first:
-        parts = swap_stage(parts, 0, "seq", seq // 2, 2)
-        parts = swap_stage(parts, 1, "dp", near, 1)
-    else:
-        parts = swap_stage(parts, 2, "dp", near, 1)
-        parts = swap_stage(parts, 0, "seq", seq // 2, 2)
-    return swap_stage(parts, 0, "dp", dp // near, near)
+MESH_ID = pl.DeviceIdType.MESH
+
+
+class Summed:
+    def __init__(self, seq_first, keep, send, bufs):
+        self.seq_first = seq_first
+        self.keep, self.send = keep, send
+        self.core_in, self.one_in, self.two_in, self.three_in, self.out_sem, self.in_sem = bufs
+        self.ny, self.nz, self.nx = keep.shape[:3]
+        here, row = lax.axis_index("seq"), lax.axis_index("dp")
+        self.y, self.core = here // 2, here % 2
+        self.z, self.x = row // self.nx, row % self.nx
+        self.row, self.here = row, here
+
+    def copy(self, src, dst, slot, device):
+        return pltpu.make_async_remote_copy(
+            src_ref=src,
+            dst_ref=dst,
+            send_sem=self.out_sem.at[slot],
+            recv_sem=self.in_sem.at[slot],
+            device_id=device,
+            device_id_type=MESH_ID,
+        )
+
+    def core_copies(self):
+        partner = (self.y * 2 + 1 - self.core, self.row)
+        copies = []
+        for i in range(self.ny):
+            block = (self.y + 1 + i) % self.ny
+            copies.append(self.copy(self.send.at[block], self.core_in.at[block], i, partner))
+        return copies
+
+    def y_copies(self, two):
+        copies = []
+        for hop in range(1, self.ny):
+            other = (self.y + hop) % self.ny
+            device = (other * 2 + self.core, self.row)
+            source = self.keep.at[other, :, self.x] if two else self.keep.at[other]
+            into = self.two_in if two else self.one_in
+            slot = (self.ny + self.nx - 1 if two else self.ny) + hop - 1
+            copies.append(self.copy(source, into.at[hop - 1], slot, device))
+        return copies
+
+    def x_copies(self, two):
+        copies = []
+        for hop in range(1, self.nx):
+            other = (self.x + hop) % self.nx
+            device = (self.here, self.z * self.nx + other)
+            source = self.keep.at[self.y, :, other] if two else self.keep.at[:, :, other]
+            into = self.two_in if two else self.one_in
+            slot = (2 * self.ny - 1 if two else self.ny) + hop - 1
+            copies.append(self.copy(source, into.at[hop - 1], slot, device))
+        return copies
+
+    def one_copies(self):
+        return self.y_copies(False) if self.seq_first else self.x_copies(False)
+
+    def two_copies(self):
+        return self.x_copies(True) if self.seq_first else self.y_copies(True)
+
+    def three_copies(self):
+        copies = []
+        for hop in range(1, self.nz):
+            other = (self.z + hop) % self.nz
+            device = (self.here, other * self.nx + self.x)
+            slot = 2 * self.ny + self.nx - 2 + hop - 1
+            source = self.keep.at[self.y, other, self.x]
+            copies.append(self.copy(source, self.three_in.at[hop - 1], slot, device))
+        return copies
+
+    def start(self):
+        for copy in self.core_copies():
+            copy.start()
+
+    def add_core(self):
+        copies = self.core_copies()
+        for i, copy in enumerate(copies):
+            block = (self.y + 1 + i) % self.ny
+            copy.wait_recv()
+            self.keep[block] = self.keep[block] + self.core_in[block]
+            if self.seq_first and i < self.ny - 1:
+                self.one_copies()[i].start()
+        if not self.seq_first:
+            for copy in self.one_copies():
+                copy.start()
+
+    def add_one(self):
+        for hop, copy in enumerate(self.one_copies()):
+            copy.wait_recv()
+            if self.seq_first:
+                self.keep[self.y] = self.keep[self.y] + self.one_in[hop]
+            else:
+                for y in range(self.ny):
+                    for z in range(self.nz):
+                        total = self.keep[y, z, self.x] + self.one_in[hop, y, z]
+                        self.keep[y, z, self.x] = total
+        for copy in self.two_copies():
+            copy.start()
+
+    def add_two(self):
+        for hop, copy in enumerate(self.two_copies()):
+            copy.wait_recv()
+            for z in range(self.nz):
+                total = self.keep[self.y, z, self.x] + self.two_in[hop, z]
+                self.keep[self.y, z, self.x] = total
+        for copy in self.three_copies():
+            copy.start()
+
+    def total(self):
+        total = self.keep[self.y, self.z, self.x].astype(F32)
+        for hop, copy in enumerate(self.three_copies()):
+            copy.wait_recv()
+            total = total + self.three_in[hop].astype(F32)
+        return total
+
+    def finish(self):
+        copies = self.core_copies() + self.one_copies() + self.two_copies() + self.three_copies()
+        for copy in copies:
+            copy.wait_send()
+
+
+def summed_scratch(shape, seq_first):
+    ny, nz, nx = shape[:3]
+    chunk = shape[3:]
+    one = (ny - 1, nz, nx) if seq_first else (nx - 1, ny, nz)
+    two = (nx - 1, nz) if seq_first else (ny - 1, nz)
+    slots = 2 * ny + nx + nz - 3
+    return [
+        pltpu.VMEM(shape, BF16),
+        pltpu.VMEM(one + chunk, BF16),
+        pltpu.VMEM(two + chunk, BF16),
+        pltpu.VMEM((nz - 1,) + chunk, BF16),
+        pltpu.SemaphoreType.DMA((slots,)),
+        pltpu.SemaphoreType.DMA((slots,)),
+    ]
+
+
+def greet(ny, nz, nx):
+    here, row = lax.axis_index("seq"), lax.axis_index("dp")
+    y, core, z, x = here // 2, here % 2, row // nx, row % nx
+    peers = [(y * 2 + 1 - core, row)]
+    peers += [(((y + hop) % ny) * 2 + core, row) for hop in range(1, ny)]
+    peers += [(here, z * nx + (x + hop) % nx) for hop in range(1, nx)]
+    peers += [(here, ((z + hop) % nz) * nx + x) for hop in range(1, nz)]
+    barrier = pltpu.get_barrier_semaphore()
+    for peer in peers:
+        pl.semaphore_signal(barrier, inc=1, device_id=peer, device_id_type=MESH_ID)
+    pl.semaphore_wait(barrier, len(peers))
+
+
+def sum_kernel(*refs, order, grid):
+    n = len(order)
+    keeps, sends, outs = refs[:n], refs[n : 2 * n], refs[2 * n : 3 * n]
+    rest = refs[3 * n :]
+    held, local = rest[:n], rest[n]
+    greet(*grid)
+    units = []
+    for i in range(n):
+        units.append(Summed(order[i], held[i], sends[i], rest[n + 1 + 6 * i : n + 7 + 6 * i]))
+    loads = [pltpu.make_async_copy(keeps[i], held[i], local.at[i]) for i in range(n)]
+    for unit, load in zip(units, loads):
+        unit.start()
+        load.start()
+    for unit, load in zip(units, loads):
+        load.wait()
+        unit.add_core()
+    for unit in units:
+        unit.add_one()
+    for unit in units:
+        unit.add_two()
+    for unit, out in zip(units, outs):
+        out[...] = unit.total()
+    for unit in units:
+        unit.finish()
+
+
+def sum_all(keeps, sends, order):
+    grid = keeps[0].shape[:3]
+    outs = tuple(jax.ShapeDtypeStruct(a.shape[3:], F32) for a in keeps)
+    scratch = [pltpu.VMEM(a.shape, BF16) for a in keeps] + [pltpu.SemaphoreType.DMA((len(order),))]
+    for a, seq_first in zip(keeps, order):
+        scratch += summed_scratch(a.shape, seq_first)
+    return pl.pallas_call(
+        partial(sum_kernel, order=order, grid=grid),
+        out_shape=outs,
+        in_specs=[pl.BlockSpec(memory_space=pl.ANY)] * (2 * len(order)),
+        out_specs=[pl.BlockSpec(memory_space=pltpu.VMEM)] * len(order),
+        scratch_shapes=scratch,
+        compiler_params=pltpu.CompilerParams(
+            collective_id=0, has_side_effects=True, vmem_limit_bytes=56 * MB
+        ),
+        name="sum_all",
+    )(*keeps, *sends)
 
 
 def shifted(block, by):
@@ -492,7 +702,6 @@
     row_len = count * seq
     span = count + 2 * HALF
     size = count // 4
-    rc = D // seq
     here = lax.axis_index("seq")
     core, y = here % 2, here // 2
     owners = []
@@ -597,9 +806,13 @@
 
     width = FF // seq
     args = (attention, near_scale, pool_scale, tok, og, vecs, w_out, w_in, w_back)
-    half_in = shape((ny, rc, FF), BF16)
-    half_back = shape((ny, width, D), BF16)
-    half_out = shape((ny, rc, D), BF16)
+    dp = lax.axis_size("dp")
+    nx = 2 if dp % 2 == 0 else 1
+    nz = dp // nx
+    rows = D // (seq * dp)
+    half_in = shape((ny, nz, nx, seq) + folded(rows, width), BF16)
+    half_back = shape((ny, nz, nx) + folded(FF // (seq * dp), D), BF16)
+    half_out = shape((ny, nz, nx) + folded(rows, D), BF16)
     outs = (
         shape((count, D), BF16),
         shape((count, D), F32),
@@ -614,8 +827,8 @@
         shape((8, D), F32),
     )
     in_columns = pl.BlockSpec(
-        (ny, rc, width),
-        lambda i, info: (0, 0, block_of(jnp.maximum(i, seq), info, seq)),
+        (ny, nz, nx, 1) + half_in.shape[4:],
+        lambda i, info: (0, 0, 0, block_of(jnp.maximum(i, seq), info, seq), 0, 0),
     )
     (
         mixed,
@@ -644,10 +857,12 @@
             in_columns,
             in_columns,
             pl.BlockSpec(
-                (1, width, D), lambda i, info: (jnp.maximum(i - seq - ny, 0), 0, 0)
+                (1,) + half_back.shape[1:],
+                lambda i, info: (jnp.maximum(i - seq - ny, 0), 0, 0, 0, 0),
             ),
             pl.BlockSpec(
-                (1, width, D), lambda i, info: (jnp.clip(i - seq, 0, ny - 1), 0, 0)
+                (1,) + half_back.shape[1:],
+                lambda i, info: (jnp.clip(i - seq, 0, ny - 1), 0, 0, 0, 0),
             ),
         ]
         + [whole(a) for a in outs[8:]],
@@ -668,9 +883,6 @@
         58,
         "dense",
     )
-    sum_in = scatter_sum(in_keep, in_send, True)
-    sum_back = scatter_sum(back_keep, back_send, False)
-    sum_out = scatter_sum(out_keep, out_send, True)
 
     args = (queries, pool_grad, attention, pool_e) + tuple(pieces)
     half_pool = shape((ny, 2, size + EXTRA, D), BF16)
@@ -733,12 +945,11 @@
         32,
         "query_grad",
     )
-    sum_query = scatter_sum(query_keep, query_send, False)
 
     args = (tok_t, own, above, below, keys, values, w_key, w_value, part, sums, taps) + tuple(pooled)
-    half_both = shape((ny, rc, 2 * D + LANES), BF16)
-    outs = (half_both, half_both, shape((count, D), BF16))
-    both_keep, both_send, tokens_grad = call(
+    half_small = shape((ny, nz, nx, -(-rows // 16) * 16, LANES), BF16)
+    outs = (half_out, half_out, half_out, half_out, half_small, half_small, shape((count, D), BF16))
+    key_keep, key_send, value_keep, value_send, small_keep, small_send, tokens_grad = call(
         partial(key_grad_kernel, row_len=row_len, pieces=len(pooled)),
         info,
         args,
@@ -751,7 +962,7 @@
             pltpu.VMEM((span, LANES), F32),
             pltpu.VMEM((size + EXTRA, LANES), F32),
             pltpu.VMEM((LANES, D), F32),
-            pltpu.VMEM((D, LANES), BF16),
+            pltpu.VMEM((D, LANES), F32),
             pltpu.VMEM((count, D), BF16),
             pltpu.VMEM((count, D), BF16),
         ],
@@ -759,15 +970,21 @@
         56,
         "key_grad",
     )
-    sum_key = scatter_sum(both_keep[:, :, :D], both_send[:, :, :D], True)
-    sum_rest = scatter_sum(both_keep[:, :, D:], both_send[:, :, D:], False)
-    vectors = sum_rest[:, D:]
+    totals = sum_all(
+        (in_keep, back_keep, out_keep, query_keep, key_keep, value_keep, small_keep),
+        (in_send, back_send, out_send, query_send, key_send, value_send, small_send),
+        (True, False, True, False, True, False, False),
+    )
+    sum_in = jnp.concatenate([unfold_rows(totals[0][g], rows) for g in range(seq)], axis=1)
+    sum_back = unfold_rows(totals[1], FF // (seq * dp))
+    sum_out, sum_query, sum_key, sum_value = (unfold_rows(t, rows) for t in totals[2:6])
+    vectors = totals[6][:rows]
     return (
         mixed[None],
         tokens_grad[None],
         sum_query,
         sum_key,
-        sum_rest[:, :D],
+        sum_value,
         sum_out,
         sum_in,
         sum_back,

time: 291 us -> 278 us (0.955)
  Pallas kernels: 102 us -> 209 us
  waiting for transfers between devices: 78.2 us -> 11.2 us
  starting transfers between devices: 56.1 us -> 14.1 us
  other arithmetic: 15.9 us -> 3.54 us
    pallas_call x0 -> x1, Pallas kernels: none -> 107 us  [sum_all(): pl.pallas_call(partial(sum_kernel, order=order, grid=grid), out_shape=out...]
    ppermute x36 -> x0, waiting for transfers between devices: 60.1 us -> none  [the longest x30 60.1 us: swap_stage(): lax.ppermute(block.astype(BF16), axis, hop_pairs(axis, count, stride, hop))]
    ppermute x36 -> x0, starting transfers between devices: 43.2 us -> none  [the longest x30 40.8 us: swap_stage(): lax.ppermute(block.astype(BF16), axis, hop_pairs(axis, count, stride, hop))]
    add x24 -> x0, other arithmetic: 13.9 us -> none  [the longest x18 7.72 us: swap_stage(): total = total + moved.astype(F32)]
    ppermute x1, waiting for transfers between devices: 7.16 us -> 0.01 us  [per_device(): lax.ppermute(both.astype(BF16), 'seq', hop_pairs('seq', ny, 2, hop))]
    unnamed x95 -> x87, local copies, waits for them, and re-layouts: 23.9 us -> 28.7 us
    convert_element_type x18 -> x0, local copies, waits for them, and re-layouts: 3.39 us -> none  [swap_stage(): block.astype(BF16)]
  transfers between devices with their start and end apart: 45 -> 9, of which waited for: 16 -> 2; matrix products, arithmetic and copies ran while one was open for 9% -> 1% of each run, Pallas kernels for 7% -> 8%
where the time goes in v3:
time: 278 us; the launch traced here: 277 us
  Pallas kernels  209 us (75%)
  local copies, waits for them, and re-layouts  37.6 us (14%)
  starting transfers between devices  14.1 us (5%)
  waiting for transfers between devices  11.2 us (4%)
  other arithmetic  3.54 us (1%)
    pallas_call x1, Pallas kernels, sum_all(): pl.pallas_call(partial(sum_kernel, order=order, grid=grid), out_shape=out...  107 us
    pallas_call x8, Pallas kernels, call(): pl.pallas_call(kernel, grid_spec=pltpu.PrefetchScalarGridSpec(num_scalar_...  101 us
    unnamed x87, local copies, waits for them, and re-layouts  28.7 us
    ppermute x1, waiting for transfers between devices, per_device(): lax.ppermute(pool_own, 'seq', hop_pairs('seq', ny, 2, ny - hop))  9.17 us
    ppermute x4, starting transfers between devices, shifted(): lax.ppermute(block, 'seq', [(i, i + by) for i in range(size) if 0 <= i +...  8.66 us
  transfers between devices with their start and end apart: 9, of which 2 were waited for; matrix products, arithmetic and copies ran while one was open for 1% of the time, Pallas kernels for 8%

profile of v3, /device:TPU:0, one launch (start us, length us, event | category | flops | bytes accessed | tf_op | source)
XLA Modules:
  0.0 276.6 jit_solution(3089527349335664098)
XLA Ops:
  1.6 1.3 collective-permute-start.1
  2.9 3.0 %collective-permute-start = (bf16[64,768]{1,0:T(8,128)(2,1)S(1)}, bf16[64,768]{1,0:T(8,128)(2,1)S(1)}, u32[]{:S(2)}, u32[]{:S(2)}) collective-permute-start(bf16[64,768]{1,0:T(8,128)(2,1)S(1)} %get-tuple-element.138), channel_id=1, source_target_pairs={{0,8},{8,16},{16,24},{1,9},{9,17},{17,25},{2,10},{10,18},{18,26},{... | collective-permute-start | bytes 294920 | tf_op jit(solution)/shard_map/ppermute | solution.py:645
  7.9 1.3 copy-done.2
  9.2 1.3 copy-done.3
  11.6 1.3 copy-done.13
  12.9 3.1 %project.1 = (bf16[512,768]{1,0:T(8,128)(2,1)S(1)}, bf16[640,768]{1,0:T(8,128)(2,1)S(1)}, bf16[640,768]{1,0:T(8,128)(2,1)S(1)}, bf16[2,128,768]{2,1,0:T(8,128)(2,1)S(1)}, bf16[768,512]{1,0:T(8,128)(2,1)S(1)}) custom-call(s32[16]{0:T(128)S(1)} %concatenate.21.info, bf16[512,768]{1,0:T(8,128)(2,1)S(1)} %bitcast.39, ...), custom_call_target="tpu_custom_call" | custom-call | flops 2113929216 | bytes 8478720 | tf_op jit(solution)/shard_map/project/pallas_call | solution.py:650
  16.8 4.5 %collective-permute-start.2 = (bf16[2,128,768]{2,1,0:T(8,128)(2,1)S(1)}, bf16[2,128,768]{2,1,0:T(8,128)(2,1)}, u32[]{:S(2)}, u32[]{:S(2)}) collective-permute-start(bf16[2,128,768]{2,1,0:T(8,128)(2,1)S(1)} %get-tuple-element.65.rest_0_), channel_id=1, source_target_pairs={{0,16},{8,24},{16,0},{24,8},{1,17},{9,25},{17,1},{25,9},{2,18},{10... | collective-permute-start | bytes 1179656 | tf_op jit(solution)/shard_map/ppermute | solution.py:761
  21.4 9.2 %collective-permute-done.2.rest_1_ = bf16[2,128,768]{2,1,0:T(8,128)(2,1)} collective-permute-done((bf16[2,128,768]{2,1,0:T(8,128)(2,1)S(1)}, bf16[2,128,768]{2,1,0:T(8,128)(2,1)}, u32[]{:S(2)}, u32[]{:S(2)}) %collective-permute-start.2) | collective-permute-done | bytes 393248 | tf_op jit(solution)/shard_map/ppermute | solution.py:761
  32.4 8.9 %near_forward.1 = (bf16[12,4,256,128]{3,2,1,0:T(8,128)(2,1)S(1)}, f32[768,512]{1,0:T(8,128)S(1)}, f32[6,8,512]{2,1,0:T(8,128)S(1)}) custom-call(s32[16]{0:T(128)S(1)} %concatenate.21.info, bf16[512,768]{1,0:T(8,128)(2,1)S(1)} %copy-done.22, bf16[640,768]{1,0:T(8,128)(2,1)S(1)} %get-tuple-element.61.k.refs_4_, bf16[640,768]{1,0:T(8,128)(2,1)S(1)} %get-tuple-element.62.v.refs_5_), custom_call_target="tpu_custom_call" | custom-call | flops 1610612736 | bytes 7569408 | tf_op jit(solution)/shard_map/near_forward/pallas_call | solution.py:650
  41.3 1.7 copy-done.16
  43.0 14.2 %pool_forward.1 = (bf16[12,512,512]{2,1,0:T(8,128)(2,1)S(1)}, f32[512,768]{1,0:T(8,128)S(1)}, f32[512,768]{1,0:T(8,128)S(1)}, f32[512,768]{1,0:T(8,128)S(1)}) custom-call(s32[16]{0:T(128)S(1)} %concatenate.21.info, bf16[512,768]{1,0:T(8,128)(2,1)S(1)} %copy-done.22, f32[768,512]{1,0:T(8,128)S(1)} %get-tuple-element.63.o_near, ...), custom_call_target="tpu_custom_call" | custom-call | flops 3221225472 | bytes 15040512 | tf_op jit(solution)/shard_map/pool_forward/pallas_call | solution.py:650
  58.4 2.7 copy-done.25
  62.2 1.2 copy-done.28
  63.5 38.7 %dense.1 = (bf16[512,768]{1,0:T(8,128)(2,1)}, f32[512,768]{1,0:T(8,128)}, bf16[512,768]{1,0:T(8,128)(2,1)}, bf16[512,768]{1,0:T(8,128)(2,1)}, bf16[2,4,2,4,48,38...) custom-call(s32[16]{0:T(128)} %copy-done.11, ...), custom_call_target="tpu_custom_call" | custom-call | flops 16307453952 | bytes 31506432 | tf_op jit(solution)/shard_map/dense/pallas_call | solution.py:650
  102.2 2.8 %copy-done.26 = bf16[12,512,512]{2,1,0:T(8,128)(2,1)S(1)} copy-done((bf16[12,512,512]{2,1,0:T(8,128)(2,1)S(1)}, bf16[12,512,512]{2,1,0:T(8,128)(2,1)}, u32[]{:S(2)}) %copy-start.26) | copy-done | bytes 6291480
  106.1 12.3 %pool_backward.1 = (bf16[2,2,144,768]{3,2,1,0:T(8,128)(2,1)S(1)}, bf16[2,2,144,768]{3,2,1,0:T(8,128)(2,1)S(1)}, f32[768,512]{1,0:T(8,128)S(1)}) custom-call(s32[16]{0:T(128)S(1)} %copy-done.12, bf16[512,768]{1,0:T(8,128)(2,1)S(1)} %copy-done.23, bf16[512,768]{1,0:T(8,128)(2,1)S(1)} %copy-done.29, f32[512,768]{1,0:T(8,128)S(1)} %copy-done.19, ...), custom_call_target="tpu_custom_call" | custom-call | flops 6442450944 | bytes 14352384 | tf_op jit(solution)/shard_map/pool_backward/pallas_call | solution.py:650
  119.0 2.1 collective-permute-done.7
  121.5 11.6 %near_backward.1 = (f32[2,512,768]{2,1,0:T(8,128)S(1)}, bf16[2,64,768]{2,1,0:T(8,128)(2,1)S(1)}, bf16[2,64,768]{2,1,0:T(8,128)(2,1)S(1)}, bf16[512,768]{1,0:T(8,128)(2,1)S(1)}) custom-call(s32[16]{0:T(128)S(1)} %copy-done.12, bf16[512,768]{1,0:T(8,128)(2,1)S(1)} %copy-done.23, bf16[512,768]{1,0:T(8,128)(2,1)S(1)} %copy-done.24, f32[512,768]{1,0:T(8,128)S(1)} %copy-done.20, ...), custom_call_target="tpu_custom_call" | custom-call | flops 3221225472 | bytes 14155776 | tf_op jit(solution)/shard_map/near_backward/pallas_call | solution.py:650
  133.2 1.3 collective-permute-start.5
  134.5 3.0 %collective-permute-start.6 = (bf16[2,64,768]{2,1,0:T(8,128)(2,1)S(1)}, bf16[2,64,768]{2,1,0:T(8,128)(2,1)S(1)}, u32[]{:S(2)}, u32[]{:S(2)}) collective-permute-start(bf16[2,64,768]{2,1,0:T(8,128)(2,1)S(1)} %get-tuple-element.78), channel_id=1, source_target_pairs={{0,8},{8,16},{16,24},{1,9},{9,17},{17,25},{2,10},{10,18},{18,26},{... | collective-permute-start | bytes 589832 | tf_op jit(solution)/shard_map/ppermute | solution.py:645
  138.3 2.0 query_grad.1
  144.3 10.6 %key_grad.1 = (bf16[2,4,2,48,384]{4,3,2,1,0:T(8,128)(2,1)}, bf16[2,4,2,48,384]{4,3,2,1,0:T(8,128)(2,1)}, bf16[2,4,2,48,384]{4,3,2,1,0:T(8,128)(2,1)}, bf16[2,4,2...) custom-call(s32[16]{0:T(128)} %copy-done.11, ...), custom_call_target="tpu_custom_call" | custom-call | flops 2415919104 | bytes 15007744 | tf_op jit(solution)/shard_map/key_grad/pallas_call | solution.py:650
  154.9 107.5 %sum_all.1 = (f32[4,48,384]{2,1,0:T(8,128)}, f32[96,768]{1,0:T(8,128)}, f32[48,384]{1,0:T(8,128)}, f32[48,384]{1,0:T(8,128)}, f32[48,384]{1,0:T(8,128)}, /*index=5*/f32[48,384]{1,0:T(8,128)}, f32[32,128]{1,0:T(8,128)}) custom-call(bf16[2,4,2,4,48,384]{5,4,3,2,1,0:T(8,128)(2,1)} %get-tuple-element.86.refs_0_, ...), custom_call_target="tpu_custom_call" | custom-call | tf_op jit(solution)/shard_map/sum_all/pallas_call | solution.py:630
  262.3 1.6 slice_reduce_fusion
  (112 shorter events, 28.3 us)
Async XLA Ops:
  1.6 6.3 %collective-permute-start.1 = (bf16[64,768]{1,0:T(8,128)(2,1)S(1)}, bf16[64,768]{1,0:T(8,128)(2,1)S(1)}, u32[]{:S(2)}, u32[]{:S(2)}) collective-permute-start(bf16[64,768]{1,0:T(8,128)(2,1)S(1)} %get-tuple-element.137), channel_id=1, source_target_pairs={{8,0},{16,8},{24,16},{9,1},{17,9},{25,17},{10,2},{18,10},{26,18},{... | collective-permute-start | bytes 294920 | tf_op jit(solution)/shard_map/ppermute | solution.py:645
  2.9 5.0 %collective-permute-start = (bf16[64,768]{1,0:T(8,128)(2,1)S(1)}, bf16[64,768]{1,0:T(8,128)(2,1)S(1)}, u32[]{:S(2)}, u32[]{:S(2)}) collective-permute-start(bf16[64,768]{1,0:T(8,128)(2,1)S(1)} %get-tuple-element.138), channel_id=1, source_target_pairs={{0,8},{8,16},{16,24},{1,9},{9,17},{17,25},{2,10},{10,18},{18,26},{... | collective-permute-start | bytes 294920 | tf_op jit(solution)/shard_map/ppermute | solution.py:645
  7.9 35.2 %copy-start.11 = (s32[16]{0:T(128)}, s32[16]{0:T(128)S(1)}, u32[]{:S(2)}) copy-start(s32[16]{0:T(128)S(1)} %concatenate.21.info) | copy-start | bytes 196
  12.8 17.7 %copy-start.35 = (f32[768]{0:T(1024)S(1)}, f32[768]{0:T(1024)}, u32[]{:S(2)}) copy-start(f32[768]{0:T(1024)} %param.22) | copy-start | bytes 9220
  12.8 17.7 %copy-start.36 = (f32[768]{0:T(1024)S(1)}, f32[768]{0:T(1024)}, u32[]{:S(2)}) copy-start(f32[768]{0:T(1024)} %param.23) | copy-start | bytes 9220
  12.8 17.7 %copy-start.37 = (f32[768]{0:T(1024)S(1)}, f32[768]{0:T(1024)}, u32[]{:S(2)}) copy-start(f32[768]{0:T(1024)} %param.24) | copy-start | bytes 9220
  12.9 17.8 %copy-start.38 = (f32[768]{0:T(1024)S(1)}, f32[768]{0:T(1024)}, u32[]{:S(2)}) copy-start(f32[768]{0:T(1024)} %param.25) | copy-start | bytes 9220
  16.8 104.7 %copy-start.4 = (bf16[640,768]{1,0:T(8,128)(2,1)}, bf16[640,768]{1,0:T(8,128)(2,1)S(1)}, u32[]{:S(2)}) copy-start(bf16[640,768]{1,0:T(8,128)(2,1)S(1)} %get-tuple-element.61.k.refs_4_) | copy-start | bytes 2949124
  16.8 104.7 %copy-start.5 = (bf16[640,768]{1,0:T(8,128)(2,1)}, bf16[640,768]{1,0:T(8,128)(2,1)S(1)}, u32[]{:S(2)}) copy-start(bf16[640,768]{1,0:T(8,128)(2,1)S(1)} %get-tuple-element.62.v.refs_5_) | copy-start | bytes 2949124
  16.8 121.5 %copy-start.6 = (bf16[768,512]{1,0:T(8,128)(2,1)}, bf16[768,512]{1,0:T(8,128)(2,1)S(1)}, u32[]{:S(2)}) copy-start(bf16[768,512]{1,0:T(8,128)(2,1)S(1)} %get-tuple-element.70.tt) | copy-start | bytes 2359300
  16.8 13.7 %collective-permute-start.2 = (bf16[2,128,768]{2,1,0:T(8,128)(2,1)S(1)}, bf16[2,128,768]{2,1,0:T(8,128)(2,1)}, u32[]{:S(2)}, u32[]{:S(2)}) collective-permute-start(bf16[2,128,768]{2,1,0:T(8,128)(2,1)S(1)} %get-tuple-element.65.rest_0_), channel_id=1, source_target_pairs={{0,16},{8,24},{16,0},{24,8},{1,17},{9,25},{17,1},{25,9},{2,18},{10... | collective-permute-start | bytes 1179656 | tf_op jit(solution)/shard_map/ppermute | solution.py:761
  21.4 21.6 %collective-permute-start.3 = (bf16[2,128,768]{2,1,0:T(8,128)(2,1)S(1)}, bf16[2,128,768]{2,1,0:T(8,128)(2,1)}, u32[]{:S(2)}, u32[]{:S(2)}) collective-permute-start(bf16[2,128,768]{2,1,0:T(8,128)(2,1)S(1)} %get-tuple-element.65.rest_0_), channel_id=1, source_target_pairs={{0,8},{8,0},{16,24},{24,16},{1,9},{9,1},{17,25},{25,17},{2,10},{10... | collective-permute-start | bytes 1179656 | tf_op jit(solution)/shard_map/ppermute | solution.py:762
  30.6 12.5 %collective-permute-start.4 = (bf16[2,128,768]{2,1,0:T(8,128)(2,1)}, bf16[2,128,768]{2,1,0:T(8,128)(2,1)}, u32[]{:S(2)}, u32[]{:S(2)}) collective-permute-start(bf16[2,128,768]{2,1,0:T(8,128)(2,1)} %collective-permute-done.2.rest_1_), channel_id=1, source_target_pairs={{0,8},{8,0},{16,24},{24,16},{1,9},{9,1},{17,25},{25,17},{2,10},{10... | collective-permute-start | bytes 1179656 | tf_op jit(solution)/shard_map/ppermute | solution.py:762
  63.5 38.7 %copy-start.12 = (s32[16]{0:T(128)S(1)}, s32[16]{0:T(128)}, u32[]{:S(2)}) copy-start(s32[16]{0:T(128)} %copy-done.11) | copy-start | bytes 196
  63.5 38.7 %copy-start.19 = (f32[512,768]{1,0:T(8,128)S(1)}, f32[512,768]{1,0:T(8,128)}, u32[]{:S(2)}) copy-start(f32[512,768]{1,0:T(8,128)} %copy-done.18) | copy-start | bytes 4718596
  63.5 38.7 %copy-start.23 = (bf16[512,768]{1,0:T(8,128)(2,1)S(1)}, bf16[512,768]{1,0:T(8,128)(2,1)}, u32[]{:S(2)}) copy-start(bf16[512,768]{1,0:T(8,128)(2,1)} %copy-done.21) | copy-start | bytes 2359300
  106.1 15.4 %copy-start.20 = (f32[512,768]{1,0:T(8,128)S(1)}, f32[512,768]{1,0:T(8,128)}, u32[]{:S(2)}) copy-start(f32[512,768]{1,0:T(8,128)} %copy-done.18) | copy-start | bytes 4718596
  106.1 15.4 %copy-start.24 = (bf16[512,768]{1,0:T(8,128)(2,1)S(1)}, bf16[512,768]{1,0:T(8,128)(2,1)}, u32[]{:S(2)}) copy-start(bf16[512,768]{1,0:T(8,128)(2,1)} %get-tuple-element.71.refs_1_) | copy-start | bytes 2359300
  118.4 2.6 collective-permute-start.7
  121.1 22.2 %collective-permute-start.8 = (bf16[1,2,144,768]{3,2,1,0:T(8,128)(2,1)S(1)}, bf16[1,2,144,768]{3,2,1,0:T(8,128)(2,1)S(1)}, u32[]{:S(2)}, u32[]{:S(2)}) collective-permute-start(bf16[1,2,144,768]{3,2,1,0:T(8,128)(2,1)S(1)} %add_convert_fusion), channel_id=1, source_target_pairs={{0,16},{8,24},{16,0},{24,8},{1,17},{9,25},{17,1},{25,9},{2,18},{10... | collective-permute-start | bytes 1327112 | tf_op jit(solution)/shard_map/ppermute | solution.py:907
  121.5 16.8 %copy-start.14 = (bf16[768,768]{1,0:T(8,128)(2,1)S(1)}, bf16[768,768]{1,0:T(8,128)(2,1)}, u32[]{:S(2)}) copy-start(bf16[768,768]{1,0:T(8,128)(2,1)} %wq.3) | copy-start | bytes 3538948
  121.5 16.8 %copy-start.15 = (f32[512,768]{1,0:T(8,128)S(1)}, f32[512,768]{1,0:T(8,128)}, u32[]{:S(2)}) copy-start(f32[512,768]{1,0:T(8,128)} %get-tuple-element.80.sum_grad) | copy-start | bytes 4718596
  133.2 10.2 %collective-permute-start.5 = (bf16[2,64,768]{2,1,0:T(8,128)(2,1)S(1)}, bf16[2,64,768]{2,1,0:T(8,128)(2,1)S(1)}, u32[]{:S(2)}, u32[]{:S(2)}) collective-permute-start(bf16[2,64,768]{2,1,0:T(8,128)(2,1)S(1)} %get-tuple-element.77), channel_id=1, source_target_pairs={{8,0},{16,8},{24,16},{9,1},{17,9},{25,17},{10,2},{18,10},{26,18},{... | collective-permute-start | bytes 589832 | tf_op jit(solution)/shard_map/ppermute | solution.py:645
  134.5 8.9 %collective-permute-start.6 = (bf16[2,64,768]{2,1,0:T(8,128)(2,1)S(1)}, bf16[2,64,768]{2,1,0:T(8,128)(2,1)S(1)}, u32[]{:S(2)}, u32[]{:S(2)}) collective-permute-start(bf16[2,64,768]{2,1,0:T(8,128)(2,1)S(1)} %get-tuple-element.78), channel_id=1, source_target_pairs={{0,8},{8,16},{16,24},{1,9},{9,17},{17,25},{2,10},{10,18},{18,26},{... | collective-permute-start | bytes 589832 | tf_op jit(solution)/shard_map/ppermute | solution.py:645
  (24 other events, 69.8 us)

commit v4 on v2

--- a/solution.py
+++ b/solution.py
@@ -53,7 +53,50 @@
     return (same & (center < row_len)).astype(F32)
 
 
-def project_kernel(info, tok, left, right, wq, wk, wv, taps, q_out, k_out, v_out, pool_out, tt_out, x, cells, *, row_len):
+def folds(rows, width):
+    return 2 if rows % 16 and rows % 8 == 0 and (width // 2) % LANES == 0 else 1
+
+
+def folded(rows, width):
+    fold = folds(rows, width)
+    return (rows * fold, width // fold)
+
+
+def fold_rows(block):
+    rows, width = block.shape
+    fold = folds(rows, width)
+    part = width // fold
+    return jnp.concatenate([block[:, i * part : (i + 1) * part] for i in range(fold)], axis=0)
+
+
+def unfold_rows(block, rows):
+    fold = block.shape[0] // rows
+    return jnp.concatenate([block[i * rows : (i + 1) * rows] for i in range(fold)], axis=1)
+
+
+def store_chunks(target, total):
+    nz, nx = target.shape[0], target.shape[1]
+    rows = total.shape[0] // (nz * nx)
+    for z in range(nz):
+        for x in range(nx):
+            start = (z * nx + x) * rows
+            target[z, x] = fold_rows(total[start : start + rows]).astype(BF16)
+
+
+def store_blocks(target, total):
+    units, _, nz, nx, part, wide = target.shape
+    rows = total.shape[0] // (nz * nx)
+    across = total.shape[1] // wide
+    for z in range(nz):
+        for x in range(nx):
+            start = (z * nx + x) * rows
+            for unit in range(units):
+                top = start + (unit // across) * part
+                left = (unit % across) * wide
+                target[unit, 0, z, x] = total[top : top + part, left : left + wide].astype(BF16)
+
+
+def project_kernel(info, tok, left, right, wq, wk, wv, taps, q_out, k_out, v_out, pool_out, tt_out, mask_out, x, cells, *, row_len):
     count = tok.shape[0]
     x[0:HALF] = left[...]
     x[HALF : HALF + count] = tok[...]
@@ -75,6 +118,13 @@
             pool_out[which, :, lanes] = total.astype(BF16)
     q_out[...] = (nn(tok[...], wq[...]).astype(BF16).astype(F32) * 0.125).astype(BF16)
     tt_out[...] = tok[...].T
+    lane = iota((count // 4, LANES), 1)
+    for shift in range(2):
+        total = jnp.zeros((count // 4, LANES), F32)
+        for tap in range(5):
+            mask = tap_mask(info, tap, shift, count // 4, row_len)
+            total = jnp.where(lane == tap, mask, total)
+        mask_out[shift] = total
 
 
 def near_forward_kernel(info, q, k, v, e_out, o_out, st_out, bias, *, row_len):
@@ -195,7 +245,7 @@
     ny = parts // 2
     step = pl.program_id(0)
     width = w_in.shape[1]
-    rc = in_keep.shape[1]
+    rc = D // parts
     mine = info[5]
     hidden = pl.ds(pl.multiple_of(block_of(step, info, parts) * width, width), width)
     gain_one, bias_one = vecs[0:1, :], vecs[1:2, :]
@@ -239,19 +289,19 @@
     def _():
         inner_grad = (nt(feed_grad[...], w_back[...]) * slope[:, hidden].astype(F32)).astype(BF16)
         act_t = act[:, hidden].T
-        back = nn(act_t, feed_grad[...]).astype(BF16)
+        back = nn(act_t, feed_grad[...])
 
         @pl.when(step < parts + ny)
         def _():
-            back_send[0] = back
+            store_blocks(back_send, back)
 
         @pl.when(step >= parts + ny)
         def _():
-            back_keep[0] = back
+            store_blocks(back_keep, back)
 
         for y in range(ny):
-            in_send[y] = nn(low_t[rows_of(y, 1 - mine), :], inner_grad).astype(BF16)
-            in_keep[y] = nn(low_t[rows_of(y, mine), :], inner_grad).astype(BF16)
+            store_chunks(in_send.at[0, y], nn(low_t[rows_of(y, 1 - mine), :], inner_grad))
+            store_chunks(in_keep.at[0, y], nn(low_t[rows_of(y, mine), :], inner_grad))
         feed[...] += nt(inner_grad, w_in[...])
 
     @pl.when(step == 2 * parts - 1)
@@ -268,133 +318,13 @@
         dop[...] = (attended_grad * rp[...]).astype(BF16)
         low_t[...] = att[...].T
         for y in range(ny):
-            out_send[y] = nn(low_t[rows_of(y, 1 - mine), :], branch_grad).astype(BF16)
-            out_keep[y] = nn(low_t[rows_of(y, mine), :], branch_grad).astype(BF16)
+            store_chunks(out_send.at[y], nn(low_t[rows_of(y, 1 - mine), :], branch_grad))
+            store_chunks(out_keep.at[y], nn(low_t[rows_of(y, mine), :], branch_grad))
 
 
 def score_delta(grad, attended):
     pick = ((iota((8, LANES), 1) // 64) == iota((8, LANES), 0)).astype(F32)
     return nt(pick, grad.astype(F32) * attended, precision=lax.Precision.HIGHEST)
-
-
-def pool_backward_kernel(info, q, grad, o, e, *rest, pieces):
-    kv = rest[:pieces]
-    keep, send, dq_out, dk, dv = rest[pieces:]
-    ny = pieces // 2
-    count = q.shape[0]
-    size = kv[0].shape[1]
-    delta = score_delta(grad[...], o[...])
-    kp = jnp.concatenate([piece[0] for piece in kv], axis=0)
-    kt = kp.T
-    vp = jnp.concatenate([piece[1] for piece in kv], axis=0)
-    wide = min(256, count)
-    for head in range(2):
-        for b in range(count // wide):
-            cols = slice(b * wide, (b + 1) * wide)
-            gh = head_half(grad[cols, :], head)
-            qh = head_half(q[cols, :], head)
-            low = e[head, :, cols]
-            dp = nt(vp, gh) - delta[head : head + 1, cols]
-            ds = (low.astype(F32) * dp).astype(BF16)
-            key_part = nn(ds, qh)
-            value_part = nn(low, gh)
-            if head == 0 and b == 0:
-                dk[...] = key_part
-                dv[...] = value_part
-            else:
-                dk[...] += key_part
-                dv[...] += value_part
-            dq_out[head * 64 : head * 64 + 64, cols] = nn(kt[head * 64 : head * 64 + 64], ds)
-    for i in range(pieces):
-        target = keep if i < ny else send
-        after = pl.ds(pl.multiple_of(info[8 + pieces + i] * size, size), EXTRA)
-        for which, total in ((0, dk), (1, dv)):
-            target[i % ny, which, 0:size] = total[i * size : (i + 1) * size].astype(BF16)
-            target[i % ny, which, size:] = total[after, :].astype(BF16)
-
-
-def near_backward_kernel(q, grad, o, e, k, v, dq_pool, own, before, behind, dq_out, dk, dv):
-    count = q.shape[0]
-    delta = score_delta(grad[...], o[...])
-    kt = k[...].T
-    dk[...] = jnp.zeros_like(dk)
-    dv[...] = jnp.zeros_like(dv)
-    for b in range(count // QB):
-        cols = slice(b * QB, (b + 1) * QB)
-        keys = slice(b * QB, (b + 2) * QB)
-        lows, scores, grads, queries, dqs = [], [], [], [], []
-        for head in range(2):
-            gh = head_half(grad[cols, :], head)
-            low = e[head, b]
-            dp = nt(v[keys, :], gh) - delta[head : head + 1, cols]
-            ds = (low.astype(F32) * dp).astype(BF16)
-            dqs.append(nn(kt[head * 64 : head * 64 + 64, keys], ds))
-            lows.append(low)
-            scores.append(ds)
-            grads.append(gh)
-            queries.append(head_half(q[cols, :], head))
-        dk[keys, :] += nn(jnp.concatenate(scores, axis=1), jnp.concatenate(queries, axis=0))
-        dv[keys, :] += nn(jnp.concatenate(lows, axis=1), jnp.concatenate(grads, axis=0))
-        total = (jnp.concatenate(dqs, axis=0) + dq_pool[:, cols]) * 0.125
-        dq_out[cols, :] = total.T.astype(BF16)
-    for which, total in ((0, dk), (1, dv)):
-        before[which] = total[0:HALF].astype(BF16)
-        own[which] = total[HALF : HALF + count]
-        behind[which] = total[HALF + count :].astype(BF16)
-
-
-def query_grad_kernel(info, tt, dq, wq, sum_grad, keep, send, part):
-    ny, rc = keep.shape[0], keep.shape[1]
-    mine = info[5]
-    for y in range(ny):
-        for target, core in ((send, 1 - mine), (keep, mine)):
-            rows = pl.ds(pl.multiple_of((2 * y + core) * rc, rc), rc)
-            target[y] = nn(tt[rows, :], dq[...]).astype(BF16)
-    part[...] = sum_grad[...] + nt(dq[...], wq[...])
-
-
-def key_grad_kernel(info, tt, own, above, below, k, v, wk, wv, part, sums, taps, *rest, row_len, pieces):
-    pooled = rest[:pieces]
-    keep, send, tokens_grad, acc, cells, g, small, small_t, k_low, v_low = rest[pieces:]
-    ny, rc = keep.shape[0], keep.shape[1]
-    count = part.shape[0]
-    size = count // 4
-    mine = info[5]
-    small[...] = jnp.zeros_like(small)
-    small[0:8] = sums[...]
-    masks = [tap_mask(info, tap, 0, size, row_len) for tap in range(5)]
-    next_masks = [tap_mask(info, tap, 1, size, row_len) for tap in range(2)]
-    moves = ((2, 0, 0), (3, 1, 0), (4, 2, 0), (0, 2, 1), (1, 3, 1))
-    for which, source, low in ((0, k, k_low), (1, v, v_low)):
-        for c in range(D // LANES):
-            lanes = slice(c * LANES, (c + 1) * LANES)
-            grad = acc.at[c]
-            grad[...] = own[which, :, lanes]
-            grad[0:HALF, :] += below[which, :, lanes].astype(F32)
-            grad[count - HALF :, :] += above[which, :, lanes].astype(F32)
-            cells[...] = source[:, lanes].astype(F32)
-            total = pooled[0][0, which, :, lanes].astype(F32)
-            for piece in pooled[1:]:
-                total = total + piece[0, which, :, lanes].astype(F32)
-            g[...] = total
-            for tap, place, shift in moves:
-                mask = next_masks[tap] if shift else masks[tap]
-                spread = g[shift : shift + size, :] * mask * taps[tap : tap + 1, lanes]
-                grad[pl.ds(place, size, stride=4), :] += spread
-            for tap in range(5):
-                taken = cells[pl.ds(HALF + tap - 2, size, stride=4), :]
-                product = g[0:size, :] * masks[tap] * taken
-                small[8 + tap : 9 + tap, lanes] += jnp.sum(product, axis=0, keepdims=True)
-            low[:, lanes] = grad[...].astype(BF16)
-    small_t[...] = small[...].T.astype(BF16)
-    for y in range(ny):
-        for target, core in ((send, 1 - mine), (keep, mine)):
-            rows = pl.ds(pl.multiple_of((2 * y + core) * rc, rc), rc)
-            target[y, :, 0:D] = nn(tt[rows, :], k_low[...]).astype(BF16)
-            target[y, :, D : 2 * D] = nn(tt[rows, :], v_low[...]).astype(BF16)
-            target[y, :, 2 * D :] = small_t[rows, :]
-    total = part[...] + nt(k_low[...], wk[...])
-    tokens_grad[...] = (total + nt(v_low[...], wv[...])).astype(BF16)
 
 
 def hop_pairs(axis, count, stride, hop):
@@ -405,29 +335,491 @@
     return pairs
 
 
-def swap_stage(parts, dim, axis, count, stride):
-    mine = (lax.axis_index(axis) // stride) % count
-    total = lax.dynamic_index_in_dim(parts, mine, dim, keepdims=False)
-    for hop in range(1, count):
-        block = lax.dynamic_index_in_dim(parts, (mine + hop) % count, dim, keepdims=False)
-        moved = lax.ppermute(block.astype(BF16), axis, hop_pairs(axis, count, stride, hop))
-        total = total + moved.astype(F32)
-    return total
-
-
-def scatter_sum(keep, send, seq_first):
-    seq, dp = lax.axis_size("seq"), lax.axis_size("dp")
-    moved = lax.ppermute(send, "seq", hop_pairs("seq", 2, 1, 1))
-    parts = keep.astype(F32) + moved.astype(F32)
-    near = 2 if dp % 2 == 0 else 1
-    parts = parts.reshape(seq // 2, dp // near, near, parts.shape[1] // dp, parts.shape[2])
-    if seq_first:
-        parts = swap_stage(parts, 0, "seq", seq // 2, 2)
-        parts = swap_stage(parts, 1, "dp", near, 1)
-    else:
-        parts = swap_stage(parts, 2, "dp", near, 1)
-        parts = swap_stage(parts, 0, "seq", seq // 2, 2)
-    return swap_stage(parts, 0, "dp", dp // near, near)
+MESH_ID = pl.DeviceIdType.MESH
+
+
+class Summed:
+    def __init__(self, seq_first, sends, keep, core_in, one_in, two_in, three_in, out_sem, in_sem):
+        self.seq_first = seq_first
+        self.sends, self.keep = sends, keep
+        self.core_in, self.one_in, self.two_in, self.three_in = core_in, one_in, two_in, three_in
+        self.out_sem, self.in_sem = out_sem, in_sem
+        self.units, self.ny, self.nz, self.nx = keep.shape[:4]
+        self.here, self.row = lax.axis_index("seq"), lax.axis_index("dp")
+        self.y, self.mine = self.here // 2, self.here % 2
+        self.z, self.x = self.row // self.nx, self.row % self.nx
+
+    def copy(self, u, src, dst, slot, device):
+        return pltpu.make_async_remote_copy(
+            src_ref=src,
+            dst_ref=dst,
+            send_sem=self.out_sem.at[u, slot],
+            recv_sem=self.in_sem.at[u, slot],
+            device_id=device,
+            device_id_type=MESH_ID,
+        )
+
+    def core_copy(self, u, i):
+        block = (self.y + 1 + i) % self.ny
+        partner = (self.y * 2 + 1 - self.mine, self.row)
+        return self.copy(u, self.sends[u].at[block], self.core_in.at[u, block], i, partner)
+
+    def y_copy(self, u, hop, two):
+        other = (self.y + hop) % self.ny
+        device = (other * 2 + self.mine, self.row)
+        if two:
+            slot = self.ny + self.nx - 1 + hop - 1
+            return self.copy(u, self.keep.at[u, other, :, self.x], self.two_in.at[u, hop - 1], slot, device)
+        return self.copy(u, self.keep.at[u, other], self.one_in.at[u, hop - 1], self.ny + hop - 1, device)
+
+    def x_copy(self, u, hop, two):
+        other = (self.x + hop) % self.nx
+        device = (self.here, self.z * self.nx + other)
+        if two:
+            slot = 2 * self.ny - 1 + hop - 1
+            return self.copy(u, self.keep.at[u, self.y, :, other], self.two_in.at[u, hop - 1], slot, device)
+        return self.copy(u, self.keep.at[u, :, :, other], self.one_in.at[u, hop - 1], self.ny + hop - 1, device)
+
+    def z_copy(self, u, hop):
+        other = (self.z + hop) % self.nz
+        device = (self.here, other * self.nx + self.x)
+        slot = 2 * self.ny + self.nx - 2 + hop - 1
+        return self.copy(u, self.keep.at[u, self.y, other, self.x], self.three_in.at[u, hop - 1], slot, device)
+
+    def one_copies(self, u):
+        if self.seq_first:
+            return [partial(self.y_copy, u, hop, False) for hop in range(1, self.ny)]
+        return [partial(self.x_copy, u, hop, False) for hop in range(1, self.nx)]
+
+    def two_copies(self, u):
+        if self.seq_first:
+            return [partial(self.x_copy, u, hop, True) for hop in range(1, self.nx)]
+        return [partial(self.y_copy, u, hop, True) for hop in range(1, self.ny)]
+
+    def three_copies(self, u):
+        return [partial(self.z_copy, u, hop) for hop in range(1, self.nz)]
+
+    def start(self, u):
+        for i in range(self.ny):
+            self.core_copy(u, i).start()
+
+    def core(self, u):
+        ones = self.one_copies(u)
+        for i in range(self.ny):
+            block = (self.y + 1 + i) % self.ny
+            self.core_copy(u, i).wait_recv()
+            for z in range(self.nz):
+                self.keep[u, block, z] = self.keep[u, block, z] + self.core_in[u, block, z]
+            if self.seq_first and i < self.ny - 1:
+                ones[i]().start()
+        if not self.seq_first:
+            for copy in ones:
+                copy().start()
+
+    def one(self, u):
+        for hop, copy in enumerate(self.one_copies(u)):
+            copy().wait_recv()
+            for z in range(self.nz):
+                if self.seq_first:
+                    total = self.keep[u, self.y, z] + self.one_in[u, hop, z]
+                    self.keep[u, self.y, z] = total
+                else:
+                    for y in range(self.ny):
+                        total = self.keep[u, y, z, self.x] + self.one_in[u, hop, y, z]
+                        self.keep[u, y, z, self.x] = total
+        for copy in self.two_copies(u):
+            copy().start()
+
+    def two(self, u):
+        for hop, copy in enumerate(self.two_copies(u)):
+            copy().wait_recv()
+            for z in range(self.nz):
+                total = self.keep[u, self.y, z, self.x] + self.two_in[u, hop, z]
+                self.keep[u, self.y, z, self.x] = total
+        for copy in self.three_copies(u):
+            copy().start()
+
+    def three(self, u):
+        total = self.keep[u, self.y, self.z, self.x].astype(F32)
+        for hop, copy in enumerate(self.three_copies(u)):
+            copy().wait_recv()
+            total = total + self.three_in[u, hop].astype(F32)
+        return total
+
+    def finish(self, u):
+        for i in range(self.ny):
+            self.core_copy(u, i).wait_send()
+        for copy in self.one_copies(u) + self.two_copies(u) + self.three_copies(u):
+            copy().wait_send()
+
+
+def summed_scratch(units, shape, seq_first):
+    ny, nz, nx = shape[:3]
+    chunk = shape[3:]
+    one = (units, ny - 1, nz, nx) if seq_first else (units, nx - 1, ny, nz)
+    two = (units, nx - 1, nz) if seq_first else (units, ny - 1, nz)
+    slots = 2 * ny + nx + nz - 3
+    return [
+        pltpu.VMEM((units,) + shape, BF16),
+        pltpu.VMEM((units,) + shape, BF16),
+        pltpu.VMEM(one + chunk, BF16),
+        pltpu.VMEM(two + chunk, BF16),
+        pltpu.VMEM((units, nz - 1) + chunk, BF16),
+        pltpu.SemaphoreType.DMA((units, slots)),
+        pltpu.SemaphoreType.DMA((units, slots)),
+    ]
+
+
+def greet(peers):
+    barrier = pltpu.get_barrier_semaphore()
+    for peer in peers:
+        pl.semaphore_signal(barrier, inc=1, device_id=peer, device_id_type=MESH_ID)
+    pl.semaphore_wait(barrier, len(peers))
+
+
+def events(units_in, units_back):
+    last = 3 * PAIRS
+    table = []
+    pairs = max(units_in, units_back)
+    for u in range(pairs):
+        for stack, count in (("in", units_in), ("back", units_back)):
+            if u < count:
+                table.append((min(2 + 3 * u, last), stack, u, "core"))
+                table.append((min(8 + 4 * u, last), stack, u, "one"))
+                table.append((min(11 + 4 * u, last), stack, u, "two"))
+                table.append((min(15 + 4 * u, last), stack, u, "three"))
+    table.append((14, "sqy", 0, "core"))
+    table.append((15, "sqx", 0, "core"))
+    rank = {"core": 0, "one": 1, "two": 2, "three": 3}
+    table.sort(key=lambda row: (row[0], row[2] + rank[row[3]]))
+    tail = [
+        ("sqy", 1, "core"), ("sqx", 1, "core"), ("small", 0, "core"),
+        ("sqy", 0, "one"), ("sqx", 0, "one"),
+        ("sqy", 1, "one"), ("sqx", 1, "one"), ("small", 0, "one"),
+        ("sqy", 0, "two"), ("sqx", 0, "two"),
+        ("sqy", 1, "two"), ("sqx", 1, "two"), ("small", 0, "two"),
+        ("sqy", 0, "three"), ("sqx", 0, "three"),
+        ("sqy", 1, "three"), ("sqx", 1, "three"), ("small", 0, "three"),
+    ]
+    return table, tail
+
+
+class Refs:
+    pass
+
+
+def backward_kernel(*refs, names, pieces):
+    r = Refs()
+    for name, ref in zip(names, refs):
+        setattr(r, name, ref)
+    kv = [getattr(r, "piece%d" % i) for i in range(pieces)]
+    seq, ny = pieces, pieces // 2
+    step = pl.program_id(0)
+    count = r.q.shape[0]
+    size = count // 4
+    nz, nx = r.in_keep.shape[2:4]
+    here, row = lax.axis_index("seq"), lax.axis_index("dp")
+    y, core = here // 2, here % 2
+    partner = (y * 2 + 1 - core, row)
+    right, left = ((here + 1) % seq, row), ((here + seq - 1) % seq, row)
+    stacks = {}
+    sends = {
+        "in": [r.in_send.at[u] for u in range(r.in_send.shape[0])],
+        "back": [r.back_send.at[u] for u in range(r.back_send.shape[0])],
+        "sqy": [r.out_send, r.k_send],
+        "sqx": [r.q_send, r.v_send],
+        "small": [r.s_send],
+    }
+    for name, seq_first in STACKS:
+        bufs = [getattr(r, name + "_" + part) for part in BUFFERS]
+        stacks[name] = Summed(seq_first, sends[name], *bufs)
+
+    def copy(src, dst, out_sem, in_sem, device):
+        return pltpu.make_async_remote_copy(
+            src_ref=src, dst_ref=dst, send_sem=out_sem, recv_sem=in_sem,
+            device_id=device, device_id_type=MESH_ID,
+        )
+
+    def pool_core(p):
+        return copy(r.p_send.at[p], r.p_in.at[p], r.p_sem.at[0, p, 0], r.p_sem.at[1, p, 0], partner)
+
+    def pool_y(p, hop):
+        device = (((y + hop) % ny) * 2 + core, row)
+        return copy(
+            r.p_keep.at[p, hop], r.p_y.at[p, hop - 1], r.p_sem.at[0, p, hop], r.p_sem.at[1, p, hop], device
+        )
+
+    def halo(p, side):
+        device = right if side else left
+        return copy(
+            r.h_out.at[p, side], r.h_in.at[p, side], r.h_sem.at[0, p, side], r.h_sem.at[1, p, side], device
+        )
+
+    loads = [
+        pltpu.make_async_copy(r.out_keep, r.sqy_sum.at[0], r.l_sem.at[0]),
+        pltpu.make_async_copy(r.in_keep, r.in_sum, r.l_sem.at[1]),
+        pltpu.make_async_copy(r.back_keep, r.back_sum, r.l_sem.at[2]),
+        pltpu.make_async_copy(r.tt_any, r.tt, r.l_sem.at[3]),
+        pltpu.make_async_copy(r.wq_any, r.wq, r.l_sem.at[4]),
+        pltpu.make_async_copy(r.wk_any, r.wk, r.l_sem.at[5]),
+        pltpu.make_async_copy(r.wv_any, r.wv, r.l_sem.at[6]),
+        pltpu.make_async_copy(r.sg_any, r.sg, r.l_sem.at[7]),
+    ]
+
+    @pl.when(step == 0)
+    def _():
+        z, x = row // nx, row % nx
+        peers = [partner, right, left]
+        peers += [(((y + hop) % ny) * 2 + core, row) for hop in range(1, ny)]
+        peers += [(here, z * nx + (x + hop) % nx) for hop in range(1, nx)]
+        peers += [(here, ((z + hop) % nz) * nx + x) for hop in range(1, nz)]
+        greet(peers)
+        for u in range(max(len(sends["in"]), len(sends["back"]))):
+            for name in ("in", "back"):
+                if u < len(sends[name]):
+                    stacks[name].start(u)
+        stacks["sqy"].start(0)
+        for load in loads:
+            load.start()
+
+    @pl.when(step < PAIRS)
+    def _():
+        p = step
+        delta = score_delta(r.dop[...], r.o[...])
+        kp = jnp.concatenate([piece[0] for piece in kv], axis=0)
+        kt = kp.T
+        vp = jnp.concatenate([piece[1] for piece in kv], axis=0)
+        wide = min(256, count)
+        for head in range(2):
+            for b in range(count // wide):
+                cols = slice(b * wide, (b + 1) * wide)
+                gh = head_half(r.dop[cols, :], head)
+                qh = head_half(r.q[cols, :], head)
+                low = r.pool_e[head, :, cols]
+                dp = nt(vp, gh) - delta[head : head + 1, cols]
+                ds = (low.astype(F32) * dp).astype(BF16)
+                key_part = nn(ds, qh)
+                value_part = nn(low, gh)
+                if head == 0 and b == 0:
+                    r.dk[0 : seq * size] = key_part
+                    r.dv[0 : seq * size] = value_part
+                else:
+                    r.dk[0 : seq * size] += key_part
+                    r.dv[0 : seq * size] += value_part
+                r.dq_pool[p, head * 64 : head * 64 + 64, cols] = nn(kt[head * 64 : head * 64 + 64], ds)
+        for i in range(pieces):
+            target = r.p_keep if i < ny else r.p_send
+            after = (((y + i % ny) % ny) * 2 + (core + i // ny) % 2 + 1) % seq
+            index = ((after % 2 - core + 2) % 2) * ny + (after // 2 - y + ny) % ny
+            rows = pl.ds(pl.multiple_of(index * size, size), EXTRA)
+            for which, total in ((0, r.dk), (1, r.dv)):
+                target[p, i % ny, which, 0:size] = total[i * size : (i + 1) * size].astype(BF16)
+                target[p, i % ny, which, size:] = total[rows, :].astype(BF16)
+        pool_core(p).start()
+
+    @pl.when((step > 0) & (step <= PAIRS))
+    def _():
+        p = step - 1
+        pool_core(p).wait_recv()
+        for hop in range(1, ny):
+            for which in range(2):
+                r.p_keep[p, hop, which] = r.p_keep[p, hop, which] + r.p_in[p, hop, which]
+            pool_y(p, hop).start()
+
+    @pl.when((step >= PAIRS) & (step < 2 * PAIRS))
+    def _():
+        p = step - PAIRS
+        delta = score_delta(r.don[...], r.o[...])
+        kt = r.keys[...].T
+        r.dk[0 : count + 2 * HALF] = jnp.zeros((count + 2 * HALF, LANES), F32)
+        r.dv[0 : count + 2 * HALF] = jnp.zeros((count + 2 * HALF, LANES), F32)
+        for b in range(count // QB):
+            cols = slice(b * QB, (b + 1) * QB)
+            keys = slice(b * QB, (b + 2) * QB)
+            lows, scores, grads, queries, dqs = [], [], [], [], []
+            for head in range(2):
+                gh = head_half(r.don[cols, :], head)
+                low = r.near_e[head, b]
+                dp = nt(r.values[keys, :], gh) - delta[head : head + 1, cols]
+                ds = (low.astype(F32) * dp).astype(BF16)
+                dqs.append(nn(kt[head * 64 : head * 64 + 64, keys], ds))
+                lows.append(low)
+                scores.append(ds)
+                grads.append(gh)
+                queries.append(head_half(r.q[cols, :], head))
+            r.dk[keys, :] += nn(jnp.concatenate(scores, axis=1), jnp.concatenate(queries, axis=0))
+            r.dv[keys, :] += nn(jnp.concatenate(lows, axis=1), jnp.concatenate(grads, axis=0))
+            total = (jnp.concatenate(dqs, axis=0) + r.dq_pool[p, :, cols]) * 0.125
+            lanes = pl.ds(pl.multiple_of(p * LANES, LANES), LANES)
+            r.dq[cols, lanes] = total.T.astype(BF16)
+        for which, total in ((0, r.dk), (1, r.dv)):
+            r.h_out[p, 0, which] = total[0:HALF].astype(BF16)
+            r.acc[which, p] = total[HALF : HALF + count]
+            r.h_out[p, 1, which] = total[HALF + count : 2 * HALF + count].astype(BF16)
+
+        @pl.when(here > 0)
+        def _():
+            halo(p, 0).start()
+
+        @pl.when(here < seq - 1)
+        def _():
+            halo(p, 1).start()
+
+    def rows_of(block, mine):
+        rc = D // seq
+        return pl.ds(pl.multiple_of((2 * block + mine) * rc, rc), rc)
+
+    @pl.when(step == 2 * PAIRS)
+    def _():
+        for load in loads[3:]:
+            load.wait()
+        for block in range(ny):
+            store_chunks(r.q_send.at[block], nn(r.tt[rows_of(block, 1 - core), :], r.dq[...]))
+        stacks["sqx"].start(0)
+        for block in range(ny):
+            store_chunks(r.sqx_sum.at[0, block], nn(r.tt[rows_of(block, core), :], r.dq[...]))
+        r.sg[...] += nt(r.dq[...], r.wq[...])
+
+    @pl.when((step >= 2 * PAIRS) & (step < 3 * PAIRS))
+    def _():
+        p = step - 2 * PAIRS
+        lanes = pl.ds(pl.multiple_of(p * LANES, LANES), LANES)
+        for hop in range(1, ny):
+            pool_y(p, hop).wait_recv()
+
+        @pl.when(here < seq - 1)
+        def _():
+            halo(p, 0).wait_recv()
+            for which in range(2):
+                r.acc[which, p, count - HALF :, :] += r.h_in[p, 0, which].astype(F32)
+
+        @pl.when(here > 0)
+        def _():
+            halo(p, 1).wait_recv()
+            for which in range(2):
+                r.acc[which, p, 0:HALF, :] += r.h_in[p, 1, which].astype(F32)
+
+        moves = ((2, 0, 0), (3, 1, 0), (4, 2, 0), (0, 2, 1), (1, 3, 1))
+        sums = [jnp.zeros((1, LANES), F32)] * 5
+        for which, source, low in ((0, r.keys, r.k_low), (1, r.values, r.v_low)):
+            grad = r.acc.at[which, p]
+            r.cells[...] = source[...].astype(F32)
+            total = r.p_keep[p, 0, which].astype(F32) + r.p_in[p, 0, which].astype(F32)
+            for hop in range(1, ny):
+                total = total + r.p_y[p, hop - 1, which].astype(F32)
+            r.g[...] = total
+            for tap, place, shift in moves:
+                mask = r.masks[shift, :, tap : tap + 1]
+                spread = r.g[shift : shift + size, :] * mask * r.taps[tap : tap + 1, :]
+                grad[pl.ds(place, size, stride=4), :] += spread
+            for tap in range(5):
+                taken = r.cells[pl.ds(HALF + tap - 2, size, stride=4), :]
+                product = r.g[0:size, :] * r.masks[0, :, tap : tap + 1] * taken
+                sums[tap] = sums[tap] + jnp.sum(product, axis=0, keepdims=True)
+            low[:, lanes] = grad[...].astype(BF16)
+        for tap in range(5):
+            r.small[8 + tap : 9 + tap, lanes] = sums[tap]
+
+    last = 3 * PAIRS
+
+    @pl.when(step == last)
+    def _():
+        for name, index, send, low in (("sqy", 1, r.k_send, r.k_low), ("sqx", 1, r.v_send, r.v_low)):
+            keep = stacks[name].keep
+            for block in range(ny):
+                store_chunks(send.at[block], nn(r.tt[rows_of(block, 1 - core), :], low[...]))
+            stacks[name].start(index)
+            for block in range(ny):
+                store_chunks(keep.at[index, block], nn(r.tt[rows_of(block, core), :], low[...]))
+        r.small[0:8] = r.sums[...]
+        r.small[13:] = jnp.zeros((LANES - 13, D), F32)
+        r.small_t[...] = r.small[...].T
+        few = D // (seq * nz * nx)
+        for block in range(ny):
+            for part, mine in ((r.s_send.at[block], 1 - core), (r.small_sum.at[0, block], core)):
+                vectors = r.small_t[rows_of(block, mine), :]
+                for z in range(nz):
+                    for x in range(nx):
+                        start = (z * nx + x) * few
+                        part[z, x] = jnp.zeros(part.shape[2:], BF16)
+                        part[z, x, 0:few] = vectors[start : start + few].astype(BF16)
+        stacks["small"].start(0)
+        total = r.sg[...] + nt(r.k_low[...], r.wk[...])
+        r.tokens_grad[...] = (total + nt(r.v_low[...], r.wv[...])).astype(BF16)
+
+    results = {
+        "in": [r.t_in.at[u] for u in range(r.t_in.shape[0])],
+        "back": [r.t_back.at[u] for u in range(r.t_back.shape[0])],
+        "sqy": [r.t_out, r.t_key],
+        "sqx": [r.t_query, r.t_value],
+        "small": [r.t_small],
+    }
+
+    def run(name, u, stage):
+        done = getattr(stacks[name], stage)(u)
+        if stage == "three":
+            results[name][u][...] = done
+
+    table, tail = events(len(sends["in"]), len(sends["back"]))
+    for when in range(last + 1):
+        rows = [event[1:] for event in table if event[0] == when]
+        if when == last:
+            rows = rows + tail
+        if rows:
+
+            @pl.when(step == when)
+            def _(when=when, rows=rows):
+                if when == 2:
+                    for load in loads[:3]:
+                        load.wait()
+                for row in rows:
+                    run(*row)
+
+    @pl.when(step == last)
+    def _():
+        for name, _ in STACKS:
+            for u in range(len(sends[name])):
+                stacks[name].finish(u)
+        for p in range(PAIRS):
+            pool_core(p).wait_send()
+            for hop in range(1, ny):
+                pool_y(p, hop).wait_send()
+
+        @pl.when(here > 0)
+        def _():
+            for p in range(PAIRS):
+                halo(p, 0).wait_send()
+
+        @pl.when(here < seq - 1)
+        def _():
+            for p in range(PAIRS):
+                halo(p, 1).wait_send()
+
+
+STACKS = (("in", True), ("back", False), ("sqy", True), ("sqx", False), ("small", False))
+BUFFERS = ("sum", "core", "first", "second", "third", "out", "inn")
+
+
+def unpack_kernel(t_in, t_back, t_query, t_key, t_value, t_out, t_small, tg, *outs):
+    tokens_grad, query, key, value, out, inn, back = outs[:7]
+    rows = query.shape[0]
+    tokens_grad[...] = tg[...]
+    for source, target in ((t_query, query), (t_key, key), (t_value, value), (t_out, out)):
+        target[...] = unfold_rows(source[...], rows)
+    width = inn.shape[1] // t_in.shape[0]
+    for u in range(t_in.shape[0]):
+        inn[:, u * width : (u + 1) * width] = unfold_rows(t_in[u], rows)
+    units, part, wide = t_back.shape
+    across = back.shape[1] // wide
+    for u in range(units):
+        top, start = (u // across) * part, (u % across) * wide
+        back[top : top + part, start : start + wide] = t_back[u]
+    small = t_small[...]
+    pad = LANES - small.shape[0]
+    turned = jnp.concatenate([small, jnp.zeros((pad, LANES), F32)], axis=0).T
+    for i in range(4):
+        outs[7 + i][...] = turned[i : i + 1, 0:rows]
+    outs[11][...] = small[0:rows, 8:13]
 
 
 def shifted(block, by):
@@ -435,7 +827,7 @@
     return lax.ppermute(block, "seq", [(i, i + by) for i in range(size) if 0 <= i + by < size])
 
 
-def call(kernel, info, args, in_specs, outs, out_specs, grid, scratch, flops, vmem, name):
+def call(kernel, info, args, in_specs, outs, out_specs, grid, scratch, flops, name):
     moved = sum(a.size * a.dtype.itemsize for a in list(args) + list(outs))
     return pl.pallas_call(
         kernel,
@@ -448,7 +840,7 @@
         ),
         out_shape=outs,
         compiler_params=pltpu.CompilerParams(
-            vmem_limit_bytes=vmem * MB, dimension_semantics=("arbitrary",) * len(grid)
+            vmem_limit_bytes=60 * MB, dimension_semantics=("arbitrary",) * len(grid)
         ),
         cost_estimate=pl.CostEstimate(flops=flops, bytes_accessed=moved, transcendentals=0),
         name=name,
@@ -492,7 +884,6 @@
     row_len = count * seq
     span = count + 2 * HALF
     size = count // 4
-    rc = D // seq
     here = lax.axis_index("seq")
     core, y = here % 2, here // 2
     owners = []
@@ -529,8 +920,9 @@
         shape((span, D), BF16),
         shape((2, size, D), BF16),
         shape((D, count), BF16),
-    )
-    queries, keys, values, pool_own, tok_t = call(
+        shape((2, size, LANES), F32),
+    )
+    queries, keys, values, pool_own, tok_t, tap_masks = call(
         partial(project_kernel, row_len=row_len),
         info,
         args,
@@ -543,7 +935,6 @@
             pltpu.VMEM((D // LANES, span, LANES), F32),
         ],
         2 * D * D * (count + 2 * span),
-        40,
         "project",
     )
 
@@ -569,7 +960,6 @@
         (PAIRS,),
         [pltpu.VMEM((blocks, 2 * QB, QB), F32)],
         4 * H * 256 * 256 * count,
-        32,
         "near_forward",
     )
 
@@ -591,15 +981,20 @@
         (PAIRS,),
         [pltpu.VMEM((pool_all, count), F32)],
         4 * H * 512 * 256 * count,
-        32,
         "pool_forward",
     )
 
     width = FF // seq
     args = (attention, near_scale, pool_scale, tok, og, vecs, w_out, w_in, w_back)
-    half_in = shape((ny, rc, FF), BF16)
-    half_back = shape((ny, width, D), BF16)
-    half_out = shape((ny, rc, D), BF16)
+    dp = lax.axis_size("dp")
+    nx = 2 if dp % 2 == 0 else 1
+    nz = dp // nx
+    rows = D // (seq * dp)
+    back_rows = FF // (seq * dp)
+    down = 2 if back_rows % 32 == 0 else 1
+    half_in = shape((seq, ny, nz, nx) + folded(rows, width), BF16)
+    half_back = shape((2 * down, ny, nz, nx, back_rows // down, D // 2), BF16)
+    half_out = shape((ny, nz, nx) + folded(rows, D), BF16)
     outs = (
         shape((count, D), BF16),
         shape((count, D), F32),
@@ -614,8 +1009,8 @@
         shape((8, D), F32),
     )
     in_columns = pl.BlockSpec(
-        (ny, rc, width),
-        lambda i, info: (0, 0, block_of(jnp.maximum(i, seq), info, seq)),
+        (1,) + half_in.shape[1:],
+        lambda i, info: (block_of(jnp.maximum(i, seq), info, seq), 0, 0, 0, 0, 0),
     )
     (
         mixed,
@@ -644,10 +1039,12 @@
             in_columns,
             in_columns,
             pl.BlockSpec(
-                (1, width, D), lambda i, info: (jnp.maximum(i - seq - ny, 0), 0, 0)
+                (2 * down, 1) + half_back.shape[2:],
+                lambda i, info: (0, jnp.maximum(i - seq - ny, 0), 0, 0, 0, 0),
             ),
             pl.BlockSpec(
-                (1, width, D), lambda i, info: (jnp.clip(i - seq, 0, ny - 1), 0, 0)
+                (2 * down, 1) + half_back.shape[2:],
+                lambda i, info: (0, jnp.clip(i - seq, 0, ny - 1), 0, 0, 0, 0),
             ),
         ]
         + [whole(a) for a in outs[8:]],
@@ -665,117 +1062,184 @@
             pltpu.VMEM((count, D), BF16),
         ],
         2 * count * (3 * D * D + 6 * D * FF),
-        58,
         "dense",
     )
-    sum_in = scatter_sum(in_keep, in_send, True)
-    sum_back = scatter_sum(back_keep, back_send, False)
-    sum_out = scatter_sum(out_keep, out_send, True)
-
-    args = (queries, pool_grad, attention, pool_e) + tuple(pieces)
-    half_pool = shape((ny, 2, size + EXTRA, D), BF16)
-    outs = (half_pool, half_pool, shape((D, count), F32))
-    pool_keep, pool_send, dq_pool = call(
-        partial(pool_backward_kernel, pieces=seq),
+
+    half_small = shape((ny, nz, nx, -(-rows // 16) * 16, LANES), BF16)
+    half_pool = (PAIRS, ny, 2, size + EXTRA, LANES)
+    blocks_in = []
+
+    def block(name, array, spec):
+        blocks_in.append((name, array, spec))
+
+    def col_spec(array, index):
+        lead = (0,) * (len(array.shape) - 1)
+        return pl.BlockSpec(array.shape[:-1] + (LANES,), lambda i: lead + (index(i),))
+
+    def lead_spec(array, index):
+        rest = (0,) * (len(array.shape) - 1)
+        return pl.BlockSpec((2,) + array.shape[1:], lambda i: (index(i),) + rest)
+
+    def all_spec(array):
+        rest = (0,) * len(array.shape)
+        return pl.BlockSpec(array.shape, lambda i: rest)
+
+    def in_pool(i):
+        return jnp.minimum(i, PAIRS - 1)
+
+    def in_near(i):
+        return jnp.clip(i - PAIRS, 0, PAIRS - 1)
+
+    def in_both(i):
+        return jnp.minimum(i, 2 * PAIRS - 1) % PAIRS
+
+    def in_late(i):
+        return jnp.where(i < PAIRS, 0, jnp.minimum(i - PAIRS, 2 * PAIRS - 1) % PAIRS)
+
+    block("q", queries, col_spec(queries, in_both))
+    block("o", attention, col_spec(attention, in_both))
+    block("dop", pool_grad, col_spec(pool_grad, in_pool))
+    block("don", near_grad, col_spec(near_grad, in_near))
+    block("pool_e", pool_e, lead_spec(pool_e, in_pool))
+    block("near_e", near_e, lead_spec(near_e, in_near))
+    block("keys", keys, col_spec(keys, in_late))
+    block("values", values, col_spec(values, in_late))
+    for i, piece in enumerate(pieces):
+        block("piece%d" % i, piece, col_spec(piece, in_pool))
+    block("masks", tap_masks, all_spec(tap_masks))
+    block("taps", taps, col_spec(taps, in_late))
+    block("sums", sums, all_spec(sums))
+    anywhere = pl.BlockSpec(memory_space=pl.ANY)
+    for name, array in (
+        ("in_keep", in_keep),
+        ("in_send", in_send),
+        ("back_keep", back_keep),
+        ("back_send", back_send),
+        ("out_keep", out_keep),
+        ("out_send", out_send),
+        ("tt_any", tok_t),
+        ("wq_any", w_query),
+        ("wk_any", w_key),
+        ("wv_any", w_value),
+        ("sg_any", sum_grad),
+    ):
+        block(name, array, anywhere)
+    outs = [
+        ("t_in", shape((half_in.shape[0],) + half_in.shape[4:], F32)),
+        ("t_back", shape((half_back.shape[0],) + half_back.shape[4:], F32)),
+        ("t_query", shape(half_out.shape[3:], F32)),
+        ("t_key", shape(half_out.shape[3:], F32)),
+        ("t_value", shape(half_out.shape[3:], F32)),
+        ("t_out", shape(half_out.shape[3:], F32)),
+        ("t_small", shape(half_small.shape[3:], F32)),
+        ("tokens_grad", shape((count, D), BF16)),
+    ]
+    tall = max(pool_all, span)
+    scratch = [
+        ("dk", pltpu.VMEM((tall, LANES), F32)),
+        ("dv", pltpu.VMEM((tall, LANES), F32)),
+        ("dq_pool", pltpu.VMEM((PAIRS, LANES, count), F32)),
+        ("dq", pltpu.VMEM((count, D), BF16)),
+        ("acc", pltpu.VMEM((2, PAIRS, count, LANES), F32)),
+        ("k_low", pltpu.VMEM((count, D), BF16)),
+        ("v_low", pltpu.VMEM((count, D), BF16)),
+        ("cells", pltpu.VMEM((span, LANES), F32)),
+        ("g", pltpu.VMEM((size + EXTRA, LANES), F32)),
+        ("small", pltpu.VMEM((LANES, D), F32)),
+        ("small_t", pltpu.VMEM((D, LANES), F32)),
+        ("p_keep", pltpu.VMEM(half_pool, BF16)),
+        ("p_send", pltpu.VMEM(half_pool, BF16)),
+        ("p_in", pltpu.VMEM(half_pool, BF16)),
+        ("p_y", pltpu.VMEM((PAIRS, ny - 1) + half_pool[2:], BF16)),
+        ("h_out", pltpu.VMEM((PAIRS, 2, 2, HALF, LANES), BF16)),
+        ("h_in", pltpu.VMEM((PAIRS, 2, 2, HALF, LANES), BF16)),
+        ("p_sem", pltpu.SemaphoreType.DMA((2, PAIRS, ny))),
+        ("h_sem", pltpu.SemaphoreType.DMA((2, PAIRS, 2))),
+        ("l_sem", pltpu.SemaphoreType.DMA((8,))),
+        ("tt", pltpu.VMEM((D, count), BF16)),
+        ("wq", pltpu.VMEM((D, D), BF16)),
+        ("wk", pltpu.VMEM((D, D), BF16)),
+        ("wv", pltpu.VMEM((D, D), BF16)),
+        ("sg", pltpu.VMEM((count, D), F32)),
+        ("q_send", pltpu.VMEM(half_out.shape, BF16)),
+        ("k_send", pltpu.VMEM(half_out.shape, BF16)),
+        ("v_send", pltpu.VMEM(half_out.shape, BF16)),
+        ("s_send", pltpu.VMEM(half_small.shape, BF16)),
+    ]
+    sizes = {
+        "in": (half_in.shape[0], half_in.shape[1:]),
+        "back": (half_back.shape[0], half_back.shape[1:]),
+        "sqy": (2, half_out.shape),
+        "sqx": (2, half_out.shape),
+        "small": (1, half_small.shape),
+    }
+    for name, seq_first in STACKS:
+        bufs = summed_scratch(sizes[name][0], sizes[name][1], seq_first)
+        scratch += [(name + "_" + part, buf) for part, buf in zip(BUFFERS, bufs)]
+    names = [entry[0] for entry in blocks_in] + [entry[0] for entry in outs + scratch]
+    moved = sum(entry[1].size * entry[1].dtype.itemsize for entry in blocks_in)
+    totals = pl.pallas_call(
+        partial(backward_kernel, names=names, pieces=seq),
+        grid_spec=pltpu.PrefetchScalarGridSpec(
+            num_scalar_prefetch=0,
+            grid=(3 * PAIRS + 1,),
+            in_specs=[entry[2] for entry in blocks_in],
+            out_specs=[all_spec(entry[1]) for entry in outs],
+            scratch_shapes=[entry[1] for entry in scratch],
+        ),
+        out_shape=[entry[1] for entry in outs],
+        compiler_params=pltpu.CompilerParams(
+            collective_id=0,
+            has_side_effects=True,
+            vmem_limit_bytes=60 * MB,
+            dimension_semantics=("arbitrary",),
+        ),
+        cost_estimate=pl.CostEstimate(
+            flops=8 * H * 768 * 256 * count + 12 * count * D * D, bytes_accessed=moved, transcendentals=0
+        ),
+        name="backward",
+    )(*[entry[1] for entry in blocks_in])
+
+    outs = (
+        shape((count, D), BF16),
+        shape((rows, D), F32),
+        shape((rows, D), F32),
+        shape((rows, D), F32),
+        shape((rows, D), F32),
+        shape((rows, FF), F32),
+        shape((back_rows, D), F32),
+        shape((1, rows), F32),
+        shape((1, rows), F32),
+        shape((1, rows), F32),
+        shape((1, rows), F32),
+        shape((rows, 5), F32),
+    )
+    done = call(
+        lambda info, *refs: unpack_kernel(*refs),
         info,
-        args,
-        [columns(a) for a in args[:3]] + [leading(pool_e, 2)] + [columns(p) for p in pieces],
-        outs,
-        [columns(half_pool), columns(half_pool), leading(outs[2], LANES)],
-        (PAIRS,),
-        [pltpu.VMEM((pool_all, LANES), F32), pltpu.VMEM((pool_all, LANES), F32)],
-        8 * H * 512 * 256 * count,
-        32,
-        "pool_backward",
-    )
-    pool_moved = lax.ppermute(pool_send, "seq", hop_pairs("seq", 2, 1, 1))
-    pooled = [pool_keep[0:1], pool_moved[0:1]]
-    for hop in range(1, ny):
-        both = pool_keep[hop : hop + 1].astype(F32) + pool_moved[hop : hop + 1].astype(F32)
-        pooled.append(lax.ppermute(both.astype(BF16), "seq", hop_pairs("seq", ny, 2, hop)))
-
-    args = (queries, near_grad, attention, near_e, keys, values, dq_pool)
-    outs = (
-        shape((2, count, D), F32),
-        shape((2, HALF, D), BF16),
-        shape((2, HALF, D), BF16),
-        shape((count, D), BF16),
-    )
-    own, before, behind, query_grad = call(
-        lambda info, *refs: near_backward_kernel(*refs),
-        info,
-        args,
-        [columns(a) for a in args[:3]]
-        + [leading(near_e, 2), columns(keys), columns(values), leading(dq_pool, LANES)],
-        outs,
-        [columns(a) for a in outs],
-        (PAIRS,),
-        [pltpu.VMEM((span, LANES), F32), pltpu.VMEM((span, LANES), F32)],
-        8 * H * 256 * 256 * count,
-        32,
-        "near_backward",
-    )
-    above = shifted(before, -1)
-    below = shifted(behind, 1)
-
-    args = (tok_t, query_grad, w_query, sum_grad)
-    outs = (half_out, half_out, shape((count, D), F32))
-    query_keep, query_send, part = call(
-        query_grad_kernel,
-        info,
-        args,
-        [whole(a) for a in args],
+        tuple(totals),
+        [whole(a) for a in totals],
         outs,
         [whole(a) for a in outs],
         (1,),
         [],
-        4 * count * D * D,
-        32,
-        "query_grad",
-    )
-    sum_query = scatter_sum(query_keep, query_send, False)
-
-    args = (tok_t, own, above, below, keys, values, w_key, w_value, part, sums, taps) + tuple(pooled)
-    half_both = shape((ny, rc, 2 * D + LANES), BF16)
-    outs = (half_both, half_both, shape((count, D), BF16))
-    both_keep, both_send, tokens_grad = call(
-        partial(key_grad_kernel, row_len=row_len, pieces=len(pooled)),
-        info,
-        args,
-        [whole(a) for a in args],
-        outs,
-        [whole(a) for a in outs],
-        (1,),
-        [
-            pltpu.VMEM((D // LANES, count, LANES), F32),
-            pltpu.VMEM((span, LANES), F32),
-            pltpu.VMEM((size + EXTRA, LANES), F32),
-            pltpu.VMEM((LANES, D), F32),
-            pltpu.VMEM((D, LANES), BF16),
-            pltpu.VMEM((count, D), BF16),
-            pltpu.VMEM((count, D), BF16),
-        ],
-        8 * count * D * D,
-        56,
-        "key_grad",
-    )
-    sum_key = scatter_sum(both_keep[:, :, :D], both_send[:, :, :D], True)
-    sum_rest = scatter_sum(both_keep[:, :, D:], both_send[:, :, D:], False)
-    vectors = sum_rest[:, D:]
+        0,
+        "unpack",
+    )
     return (
         mixed[None],
-        tokens_grad[None],
-        sum_query,
-        sum_key,
-        sum_rest[:, :D],
-        sum_out,
-        sum_in,
-        sum_back,
-        vectors[:, 0],
-        vectors[:, 1],
-        vectors[:, 2],
-        vectors[:, 3],
-        vectors[:, 8:13],
+        done[0][None],
+        done[1],
+        done[2],
+        done[3],
+        done[4],
+        done[5],
+        done[6],
+        done[7].reshape(rows),
+        done[8].reshape(rows),
+        done[9].reshape(rows),
+        done[10].reshape(rows),
+        done[11],
     )
 
 

time: 291 us -> 207 us (0.71)
  Pallas kernels: 102 us -> 179 us
  waiting for transfers between devices: 78.2 us -> 9.99 us
  starting transfers between devices: 56.1 us -> 7.89 us
  local copies, waits for them, and re-layouts: 35.9 us -> 6.48 us
  other arithmetic: 15.9 us -> 0.83 us
    pallas_call x0 -> x1, Pallas kernels: none -> 105 us  [per_device(): pl.pallas_call(partial(backward_kernel, names=names, pieces=seq), grid_sp...]
    ppermute x38 -> x0, waiting for transfers between devices: 67.3 us -> none  [the longest x30 60.1 us: swap_stage(): lax.ppermute(block.astype(BF16), axis, hop_pairs(axis, count, stride, hop))]
    ppermute x38 -> x0, starting transfers between devices: 44.1 us -> none  [the longest x30 40.8 us: swap_stage(): lax.ppermute(block.astype(BF16), axis, hop_pairs(axis, count, stride, hop))]
    pallas_call x8 -> x5, Pallas kernels: 102 us -> 74.3 us  [call(): pl.pallas_call(kernel, grid_spec=pltpu.PrefetchScalarGridSpec(num_scalar_...]
    unnamed x95 -> x19, local copies, waits for them, and re-layouts: 23.9 us -> 2.94 us
    add x24 -> x0, other arithmetic: 13.9 us -> none  [the longest x18 7.72 us: swap_stage(): total = total + moved.astype(F32)]
    slice x7 -> x0, local copies, waits for them, and re-layouts: 6.26 us -> none  [the longest x2 2.68 us: per_device(): pooled = [pool_keep[0:1], pool_moved[0:1]]]
    ppermute x4 -> x2, starting transfers between devices: 7.98 us -> 4.33 us  [shifted(): lax.ppermute(block, 'seq', [(i, i + by) for i in range(size) if 0 <= i +...]
  transfers between devices with their start and end apart: 45 -> 5, of which waited for: 16 -> 1; matrix products, arithmetic and copies ran while one was open for 9% -> 2% of each run, Pallas kernels for 7% -> 5%
where the time goes in v4:
time: 207 us; the launch traced here: 206 us
  Pallas kernels  179 us (86%)
  waiting for transfers between devices  9.99 us (5%)
  starting transfers between devices  7.89 us (4%)
  local copies, waits for them, and re-layouts  6.48 us (3%)
    pallas_call x1, Pallas kernels, per_device(): pl.pallas_call(partial(backward_kernel, names=names, pieces=seq), grid_sp...  105 us
    pallas_call x5, Pallas kernels, call(): pl.pallas_call(kernel, grid_spec=pltpu.PrefetchScalarGridSpec(num_scalar_...  74.3 us
    ppermute x1, waiting for transfers between devices, per_device(): lax.ppermute(pool_own, 'seq', hop_pairs('seq', ny, 2, ny - hop))  9.98 us
    ppermute x2, starting transfers between devices, shifted(): lax.ppermute(block, 'seq', [(i, i + by) for i in range(size) if 0 <= i +...  4.33 us
  transfers between devices with their start and end apart: 5, of which 1 were waited for; matrix products, arithmetic and copies ran while one was open for 2% of the time, Pallas kernels for 5%

profile of v4, /device:TPU:0, one launch (start us, length us, event | category | flops | bytes accessed | tf_op | source)
XLA Modules:
  0.0 205.7 jit_solution(2378508397014077749)
XLA Ops:
  0.6 1.0 slice_bitcast_fusion
  1.6 1.3 collective-permute-start.1
  2.9 3.0 %collective-permute-start = (bf16[64,768]{1,0:T(8,128)(2,1)S(1)}, bf16[64,768]{1,0:T(8,128)(2,1)S(1)}, u32[]{:S(2)}, u32[]{:S(2)}) collective-permute-start(bf16[64,768]{1,0:T(8,128)(2,1)S(1)} %get-tuple-element.115), channel_id=1, source_target_pairs={{0,8},{8,16},{16,24},{1,9},{9,17},{17,25},{2,10},{10,18},{18,26},{... | collective-permute-start | bytes 294920 | tf_op jit(solution)/shard_map/ppermute | solution.py:827
  6.2 0.8 reduce-window.9
  7.0 1.3 pad.4.taps.refs_13_
  8.4 0.6 concatenate.6.info
  9.0 0.0 collective-permute-done.1.right
  9.0 0.0 copy-start.8
  9.0 0.6 copy-done.7
  9.6 0.0 copy-done.8
  9.6 7.0 %project.1 = (bf16[512,768]{1,0:T(8,128)(2,1)}, bf16[640,768]{1,0:T(8,128)(2,1)}, bf16[640,768]{1,0:T(8,128)(2,1)}, bf16[2,128,768]{2,1,0:T(8,128)(2,1)}, bf16[7...) custom-call(s32[16]{0:T(128)} %concatenate.6.info, bf16[512,768]{1,0:T(8,128)(2,1)} %bitcast.26, bf16[64,768]{1,0:T(8,128)(2,1)} %copy-done.8, ...), custom_call_target="tpu_custom_call" | custom-call | flops 2113929216 | bytes 8609792 | tf_op jit(solution)/shard_map/project/pallas_call | solution.py:832
  16.6 3.4 %collective-permute-start.2 = (bf16[2,128,768]{2,1,0:T(8,128)(2,1)}, bf16[2,128,768]{2,1,0:T(8,128)(2,1)S(1)}, u32[]{:S(2)}, u32[]{:S(2)}) collective-permute-start(bf16[2,128,768]{2,1,0:T(8,128)(2,1)} %get-tuple-element.62.rest_0_.refs_8_), channel_id=1, source_target_pairs={{0,16},{8,24},{16,0},{24,8},{1,17},{9,25},{17,1},{25,9},{2,18},{10... | collective-permute-start | bytes 1179656 | tf_op jit(solution)/shard_map/ppermute | solution.py:943
  20.1 10.0 %collective-permute-done.2.rest_1_.refs_9_ = bf16[2,128,768]{2,1,0:T(8,128)(2,1)S(1)} collective-permute-done((bf16[2,128,768]{2,1,0:T(8,128)(2,1)}, bf16[2,128,768]{2,1,0:T(8,128)(2,1)S(1)}, u32[]{:S(2)}, u32[]{:S(2)}) %collective-permute-start.2) | collective-permute-done | bytes 393248 | tf_op jit(solution)/shard_map/ppermute | solution.py:943
  30.1 0.1 collective-permute-start.4
  30.3 0.6 concatenate.7.vecs
  30.9 10.4 %near_forward.1 = (bf16[12,4,256,128]{3,2,1,0:T(8,128)(2,1)}, f32[768,512]{1,0:T(8,128)}, f32[6,8,512]{2,1,0:T(8,128)}) custom-call(s32[16]{0:T(128)} %concatenate.6.info, bf16[512,768]{1,0:T(8,128)(2,1)} %get-tuple-element.57.q.refs_0_, bf16[640,768]{1,0:T(8,128)(2,1)} %get-tuple-element.58.k.refs_6_, bf16[640,768]{1,0:T(8,128)(2,1)} %get-tuple-element.59.v.refs_7_), custom_call_target="tpu_custom_call" | custom-call | flops 1610612736 | bytes 7569408 | tf_op jit(solution)/shard_map/near_forward/pallas_call | solution.py:832
  41.4 0.0 collective-permute-done.4.rest_3_.refs_11_
  41.4 0.7 copy-done.5
  42.1 0.2 copy-done.6
  42.3 15.4 %pool_forward.1 = (bf16[12,512,512]{2,1,0:T(8,128)(2,1)}, f32[512,768]{1,0:T(8,128)}, f32[512,768]{1,0:T(8,128)}, f32[512,768]{1,0:T(8,128)}) custom-call(s32[16]{0:T(128)} %concatenate.6.info, bf16[512,768]{1,0:T(8,128)(2,1)} %get-tuple-element.57.q.refs_0_, f32[768,512]{1,0:T(8,128)} %get-tuple-element.60.o_near, f32[6,8,512]{2,1,0:T(8,128)} %get-tuple-element.61.st, ...), custom_call_target="tpu_custom_call" | custom-call | flops 3221225472 | bytes 15040512 | tf_op jit(solution)/shard_map/pool_forward/pallas_call | solution.py:832
  57.6 38.1 %dense.1 = (bf16[512,768]{1,0:T(8,128)(2,1)}, f32[512,768]{1,0:T(8,128)}, bf16[512,768]{1,0:T(8,128)(2,1)}, bf16[512,768]{1,0:T(8,128)(2,1)}, bf16[4,2,4,2,48,38...) custom-call(s32[16]{0:T(128)} %concatenate.6.info, ...), custom_call_target="tpu_custom_call" | custom-call | flops 16307453952 | bytes 31506432 | tf_op jit(solution)/shard_map/dense/pallas_call | solution.py:832
  95.8 105.2 %backward.1 = (f32[4,48,384]{2,1,0:T(8,128)}, f32[4,48,384]{2,1,0:T(8,128)}, f32[48,384]{1,0:T(8,128)}, f32[48,384]{1,0:T(8,128)}, f32[48,384]{1,0:T(8,128)}, /*...) custom-call(bf16[512,768]{1,0:T(8,128)(2,1)} %get-tuple-element.57.q.refs_0_, ...), custom_call_target="tpu_custom_call" | custom-call | flops 13287555072 | bytes 33603584 | tf_op jit(solution)/shard_map/backward/pallas_call | solution.py:1181
  200.9 3.3 %unpack.1 = (bf16[512,768]{1,0:T(8,128)(2,1)}, f32[24,768]{1,0:T(8,128)}, f32[24,768]{1,0:T(8,128)}, f32[24,768]{1,0:T(8,128)}, f32[24,768]{1,0:T(8,128)}, /*ind...) custom-call(s32[16]{0:T(128)} %concatenate.6.info, ...), custom_call_target="tpu_custom_call" | custom-call | bytes 3359584 | tf_op jit(solution)/shard_map/unpack/pallas_call | solution.py:832
  204.3 1.4 copy.27
  (21 shorter events, 0.1 us)
Async XLA Ops:
  1.6 7.4 %collective-permute-start.1 = (bf16[64,768]{1,0:T(8,128)(2,1)S(1)}, bf16[64,768]{1,0:T(8,128)(2,1)S(1)}, u32[]{:S(2)}, u32[]{:S(2)}) collective-permute-start(bf16[64,768]{1,0:T(8,128)(2,1)S(1)} %get-tuple-element.114), channel_id=1, source_target_pairs={{8,0},{16,8},{24,16},{9,1},{17,9},{25,17},{10,2},{18,10},{26,18},{... | collective-permute-start | bytes 294920 | tf_op jit(solution)/shard_map/ppermute | solution.py:827
  2.9 6.1 %collective-permute-start = (bf16[64,768]{1,0:T(8,128)(2,1)S(1)}, bf16[64,768]{1,0:T(8,128)(2,1)S(1)}, u32[]{:S(2)}, u32[]{:S(2)}) collective-permute-start(bf16[64,768]{1,0:T(8,128)(2,1)S(1)} %get-tuple-element.115), channel_id=1, source_target_pairs={{0,8},{8,16},{16,24},{1,9},{9,17},{17,25},{2,10},{10,18},{18,26},{... | collective-permute-start | bytes 294920 | tf_op jit(solution)/shard_map/ppermute | solution.py:827
  9.0 0.6 copy-start.7
  9.0 0.7 copy-start.8
  9.6 20.6 %copy-start = (f32[768]{0:T(1024)S(1)}, f32[768]{0:T(1024)}, u32[]{:S(2)}) copy-start(f32[768]{0:T(1024)} %param.22) | copy-start | bytes 9220
  9.6 20.6 %copy-start.1 = (f32[768]{0:T(1024)S(1)}, f32[768]{0:T(1024)}, u32[]{:S(2)}) copy-start(f32[768]{0:T(1024)} %param.23) | copy-start | bytes 9220
  9.6 20.6 %copy-start.2 = (f32[768]{0:T(1024)S(1)}, f32[768]{0:T(1024)}, u32[]{:S(2)}) copy-start(f32[768]{0:T(1024)} %param.24) | copy-start | bytes 9220
  9.6 20.6 %copy-start.3 = (f32[768]{0:T(1024)S(1)}, f32[768]{0:T(1024)}, u32[]{:S(2)}) copy-start(f32[768]{0:T(1024)} %param.25) | copy-start | bytes 9220
  16.6 13.4 %collective-permute-start.2 = (bf16[2,128,768]{2,1,0:T(8,128)(2,1)}, bf16[2,128,768]{2,1,0:T(8,128)(2,1)S(1)}, u32[]{:S(2)}, u32[]{:S(2)}) collective-permute-start(bf16[2,128,768]{2,1,0:T(8,128)(2,1)} %get-tuple-element.62.rest_0_.refs_8_), channel_id=1, source_target_pairs={{0,16},{8,24},{16,0},{24,8},{1,17},{9,25},{17,1},{25,9},{2,18},{10... | collective-permute-start | bytes 1179656 | tf_op jit(solution)/shard_map/ppermute | solution.py:943
  20.1 21.3 %collective-permute-start.3 = (bf16[2,128,768]{2,1,0:T(8,128)(2,1)}, bf16[2,128,768]{2,1,0:T(8,128)(2,1)S(1)}, u32[]{:S(2)}, u32[]{:S(2)}) collective-permute-start(bf16[2,128,768]{2,1,0:T(8,128)(2,1)} %get-tuple-element.62.rest_0_.refs_8_), channel_id=1, source_target_pairs={{0,8},{8,0},{16,24},{24,16},{1,9},{9,1},{17,25},{25,17},{2,10},{10... | collective-permute-start | bytes 1179656 | tf_op jit(solution)/shard_map/ppermute | solution.py:944
  30.1 11.3 %copy-start.4 = (bf16[2,128,768]{2,1,0:T(8,128)(2,1)}, bf16[2,128,768]{2,1,0:T(8,128)(2,1)S(1)}, u32[]{:S(2)}) copy-start(bf16[2,128,768]{2,1,0:T(8,128)(2,1)S(1)} %collective-permute-done.2.rest_1_.refs_9_) | copy-start | bytes 1179652
  30.1 11.3 %collective-permute-start.4 = (bf16[2,128,768]{2,1,0:T(8,128)(2,1)S(1)}, bf16[2,128,768]{2,1,0:T(8,128)(2,1)S(1)}, u32[]{:S(2)}, u32[]{:S(2)}) collective-permute-start(bf16[2,128,768]{2,1,0:T(8,128)(2,1)S(1)} %collective-permute-done.2.rest_1_.refs_9_), channel_id=1, source_target_pairs={{0,8},{8,0},{16,24},{24,16},{1,9},{9,1},{17,25},{25,17},{2,10},{10... | collective-permute-start | bytes 1179656 | tf_op jit(solution)/shard_map/ppermute | solution.py:944
  41.3 0.7 copy-start.5
  41.4 0.9 copy-start.6

commit v5 on v4

v5 whole, which is shorter than its diff:
```python
import itertools
from functools import partial

import jax
import jax.numpy as jnp
from jax import lax
from jax.experimental import pallas as pl
from jax.experimental.pallas import tpu as pltpu
from jax.sharding import PartitionSpec as P

D = 768
FF = 3072
H = 12
PAIRS = H // 2
HALF = 64
PWIN = 512
QB = 128
EXTRA = 16
LANES = 128
BF16 = jnp.bfloat16
F32 = jnp.float32
MB = 1 << 20


def nn(left, right):
    return jnp.dot(left, right, preferred_element_type=F32)


def nt(left, right, precision=None):
    return lax.dot_general(
        left, right, (((1,), (1,)), ((), ())), preferred_element_type=F32, precision=precision
    )


def iota(shape, dim):
    return lax.broadcasted_iota(jnp.int32, shape, dim)


def segment_of(info, place, row_len):
    item = jnp.zeros_like(place)
    for m in range(4):
        item = item + (place >= info[m]).astype(jnp.int32)
    return jnp.where((place >= 0) & (place < row_len), item, -2)


def head_half(block, head):
    lane = iota(block.shape, 1)
    return jnp.where((lane < 64) == (head == 0), block, jnp.zeros_like(block))


def tap_mask(info, tap, shift, count, row_len):
    center = info[4] + 4 * (iota((count, 1), 0) + shift)
    same = segment_of(info, center + tap - 2, row_len) == segment_of(info, center, row_len)
    return (same & (center < row_len)).astype(F32)


def folds(rows, width):
    return 2 if rows % 16 and rows % 8 == 0 and (width // 2) % LANES == 0 else 1


def folded(rows, width):
    fold = folds(rows, width)
    return (rows * fold, width // fold)


def fold_rows(block):
    rows, width = block.shape
    fold = folds(rows, width)
    part = width // fold
    return jnp.concatenate([block[:, i * part : (i + 1) * part] for i in range(fold)], axis=0)


def unfold_rows(block, rows):
    fold = block.shape[0] // rows
    return jnp.concatenate([block[i * rows : (i + 1) * rows] for i in range(fold)], axis=1)


def store_chunks(target, total):
    nz, nx = target.shape[0], target.shape[1]
    rows = total.shape[0] // (nz * nx)
    for z in range(nz):
        for x in range(nx):
            start = (z * nx + x) * rows
            target[z, x] = fold_rows(total[start : start + rows]).astype(BF16)


def store_blocks(targets, block, total):
    _, nz, nx, part, wide = targets[0].shape
    rows = total.shape[0] // (nz * nx)
    across = total.shape[1] // wide
    for z in range(nz):
        for x in range(nx):
            start = (z * nx + x) * rows
            for unit, target in enumerate(targets):
                top = start + (unit // across) * part
                left = (unit % across) * wide
                target[block, z, x] = total[top : top + part, left : left + wide].astype(BF16)


def project_kernel(info, tok, left, right, wq, wk, wv, taps, q_out, k_out, v_out, pool_out, tt_out, mask_out, x, cells, *, row_len):
    count = tok.shape[0]
    x[0:HALF] = left[...]
    x[HALF : HALF + count] = tok[...]
    x[HALF + count :] = right[...]
    k_low = nn(x[...], wk[...]).astype(BF16)
    k_out[...] = k_low
    v_low = nn(x[...], wv[...]).astype(BF16)
    v_out[...] = v_low
    masks = [tap_mask(info, tap, 0, count // 4, row_len) for tap in range(5)]
    for which, low in ((0, k_low), (1, v_low)):
        wide = low.astype(F32)
        for c in range(D // LANES):
            lanes = slice(c * LANES, (c + 1) * LANES)
            cells[c] = wide[:, lanes]
            total = jnp.zeros((count // 4, LANES), F32)
            for tap in range(5):
                taken = cells.at[c][pl.ds(HALF + tap - 2, count // 4, stride=4), :]
                total = total + taken * masks[tap] * taps[tap : tap + 1, lanes]
            pool_out[which, :, lanes] = total.astype(BF16)
    q_out[...] = (nn(tok[...], wq[...]).astype(BF16).astype(F32) * 0.125).astype(BF16)
    tt_out[...] = tok[...].T
    lane = iota((count // 4, LANES), 1)
    for shift in range(2):
        total = jnp.zeros((count // 4, LANES), F32)
        for tap in range(5):
            mask = tap_mask(info, tap, shift, count // 4, row_len)
            total = jnp.where(lane == tap, mask, total)
        mask_out[shift] = total


def near_forward_kernel(info, q, k, v, e_out, o_out, st_out, bias, *, row_len):
    count, span = q.shape[0], k.shape[0]
    blocks = count // QB

    @pl.when(pl.program_id(0) == 0)
    def _():
        for b in range(blocks):
            query_place = info[4] + b * QB + iota((1, QB), 1)
            key_place = info[4] - HALF + b * QB + iota((2 * QB, 1), 0)
            same = segment_of(info, key_place, row_len) == segment_of(info, query_place, row_len)
            near = jnp.abs(key_place - query_place) <= HALF
            bias[b] = jnp.where(same & near, 0.0, -1e30)

    vt = v[...].T
    ones = jnp.ones((16, span), BF16)
    st_out[...] = jnp.zeros_like(st_out)
    for head in range(2):
        qh = head_half(q[...], head)
        va = jnp.concatenate([vt[head * 64 : head * 64 + 64], ones], axis=0)
        for b in range(blocks):
            cols = slice(b * QB, (b + 1) * QB)
            keys = slice(b * QB, (b + 2) * QB)
            s = nt(k[keys, :], qh[cols]) + bias[b]
            top = jnp.max(s, axis=0, keepdims=True)
            e = jnp.exp(s - top).astype(BF16)
            e_out[head, b] = e
            oa = nn(va[:, keys], e)
            o_out[head * 64 : head * 64 + 64, cols] = oa[:64]
            st_out[0, head : head + 1, cols] = top
            st_out[0, 2 + head : 3 + head, cols] = oa[64:65]


def pool_forward_kernel(info, q, o_near, st, *rest, row_len, pieces):
    kv = rest[:pieces]
    e_out, o_out, rn_out, rp_out, bias = rest[pieces:]
    count = q.shape[0]
    size = kv[0].shape[1]

    @pl.when(pl.program_id(0) == 0)
    def _():
        query_place = info[4] + iota((1, count), 1)
        query_item = segment_of(info, query_place, row_len)
        for i in range(pieces):
            key_place = 4 * (info[8 + i] * size + iota((size, 1), 0))
            same = segment_of(info, key_place, row_len) == query_item
            near = jnp.abs(key_place - query_place) <= 2 * PWIN
            bias[i * size : (i + 1) * size] = jnp.where(same & near, 0.0, -1e30)

    kp = jnp.concatenate([piece[0] for piece in kv], axis=0)
    vt = jnp.concatenate([piece[1] for piece in kv], axis=0).T
    ones = jnp.ones((16, pieces * size), BF16)
    wide = min(256, count)
    for b in range(count // wide):
        cols = slice(b * wide, (b + 1) * wide)
        outs, near_scale, pool_scale = [], [], []
        for head in range(2):
            qh = head_half(q[cols, :], head)
            va = jnp.concatenate([vt[head * 64 : head * 64 + 64], ones], axis=0)
            s = nt(kp, qh) + bias[:, cols]
            near_top = st[0, head : head + 1, cols]
            top = jnp.maximum(jnp.max(s, axis=0, keepdims=True), near_top)
            e = jnp.exp(s - top).astype(BF16)
            e_out[head, :, cols] = e
            oa = nn(va, e)
            fade = jnp.exp(near_top - top)
            inverse = 1.0 / (fade * st[0, 2 + head : 3 + head, cols] + oa[64:65])
            outs.append((fade * o_near[head * 64 : head * 64 + 64, cols] + oa[:64]) * inverse)
            near_scale.append(jnp.broadcast_to(fade * inverse, (64, wide)))
            pool_scale.append(jnp.broadcast_to(inverse, (64, wide)))
        o_out[cols, :] = jnp.concatenate(outs, axis=0).T
        rn_out[cols, :] = jnp.concatenate(near_scale, axis=0).T
        rp_out[cols, :] = jnp.concatenate(pool_scale, axis=0).T


def normal_parts(v):
    bell = jnp.exp(v * v * -0.5)
    t = 1.0 / (1.0 + jnp.abs(v) * (0.3275911 * 0.7071067811865476))
    poly = t * (
        0.127414796 + t * (-0.142248368 + t * (0.7107068705 + t * (-0.7265760135 + t * 0.5307027145)))
    )
    tail = poly * bell
    return jnp.where(v < 0, tail, 1.0 - tail), v * bell * 0.3989422804014327


def normalized(values):
    shifted = values - jnp.mean(values, axis=1, keepdims=True)
    inverse = lax.rsqrt(jnp.mean(shifted * shifted, axis=1, keepdims=True) + 1e-05)
    return shifted * inverse, inverse


def dense_kernel(
    info, o, tok, og, vecs, w_out, w_in, w_back,
    mixed, act, slope, low_t, feed_grad, z_grad, unit_out, inv_out, att_t, sums,
    first, low, feed,
):
    step = pl.program_id(0)
    gain_one, bias_one = vecs[0:1, :], vecs[1:2, :]
    gain_two, bias_two = vecs[2:3, :], vecs[3:4, :]

    @pl.when(step == 0)
    def _():
        att = o[...].astype(BF16)
        att_t[...] = att.T
        unit, inverse = normalized(tok[...].astype(F32) + nn(att, w_out[...]))
        for c in range(PAIRS):
            unit_out[c] = unit[:, c * LANES : (c + 1) * LANES]
        inv_out[...] = jnp.broadcast_to(inverse, inv_out.shape)
        first[...] = unit * gain_one + bias_one
        low[...] = first[...].astype(BF16)
        low_t[...] = low[...].T
        feed[...] = jnp.zeros_like(feed)

    inner = nn(low[...], w_in[...])
    phi, bell = normal_parts(inner)
    act[...] = (inner * phi).astype(BF16)
    slope[...] = (phi + bell).astype(BF16)
    feed[...] += nn(act[...], w_back[...])

    @pl.when(step == CHUNKS - 1)
    def _():
        unit, inverse = normalized(first[...] + feed[...])
        mixed[...] = (unit * gain_two + bias_two).astype(BF16)
        upstream = og[...].astype(F32)
        sums[...] = jnp.zeros_like(sums)
        sums[2:3] = jnp.sum(upstream * unit, axis=0, keepdims=True)
        sums[3:4] = jnp.sum(upstream, axis=0, keepdims=True)
        e = upstream * gain_two
        centred = e - jnp.mean(e, axis=1, keepdims=True)
        total = inverse * (centred - unit * jnp.mean(e * unit, axis=1, keepdims=True))
        z_grad[...] = total
        feed_grad[...] = total.astype(BF16)


def score_delta(grad, attended):
    pick = ((iota((8, LANES), 1) // 64) == iota((8, LANES), 0)).astype(F32)
    return nt(pick, grad.astype(F32) * attended, precision=lax.Precision.HIGHEST)


def hop_pairs(axis, count, stride, hop):
    pairs = []
    for device in range(lax.axis_size(axis)):
        place = (device // stride) % count
        pairs.append((device, device + ((place + hop) % count - place) * stride))
    return pairs


MESH_ID = pl.DeviceIdType.MESH


class Summed:
    def __init__(self, order, send_of, keep, core_in, first, second, third, out_sem, in_sem):
        self.order, self.send_of = order, send_of
        self.keep, self.core_in = keep, core_in
        self.bufs = (first, second, third)
        self.out_sem, self.in_sem = out_sem, in_sem
        self.units = keep.shape[0]
        self.count = dict(zip("yzx", keep.shape[1:4]))
        self.here, self.row = lax.axis_index("seq"), lax.axis_index("dp")
        self.mine = self.here % 2
        nx = self.count["x"]
        self.own = {"y": self.here // 2, "z": self.row // nx, "x": self.row % nx}
        self.base = {"y": 1}
        self.base["x"] = self.base["y"] + self.count["y"] - 1
        self.base["z"] = self.base["x"] + nx - 1

    def copy(self, u, src, dst, slot, device):
        return pltpu.make_async_remote_copy(
            src_ref=src,
            dst_ref=dst,
            send_sem=self.out_sem.at[u, slot],
            recv_sem=self.in_sem.at[u, slot],
            device_id=device,
            device_id_type=MESH_ID,
        )

    def core_copy(self, u):
        partner = (self.own["y"] * 2 + 1 - self.mine, self.row)
        return self.copy(u, self.send_of(u), self.core_in.at[u], 0, partner)

    def hop_copy(self, u, stage, hop):
        axis = self.order[stage]
        other = (self.own[axis] + hop) % self.count[axis]
        place = dict(self.own)
        place[axis] = other
        device = (place["y"] * 2 + self.mine, place["z"] * self.count["x"] + place["x"])
        index = []
        for dim in "yzx":
            known = dim in self.order[: stage + 1]
            index.append(place[dim] if known else slice(None))
        source = self.keep.at[(u,) + tuple(index)]
        slot = self.base[axis] + hop - 1
        return self.copy(u, source, self.bufs[stage].at[u, hop - 1], slot, device)

    def hops(self, stage):
        return range(1, self.count[self.order[stage]])

    def start(self, u):
        self.core_copy(u).start()

    def core(self, u):
        self.core_copy(u).wait_recv()
        for y in range(self.count["y"]):
            for z in range(self.count["z"]):
                self.keep[u, y, z] = self.keep[u, y, z] + self.core_in[u, y, z]
        for hop in self.hops(0):
            self.hop_copy(u, 0, hop).start()

    def add(self, u, stage):
        left = [dim for dim in "yzx" if dim not in self.order[: stage + 1]]
        for hop in self.hops(stage):
            self.hop_copy(u, stage, hop).wait_recv()
            for place in itertools.product(*[range(self.count[dim]) for dim in left]):
                at = dict(self.own)
                at.update(zip(left, place))
                index = (u,) + tuple(at[dim] for dim in "yzx")
                self.keep[index] = self.keep[index] + self.bufs[stage][(u, hop - 1) + place]
        for hop in self.hops(stage + 1):
            self.hop_copy(u, stage + 1, hop).start()

    def one(self, u):
        self.add(u, 0)

    def two(self, u):
        self.add(u, 1)

    def three(self, u):
        total = self.keep[(u,) + tuple(self.own[dim] for dim in "yzx")].astype(F32)
        for hop in self.hops(2):
            self.hop_copy(u, 2, hop).wait_recv()
            total = total + self.bufs[2][u, hop - 1].astype(F32)
        return total

    def sent_core(self, u):
        self.core_copy(u).wait_send()

    def sent(self, u):
        for stage in range(3):
            for hop in self.hops(stage):
                self.hop_copy(u, stage, hop).wait_send()


def summed_scratch(units, shape, order):
    count = dict(zip("yzx", shape[:3]))
    chunk = shape[3:]
    bufs = [pltpu.VMEM((units,) + shape, BF16), pltpu.VMEM((units,) + shape, BF16)]
    for stage in range(3):
        left = tuple(count[dim] for dim in "yzx" if dim not in order[: stage + 1])
        bufs.append(pltpu.VMEM((units, max(count[order[stage]] - 1, 1)) + left + chunk, BF16))
    slots = count["y"] + count["x"] + count["z"] - 2
    bufs += [pltpu.SemaphoreType.DMA((units, slots)), pltpu.SemaphoreType.DMA((units, slots))]
    return bufs


def greet(peers):
    barrier = pltpu.get_barrier_semaphore()
    for peer in peers:
        pl.semaphore_signal(barrier, inc=1, device_id=peer, device_id_type=MESH_ID)
    pl.semaphore_wait(barrier, len(peers))


CHUNKS = FF // D
BUFFERS = ("sum", "core", "first", "second", "third", "out", "inn")
POOL = CHUNKS + 1
NEAR = POOL + PAIRS
LATE = NEAR + PAIRS
LAST = LATE + PAIRS
ORDERS = {
    "in0": "zxy",
    "in1": "xzy",
    "in2": "yzx",
    "in3": "yzx",
    "b0": "xzy",
    "b1": "xzy",
    "b2": "zxy",
    "b3": "xyz",
    "out": "yzx",
    "q": "xyz",
    "k": "xyz",
    "v": "yxz",
    "small": "yzx",
}
PLAN = {
    1: (
        ("in0", 0),
    ),
    3: (
        ("in1", 0),
    ),
    4: (
        ("b0", 0),
        ("in3", 0),
        ("b2", 0),
    ),
    8: (
        ("out", 0),
    ),
    9: (
        ("b1", 0),
    ),
    10: (
        ("in1", 1),
    ),
    11: (
        ("b0", 1),
    ),
    13: (
        ("b3", 0),
    ),
    14: (
        ("b1", 1),
    ),
    15: (
        ("in2", 0),
    ),
    17: (
        ("query", 0),
        ("in3", 1),
    ),
    19: (
        ("q", 0),
    ),
    20: (
        ("in2", 1),
        ("b3", 1),
    ),
    23: (
        ("in0", 1),
        ("b1", 2),
        ("q", 1),
        ("in3", 2),
        ("out", 1),
        ("k", 0),
        ("small", 0),
        ("v", 0),
        ("tokens", 0),
        ("b3", 2),
        ("small", 1),
        ("q", 2),
        ("k", 1),
        ("b2", 1),
        ("v", 1),
        ("small", 2),
        ("b0", 2),
        ("b2", 2),
        ("k", 2),
        ("q", 3),
        ("in0", 2),
        ("in3", 3),
        ("b1", 3),
        ("in2", 2),
        ("small", 3),
        ("out", 2),
        ("in1", 2),
        ("v", 2),
        ("out", 3),
        ("b3", 3),
        ("in0", 3),
        ("in1", 3),
        ("in2", 3),
        ("b0", 3),
        ("b2", 3),
        ("k", 3),
        ("v", 3),
    ),
}

class Refs:
    pass


def backward_kernel(*refs, names, pieces):
    r = Refs()
    for name, ref in zip(names, refs):
        setattr(r, name, ref)
    kv = [getattr(r, "piece%d" % i) for i in range(pieces)]
    seq, ny = pieces, pieces // 2
    step = pl.program_id(0)
    count = r.q.shape[0]
    size = count // 4
    nz, nx = r.b_send.shape[2:4]
    here, row = lax.axis_index("seq"), lax.axis_index("dp")
    y, core = here // 2, here % 2
    partner = (y * 2 + 1 - core, row)
    right, left = ((here + 1) % seq, row), ((here + seq - 1) % seq, row)
    units_back = r.b_send.shape[0]
    senders = {"small": r.s_send}
    for f in range(CHUNKS):
        senders["in%d" % f] = r.a_send.at[f]
    for place, name in enumerate(("out", "q", "k", "v")):
        senders[name] = r.a_send.at[place]
    for u in range(units_back):
        senders["b%d" % u] = r.b_send.at[u]
    sums = {}
    for name in senders:
        bufs = [getattr(r, name + "_" + part) for part in BUFFERS]
        sums[name] = Summed(ORDERS[name], lambda u, name=name: senders[name], *bufs)

    def copy(src, dst, out_sem, in_sem, device):
        return pltpu.make_async_remote_copy(
            src_ref=src, dst_ref=dst, send_sem=out_sem, recv_sem=in_sem,
            device_id=device, device_id_type=MESH_ID,
        )

    def pool_core(p):
        return copy(r.p_send.at[p], r.p_in.at[p], r.p_sem.at[0, p, 0], r.p_sem.at[1, p, 0], partner)

    def pool_y(p, hop):
        device = (((y + hop) % ny) * 2 + core, row)
        return copy(
            r.p_keep.at[p, hop], r.p_y.at[p, hop - 1], r.p_sem.at[0, p, hop], r.p_sem.at[1, p, hop], device
        )

    def halo(p, side):
        device = right if side else left
        return copy(
            r.h_out.at[p, side], r.h_in.at[p, side], r.h_sem.at[0, p, side], r.h_sem.at[1, p, side], device
        )

    def chunk_loads(f):
        slot = f % 2
        part = pl.ds(pl.multiple_of(f * D, D), D)
        return [
            pltpu.make_async_copy(r.win_any.at[:, part], r.wbuf.at[slot], r.l_sem.at[0, slot]),
            pltpu.make_async_copy(r.wback_any.at[part, :], r.wbuf.at[2 + slot], r.l_sem.at[1, slot]),
            pltpu.make_async_copy(r.act_any.at[:, part], r.tbuf.at[slot], r.l_sem.at[2, slot]),
            pltpu.make_async_copy(r.slope_any.at[:, part], r.tbuf.at[2 + slot], r.l_sem.at[3, slot]),
        ]

    load_feed = [
        pltpu.make_async_copy(r.fg_any, r.fg, r.l_sem.at[4, 0]),
        pltpu.make_async_copy(r.lowt_any, r.lt, r.l_sem.at[4, 1]),
        pltpu.make_async_copy(r.zg_any, r.sg, r.l_sem.at[5, 0]),
    ]
    load_unit = pltpu.make_async_copy(r.unit_any, r.acc.at[0], r.l_sem.at[5, 1])
    load_wout = pltpu.make_async_copy(r.wout_any, r.wbuf.at[0], r.l_sem.at[6, 0])
    load_att = pltpu.make_async_copy(r.att_any, r.att, r.l_sem.at[6, 1])
    load_wq = pltpu.make_async_copy(r.wq_any, r.wbuf.at[1], r.l_sem.at[7, 0])
    load_wk = pltpu.make_async_copy(r.wk_any, r.wbuf.at[2], r.l_sem.at[7, 1])
    load_wv = pltpu.make_async_copy(r.wv_any, r.wbuf.at[3], r.l_sem.at[8, 0])
    load_tt = pltpu.make_async_copy(r.tt_any, r.lt, r.l_sem.at[8, 1])

    def rows_of(block, mine):
        rc = D // seq
        return pl.ds(pl.multiple_of((2 * block + mine) * rc, rc), rc)

    @pl.when(step == 0)
    def _():
        for load in chunk_loads(0) + load_feed + [load_unit, load_att]:
            load.start()
        z, x = row // nx, row % nx
        peers = [partner, right, left]
        peers += [(((y + hop) % ny) * 2 + core, row) for hop in range(1, ny)]
        peers += [(here, z * nx + (x + hop) % nx) for hop in range(1, nx)]
        peers += [(here, ((z + hop) % nz) * nx + x) for hop in range(1, nz)]
        greet(peers)
        for load in load_feed:
            load.wait()

    @pl.when(step < CHUNKS)
    def _():
        f = step
        slot = f % 2
        for load in chunk_loads(f):
            load.wait()

        @pl.when(f < CHUNKS - 1)
        def _():
            for load in chunk_loads(f + 1):
                load.start()

        @pl.when(f == CHUNKS - 1)
        def _():
            load_wout.start()

        slope = r.tbuf[2 + slot].astype(F32)
        inner_grad = (nt(r.fg[...], r.wbuf[2 + slot]) * slope).astype(BF16)
        for block in range(ny):
            store_chunks(r.a_send.at[f, block], nn(r.lt[rows_of(block, 1 - core), :], inner_grad))

        kept = [nn(r.lt[rows_of(block, core), :], inner_grad) for block in range(ny)]
        for i in range(CHUNKS):

            @pl.when(f == i)
            def _(i=i):
                sums["in%d" % i].start(0)
                for block in range(ny):
                    store_chunks(sums["in%d" % i].keep.at[0, block], kept[block])

        r.sg[...] += nt(inner_grad, r.wbuf[slot])
        back = nn(r.tbuf[slot].T, r.fg[...])
        part = FF // seq
        for sub in range(D // part):
            block = f * (D // part) + sub
            piece = back[sub * part : (sub + 1) * part]

            @pl.when(block % 2 == core)
            def _(block=block, piece=piece):
                keeps = [sums["b%d" % u].keep.at[0] for u in range(units_back)]
                store_blocks(keeps, block // 2, piece)

            @pl.when(block % 2 != core)
            def _(block=block, piece=piece):
                store_blocks([r.b_send.at[u] for u in range(units_back)], block // 2, piece)

        @pl.when(f == CHUNKS - 1)
        def _():
            for u in range(units_back):
                sums["b%d" % u].start(0)

    @pl.when(step == CHUNKS)
    def _():
        load_wq.start()
        load_wk.start()
        load_wv.start()
        load_unit.wait()
        inverse = r.inv[:, 0:1]
        total = jnp.zeros((count, LANES), F32)
        total_unit = jnp.zeros((count, LANES), F32)
        r.small[...] = jnp.zeros_like(r.small)
        r.small[0:8] = r.sums[...]
        for c in range(PAIRS):
            lanes = slice(c * LANES, (c + 1) * LANES)
            grad, unit = r.sg[:, lanes], r.acc[0, c]
            r.small[0:1, lanes] = jnp.sum(grad * unit, axis=0, keepdims=True)
            r.small[1:2, lanes] = jnp.sum(grad, axis=0, keepdims=True)
            e = grad * r.vecs[0:1, lanes]
            total = total + e
            total_unit = total_unit + e * unit
        mean = jnp.sum(total, axis=1, keepdims=True) * (1.0 / D)
        mean_unit = jnp.sum(total_unit, axis=1, keepdims=True) * (1.0 / D)
        for c in range(PAIRS):
            lanes = slice(c * LANES, (c + 1) * LANES)
            e = r.sg[:, lanes] * r.vecs[0:1, lanes]
            r.sg[:, lanes] = inverse * (e - mean - r.acc[0, c] * mean_unit)
        branch_grad = r.sg[...].astype(BF16)
        load_att.wait()
        load_wout.wait()
        sums["in0"].sent_core(0)
        for block in range(ny):
            store_chunks(r.a_send.at[0, block], nn(r.att[rows_of(block, 1 - core), :], branch_grad))
        sums["out"].start(0)
        for block in range(ny):
            store_chunks(sums["out"].keep.at[0, block], nn(r.att[rows_of(block, core), :], branch_grad))
        load_tt.start()
        attended_grad = nt(branch_grad, r.wbuf[0])
        for c in range(PAIRS):
            r.acc[1, c] = attended_grad[:, c * LANES : (c + 1) * LANES]

    @pl.when((step >= POOL) & (step < NEAR))
    def _():
        p = step - POOL
        r.gb[...] = (r.acc[1, p] * r.rp[...]).astype(BF16)
        delta = score_delta(r.gb[...], r.o[...])
        kp = jnp.concatenate([piece[0] for piece in kv], axis=0)
        kt = kp.T
        vp = jnp.concatenate([piece[1] for piece in kv], axis=0)
        wide = min(256, count)
        for head in range(2):
            for b in range(count // wide):
                cols = slice(b * wide, (b + 1) * wide)
                gh = head_half(r.gb[cols, :], head)
                qh = head_half(r.q[cols, :], head)
                low = r.pool_e[head, :, cols]
                dp = nt(vp, gh) - delta[head : head + 1, cols]
                ds = (low.astype(F32) * dp).astype(BF16)
                key_part = nn(ds, qh)
                value_part = nn(low, gh)
                if head == 0 and b == 0:
                    r.dk[0 : seq * size] = key_part
                    r.dv[0 : seq * size] = value_part
                else:
                    r.dk[0 : seq * size] += key_part
                    r.dv[0 : seq * size] += value_part
                r.dq_pool[p, head * 64 : head * 64 + 64, cols] = nn(kt[head * 64 : head * 64 + 64], ds)
        for i in range(pieces):
            target = r.p_keep if i < ny else r.p_send
            after = (((y + i % ny) % ny) * 2 + (core + i // ny) % 2 + 1) % seq
            index = ((after % 2 - core + 2) % 2) * ny + (after // 2 - y + ny) % ny
            rows = pl.ds(pl.multiple_of(index * size, size), EXTRA)
            for which, total in ((0, r.dk), (1, r.dv)):
                target[p, i % ny, which, 0:size] = total[i * size : (i + 1) * size].astype(BF16)
                target[p, i % ny, which, size:] = total[rows, :].astype(BF16)
        pool_core(p).start()

    @pl.when((step > POOL) & (step <= NEAR))
    def _():
        p = step - POOL - 1
        pool_core(p).wait_recv()
        for hop in range(1, ny):
            for which in range(2):
                r.p_keep[p, hop, which] = r.p_keep[p, hop, which] + r.p_in[p, hop, which]
            pool_y(p, hop).start()

    @pl.when((step >= NEAR) & (step < LATE))
    def _():
        p = step - NEAR
        r.gb[...] = (r.acc[1, p] * r.rn[...]).astype(BF16)
        delta = score_delta(r.gb[...], r.o[...])
        kt = r.keys[...].T
        r.dk[0 : count + 2 * HALF] = jnp.zeros((count + 2 * HALF, LANES), F32)
        r.dv[0 : count + 2 * HALF] = jnp.zeros((count + 2 * HALF, LANES), F32)
        for b in range(count // QB):
            cols = slice(b * QB, (b + 1) * QB)
            keys = slice(b * QB, (b + 2) * QB)
            lows, scores, grads, queries, dqs = [], [], [], [], []
            for head in range(2):
                gh = head_half(r.gb[cols, :], head)
                low = r.near_e[head, b]
                dp = nt(r.values[keys, :], gh) - delta[head : head + 1, cols]
                ds = (low.astype(F32) * dp).astype(BF16)
                dqs.append(nn(kt[head * 64 : head * 64 + 64, keys], ds))
                lows.append(low)
                scores.append(ds)
                grads.append(gh)
                queries.append(head_half(r.q[cols, :], head))
            r.dk[keys, :] += nn(jnp.concatenate(scores, axis=1), jnp.concatenate(queries, axis=0))
            r.dv[keys, :] += nn(jnp.concatenate(lows, axis=1), jnp.concatenate(grads, axis=0))
            total = (jnp.concatenate(dqs, axis=0) + r.dq_pool[p, :, cols]) * 0.125
            lanes = pl.ds(pl.multiple_of(p * LANES, LANES), LANES)
            r.tbuf[0, cols, lanes] = total.T.astype(BF16)
        for which, total in ((0, r.dk), (1, r.dv)):
            r.h_out[p, 0, which] = total[0:HALF].astype(BF16)
            r.acc[which, p] = total[HALF : HALF + count]
            r.h_out[p, 1, which] = total[HALF + count : 2 * HALF + count].astype(BF16)

        @pl.when(here > 0)
        def _():
            halo(p, 0).start()

        @pl.when(here < seq - 1)
        def _():
            halo(p, 1).start()

    def query_gradient():
        load_tt.wait()
        sums["in1"].sent_core(0)
        for block in range(ny):
            store_chunks(r.a_send.at[1, block], nn(r.lt[rows_of(block, 1 - core), :], r.tbuf[0]))
        sums["q"].start(0)
        for block in range(ny):
            store_chunks(sums["q"].keep.at[0, block], nn(r.lt[rows_of(block, core), :], r.tbuf[0]))

    def tokens_gradient():
        for load in (load_wq, load_wk, load_wv):
            load.wait()
        total = r.sg[...] + nt(r.tbuf[0], r.wbuf[1])
        total = total + nt(r.tbuf[1], r.wbuf[2])
        r.tokens_grad[...] = (total + nt(r.tbuf[2], r.wbuf[3])).astype(BF16)

    @pl.when((step >= LATE) & (step < LAST))
    def _():
        p = step - LATE
        lanes = pl.ds(pl.multiple_of(p * LANES, LANES), LANES)
        for hop in range(1, ny):
            pool_y(p, hop).wait_recv()

        @pl.when(here < seq - 1)
        def _():
            halo(p, 0).wait_recv()
            for which in range(2):
                r.acc[which, p, count - HALF :, :] += r.h_in[p, 0, which].astype(F32)

        @pl.when(here > 0)
        def _():
            halo(p, 1).wait_recv()
            for which in range(2):
                r.acc[which, p, 0:HALF, :] += r.h_in[p, 1, which].astype(F32)

        moves = ((2, 0, 0), (3, 1, 0), (4, 2, 0), (0, 2, 1), (1, 3, 1))
        sums = [jnp.zeros((1, LANES), F32)] * 5
        for which, source in ((0, r.keys), (1, r.values)):
            grad = r.acc.at[which, p]
            r.cells[...] = source[...].astype(F32)
            total = r.p_keep[p, 0, which].astype(F32) + r.p_in[p, 0, which].astype(F32)
            for hop in range(1, ny):
                total = total + r.p_y[p, hop - 1, which].astype(F32)
            r.g[...] = total
            for tap, place, shift in moves:
                mask = r.masks[shift, :, tap : tap + 1]
                spread = r.g[shift : shift + size, :] * mask * r.taps[tap : tap + 1, :]
                grad[pl.ds(place, size, stride=4), :] += spread
            for tap in range(5):
                taken = r.cells[pl.ds(HALF + tap - 2, size, stride=4), :]
                product = r.g[0:size, :] * r.masks[0, :, tap : tap + 1] * taken
                sums[tap] = sums[tap] + jnp.sum(product, axis=0, keepdims=True)
            r.tbuf[1 + which, :, lanes] = grad[...].astype(BF16)
        for tap in range(5):
            r.small[8 + tap : 9 + tap, lanes] = sums[tap]

    @pl.when(step == LAST)
    def _():
        for name, place, low in (("k", 2, 1), ("v", 3, 2)):
            sums["in%d" % place].sent_core(0)
            for block in range(ny):
                rows = rows_of(block, 1 - core)
                store_chunks(r.a_send.at[place, block], nn(r.lt[rows, :], r.tbuf[low]))
            sums[name].start(0)
            keep = sums[name].keep
            for block in range(ny):
                store_chunks(keep.at[0, block], nn(r.lt[rows_of(block, core), :], r.tbuf[low]))
        r.small_t[...] = r.small[...].T
        few = D // (seq * nz * nx)
        for block in range(ny):
            for part, mine in ((r.s_send.at[block], 1 - core), (sums["small"].keep.at[0, block], core)):
                vectors = r.small_t[rows_of(block, mine), :]
                for z in range(nz):
                    for x in range(nx):
                        start = (z * nx + x) * few
                        part[z, x] = jnp.zeros(part.shape[2:], BF16)
                        part[z, x, 0:few] = vectors[start : start + few].astype(BF16)
        sums["small"].start(0)

    results = {"out": r.t_out, "q": r.t_query, "k": r.t_key, "v": r.t_value, "small": r.t_small}
    for f in range(CHUNKS):
        results["in%d" % f] = r.t_in.at[f]
    for u in range(units_back):
        results["b%d" % u] = r.t_back.at[u]

    def run(name, stage):
        if name == "query":
            query_gradient()
        elif name == "tokens":
            tokens_gradient()
        elif name in sums:
            done = getattr(sums[name], ("core", "one", "two", "three")[stage])(0)
            if stage == 3:
                results[name][...] = done

    for when, todo in PLAN.items():

        @pl.when(step == when)
        def _(todo=todo):
            for name, stage in todo:
                run(name, stage)

    @pl.when(step == LAST)
    def _():
        reused = ["in%d" % f for f in range(CHUNKS)]
        for name in sums:
            if name not in reused:
                sums[name].sent_core(0)
            sums[name].sent(0)
        for p in range(PAIRS):
            pool_core(p).wait_send()
            for hop in range(1, ny):
                pool_y(p, hop).wait_send()

        @pl.when(here > 0)
        def _():
            for p in range(PAIRS):
                halo(p, 0).wait_send()

        @pl.when(here < seq - 1)
        def _():
            for p in range(PAIRS):
                halo(p, 1).wait_send()


def unpack_kernel(t_in, t_back, t_query, t_key, t_value, t_out, t_small, tg, *outs):
    tokens_grad, query, key, value, out, inn, back = outs[:7]
    rows = query.shape[0]
    tokens_grad[...] = tg[...]
    for source, target in ((t_query, query), (t_key, key), (t_value, value), (t_out, out)):
        target[...] = unfold_rows(source[...], rows)
    for u in range(CHUNKS):
        inn[:, u * D : (u + 1) * D] = unfold_rows(t_in[u], rows)
    units, part, wide = t_back.shape
    across = back.shape[1] // wide
    for u in range(units):
        top, start = (u // across) * part, (u % across) * wide
        back[top : top + part, start : start + wide] = t_back[u]
    small = t_small[...]
    pad = LANES - small.shape[0]
    turned = jnp.concatenate([small, jnp.zeros((pad, LANES), F32)], axis=0).T
    for i in range(4):
        outs[7 + i][...] = turned[i : i + 1, 0:rows]
    outs[11][...] = small[0:rows, 8:13]


def shifted(block, by):
    size = lax.axis_size("seq")
    return lax.ppermute(block, "seq", [(i, i + by) for i in range(size) if 0 <= i + by < size])


def call(kernel, info, args, in_specs, outs, out_specs, grid, scratch, flops, name):
    moved = sum(a.size * a.dtype.itemsize for a in list(args) + list(outs))
    return pl.pallas_call(
        kernel,
        grid_spec=pltpu.PrefetchScalarGridSpec(
            num_scalar_prefetch=1,
            grid=grid,
            in_specs=in_specs,
            out_specs=out_specs,
            scratch_shapes=scratch,
        ),
        out_shape=outs,
        compiler_params=pltpu.CompilerParams(
            vmem_limit_bytes=60 * MB, dimension_semantics=("arbitrary",) * len(grid)
        ),
        cost_estimate=pl.CostEstimate(flops=flops, bytes_accessed=moved, transcendentals=0),
        name=name,
    )(info, *args)


def whole(array):
    rank = len(array.shape)
    return pl.BlockSpec(array.shape, lambda i, info: (0,) * rank)


def columns(array, width=LANES):
    rank = len(array.shape)
    return pl.BlockSpec(array.shape[:-1] + (width,), lambda i, info: (0,) * (rank - 1) + (i,))


def leading(array, size):
    rank = len(array.shape)
    return pl.BlockSpec((size,) + array.shape[1:], lambda i, info: (i,) + (0,) * (rank - 1))


def per_device(
    tokens,
    item_lengths,
    w_query,
    w_key,
    w_value,
    w_out,
    w_in,
    w_back,
    norm1_gain,
    norm1_bias,
    norm2_gain,
    norm2_bias,
    pool_weight,
    out_grad,
):
    _, count, _ = tokens.shape
    seq = lax.axis_size("seq")
    ny = seq // 2
    row_len = count * seq
    span = count + 2 * HALF
    size = count // 4
    here = lax.axis_index("seq")
    core, y = here % 2, here // 2
    owners = []
    for other in range(2):
        for hop in range(ny):
            owners.append(((y + hop) % ny) * 2 + jnp.bitwise_xor(core, other))
    afters = []
    for owner in owners:
        after = jnp.minimum(owner + 1, seq - 1)
        afters.append(jnp.bitwise_xor(after % 2, core) * ny + (after // 2 - y) % ny)
    zero = jnp.zeros((), jnp.int32)
    info = jnp.concatenate(
        [
            jnp.cumsum(item_lengths[0]).astype(jnp.int32),
            jnp.stack([here * count, core, y, zero] + owners + afters).astype(jnp.int32),
        ]
    )
    tok = tokens[0]
    og = out_grad[0]
    left = shifted(tok[count - HALF :], 1)
    right = shifted(tok[:HALF], -1)
    taps = jnp.pad(pool_weight.T, ((0, 3), (0, 0)))
    vecs = jnp.concatenate(
        [jnp.stack([norm1_gain, norm1_bias, norm2_gain, norm2_bias]), jnp.zeros((4, D), F32)]
    )

    def shape(dims, kind):
        return jax.ShapeDtypeStruct(dims, kind)

    args = (tok, left, right, w_query, w_key, w_value, taps)
    outs = (
        shape((count, D), BF16),
        shape((span, D), BF16),
        shape((span, D), BF16),
        shape((2, size, D), BF16),
        shape((D, count), BF16),
        shape((2, size, LANES), F32),
    )
    queries, keys, values, pool_own, tok_t, tap_masks = call(
        partial(project_kernel, row_len=row_len),
        info,
        args,
        [whole(a) for a in args],
        outs,
        [whole(a) for a in outs],
        (1,),
        [
            pltpu.VMEM((span, D), BF16),
            pltpu.VMEM((D // LANES, span, LANES), F32),
        ],
        2 * D * D * (count + 2 * span),
        "project",
    )

    pieces = [pool_own]
    for hop in range(1, ny):
        pieces.append(lax.ppermute(pool_own, "seq", hop_pairs("seq", ny, 2, ny - hop)))
    pieces = pieces + [lax.ppermute(piece, "seq", hop_pairs("seq", 2, 1, 1)) for piece in pieces]

    blocks = count // QB
    args = (queries, keys, values)
    outs = (
        shape((H, blocks, 2 * QB, QB), BF16),
        shape((D, count), F32),
        shape((PAIRS, 8, count), F32),
    )
    near_e, o_near, stats = call(
        partial(near_forward_kernel, row_len=row_len),
        info,
        args,
        [columns(a) for a in args],
        outs,
        [leading(outs[0], 2), leading(outs[1], LANES), leading(outs[2], 1)],
        (PAIRS,),
        [pltpu.VMEM((blocks, 2 * QB, QB), F32)],
        4 * H * 256 * 256 * count,
        "near_forward",
    )

    pool_all = seq * size
    args = (queries, o_near, stats) + tuple(pieces)
    outs = (
        shape((H, pool_all, count), BF16),
        shape((count, D), F32),
        shape((count, D), F32),
        shape((count, D), F32),
    )
    pool_e, attention, near_scale, pool_scale = call(
        partial(pool_forward_kernel, row_len=row_len, pieces=seq),
        info,
        args,
        [columns(queries), leading(o_near, LANES), leading(stats, 1)] + [columns(p) for p in pieces],
        outs,
        [leading(outs[0], 2)] + [columns(a) for a in outs[1:]],
        (PAIRS,),
        [pltpu.VMEM((pool_all, count), F32)],
        4 * H * 512 * 256 * count,
        "pool_forward",
    )

    dp = lax.axis_size("dp")
    nx = 2 if dp % 2 == 0 else 1
    nz = dp // nx
    rows = D // (seq * dp)
    back_rows = FF // (seq * dp)
    down = 2 if back_rows % 32 == 0 else 1
    half_one = shape((ny, nz, nx) + folded(rows, D), BF16)
    half_back = shape((2 * down, ny, nz, nx, back_rows // down, D // 2), BF16)
    args = (attention, tok, og, vecs, w_out, w_in, w_back)
    outs = (
        shape((count, D), BF16),
        shape((count, FF), BF16),
        shape((count, FF), BF16),
        shape((D, count), BF16),
        shape((count, D), BF16),
        shape((count, D), F32),
        shape((PAIRS, count, LANES), F32),
        shape((count, LANES), F32),
        shape((D, count), BF16),
        shape((8, D), F32),
    )
    mixed, act, slope, low_t, feed_grad, z_grad, unit_one, inv_one, att_t, sums = call(
        dense_kernel,
        info,
        args,
        [whole(a) for a in args[:5]]
        + [columns(w_in, D), pl.BlockSpec((D, D), lambda i, info: (i, 0))],
        outs,
        [whole(outs[0]), columns(outs[1], D), columns(outs[2], D)] + [whole(a) for a in outs[3:]],
        (CHUNKS,),
        [
            pltpu.VMEM((count, D), F32),
            pltpu.VMEM((count, D), BF16),
            pltpu.VMEM((count, D), F32),
        ],
        2 * count * (D * D + 2 * D * FF),
        "dense",
    )
    half_small = shape((ny, nz, nx, -(-rows // 16) * 16, LANES), BF16)
    half_pool = (PAIRS, ny, 2, size + EXTRA, LANES)
    blocks_in = []

    def block(name, array, spec):
        blocks_in.append((name, array, spec))

    def col_spec(array, index):
        lead = (0,) * (len(array.shape) - 1)
        return pl.BlockSpec(array.shape[:-1] + (LANES,), lambda i: lead + (index(i),))

    def lead_spec(array, index):
        rest = (0,) * (len(array.shape) - 1)
        return pl.BlockSpec((2,) + array.shape[1:], lambda i: (index(i),) + rest)

    def all_spec(array):
        rest = (0,) * len(array.shape)
        return pl.BlockSpec(array.shape, lambda i: rest)

    def in_pool(i):
        return jnp.clip(i - POOL, 0, PAIRS - 1)

    def in_near(i):
        return jnp.clip(i - NEAR, 0, PAIRS - 1)

    def in_both(i):
        return jnp.clip(i - POOL, 0, 2 * PAIRS - 1) % PAIRS

    def in_late(i):
        return jnp.clip(i - NEAR, 0, 2 * PAIRS - 1) % PAIRS

    block("q", queries, col_spec(queries, in_both))
    block("o", attention, col_spec(attention, in_both))
    block("rp", pool_scale, col_spec(pool_scale, in_pool))
    block("rn", near_scale, col_spec(near_scale, in_near))
    block("pool_e", pool_e, lead_spec(pool_e, in_pool))
    block("near_e", near_e, lead_spec(near_e, in_near))
    block("keys", keys, col_spec(keys, in_late))
    block("values", values, col_spec(values, in_late))
    for i, piece in enumerate(pieces):
        block("piece%d" % i, piece, col_spec(piece, in_pool))
    block("masks", tap_masks, all_spec(tap_masks))
    block("taps", taps, col_spec(taps, in_late))
    block("sums", sums, all_spec(sums))
    block("vecs", vecs, all_spec(vecs))
    block("inv", inv_one, all_spec(inv_one))
    anywhere = pl.BlockSpec(memory_space=pl.ANY)
    for name, array in (
        ("win_any", w_in),
        ("wback_any", w_back),
        ("act_any", act),
        ("slope_any", slope),
        ("fg_any", feed_grad),
        ("lowt_any", low_t),
        ("zg_any", z_grad),
        ("unit_any", unit_one),
        ("wout_any", w_out),
        ("att_any", att_t),
        ("tt_any", tok_t),
        ("wq_any", w_query),
        ("wk_any", w_key),
        ("wv_any", w_value),
    ):
        block(name, array, anywhere)
    outs = [
        ("t_in", shape((CHUNKS,) + half_one.shape[3:], F32)),
        ("t_back", shape((half_back.shape[0],) + half_back.shape[4:], F32)),
        ("t_query", shape(half_one.shape[3:], F32)),
        ("t_key", shape(half_one.shape[3:], F32)),
        ("t_value", shape(half_one.shape[3:], F32)),
        ("t_out", shape(half_one.shape[3:], F32)),
        ("t_small", shape(half_small.shape[3:], F32)),
        ("tokens_grad", shape((count, D), BF16)),
    ]
    tall = max(pool_all, span)
    scratch = [
        ("dk", pltpu.VMEM((tall, LANES), F32)),
        ("dv", pltpu.VMEM((tall, LANES), F32)),
        ("dq_pool", pltpu.VMEM((PAIRS, LANES, count), F32)),
        ("gb", pltpu.VMEM((count, LANES), BF16)),
        ("acc", pltpu.VMEM((2, PAIRS, count, LANES), F32)),
        ("tbuf", pltpu.VMEM((4, count, D), BF16)),
        ("wbuf", pltpu.VMEM((4, D, D), BF16)),
        ("fg", pltpu.VMEM((count, D), BF16)),
        ("lt", pltpu.VMEM((D, count), BF16)),
        ("att", pltpu.VMEM((D, count), BF16)),
        ("cells", pltpu.VMEM((span, LANES), F32)),
        ("g", pltpu.VMEM((size + EXTRA, LANES), F32)),
        ("small", pltpu.VMEM((LANES, D), F32)),
        ("small_t", pltpu.VMEM((D, LANES), F32)),
        ("p_keep", pltpu.VMEM(half_pool, BF16)),
        ("p_send", pltpu.VMEM(half_pool, BF16)),
        ("p_in", pltpu.VMEM(half_pool, BF16)),
        ("p_y", pltpu.VMEM((PAIRS, ny - 1) + half_pool[2:], BF16)),
        ("h_out", pltpu.VMEM((PAIRS, 2, 2, HALF, LANES), BF16)),
        ("h_in", pltpu.VMEM((PAIRS, 2, 2, HALF, LANES), BF16)),
        ("p_sem", pltpu.SemaphoreType.DMA((2, PAIRS, ny))),
        ("h_sem", pltpu.SemaphoreType.DMA((2, PAIRS, 2))),
        ("l_sem", pltpu.SemaphoreType.DMA((9, 2))),
        ("sg", pltpu.VMEM((count, D), F32)),
        ("a_send", pltpu.VMEM((CHUNKS,) + half_one.shape, BF16)),
        ("b_send", pltpu.VMEM(half_back.shape, BF16)),
        ("s_send", pltpu.VMEM(half_small.shape, BF16)),
    ]
    sizes = {name: half_one.shape for name in ORDERS}
    sizes["small"] = half_small.shape
    for u in range(CHUNKS):
        if u < half_back.shape[0]:
            sizes["b%d" % u] = half_back.shape[1:]
        else:
            del sizes["b%d" % u]
    for name, dims in sizes.items():
        bufs = summed_scratch(1, dims, ORDERS[name])
        scratch += [(name + "_" + part, buf) for part, buf in zip(BUFFERS, bufs)]
    names = [entry[0] for entry in blocks_in] + [entry[0] for entry in outs + scratch]
    moved = sum(entry[1].size * entry[1].dtype.itemsize for entry in blocks_in)
    totals = pl.pallas_call(
        partial(backward_kernel, names=names, pieces=seq),
        grid_spec=pltpu.PrefetchScalarGridSpec(
            num_scalar_prefetch=0,
            grid=(LAST + 1,),
            in_specs=[entry[2] for entry in blocks_in],
            out_specs=[all_spec(entry[1]) for entry in outs],
            scratch_shapes=[entry[1] for entry in scratch],
        ),
        out_shape=[entry[1] for entry in outs],
        compiler_params=pltpu.CompilerParams(
            collective_id=0,
            has_side_effects=True,
            vmem_limit_bytes=63 * MB,
            dimension_semantics=("arbitrary",),
        ),
        cost_estimate=pl.CostEstimate(
            flops=8 * H * 768 * 256 * count + 12 * count * D * D + 8 * count * D * FF, bytes_accessed=moved, transcendentals=0
        ),
        name="backward",
    )(*[entry[1] for entry in blocks_in])

    outs = (
        shape((count, D), BF16),
        shape((rows, D), F32),
        shape((rows, D), F32),
        shape((rows, D), F32),
        shape((rows, D), F32),
        shape((rows, FF), F32),
        shape((back_rows, D), F32),
        shape((1, rows), F32),
        shape((1, rows), F32),
        shape((1, rows), F32),
        shape((1, rows), F32),
        shape((rows, 5), F32),
    )
    done = call(
        lambda info, *refs: unpack_kernel(*refs),
        info,
        tuple(totals),
        [whole(a) for a in totals],
        outs,
        [whole(a) for a in outs],
        (1,),
        [],
        0,
        "unpack",
    )
    return (
        mixed[None],
        done[0][None],
        done[1],
        done[2],
        done[3],
        done[4],
        done[5],
        done[6],
        done[7].reshape(rows),
        done[8].reshape(rows),
        done[9].reshape(rows),
        done[10].reshape(rows),
        done[11],
    )


def solution(mesh):
    shards, copied = P("dp", "seq", None), P()
    spread = P(("seq", "dp"), None)
    vector = P(("seq", "dp"))
    return jax.shard_map(
        per_device,
        mesh=mesh,
        in_specs=(shards, P("dp", None)) + (copied,) * 11 + (shards,),
        out_specs=(shards, shards) + (spread,) * 6 + (vector,) * 4 + (spread,),
        check_vma=False,
    )
```

time: 207 us -> 180 us (0.87)
  Pallas kernels: 179 us -> 153 us
    pallas_call x5, Pallas kernels: 74.3 us -> 56.2 us  [call(): pl.pallas_call(kernel, grid_spec=pltpu.PrefetchScalarGridSpec(num_scalar_...]
    pallas_call x1, Pallas kernels: 105 us -> 96.7 us  [per_device(): pl.pallas_call(partial(backward_kernel, names=names, pieces=seq), grid_sp...]
  transfers between devices with their start and end apart: 5 -> 5, of which waited for: 1 -> 2; matrix products, arithmetic and copies ran while one was open for 2% -> 2% of each run, Pallas kernels for 5% -> 6%
where the time goes in v5:
time: 180 us
  Pallas kernels  153 us (85%)
  waiting for transfers between devices  10.9 us (6%)
  starting transfers between devices  7.71 us (4%)
  local copies, waits for them, and re-layouts  6.48 us (4%)
    pallas_call x1, Pallas kernels, per_device(): pl.pallas_call(partial(backward_kernel, names=names, pieces=seq), grid_sp...  96.7 us
    pallas_call x5, Pallas kernels, call(): pl.pallas_call(kernel, grid_spec=pltpu.PrefetchScalarGridSpec(num_scalar_...  56.2 us
    ppermute x1, waiting for transfers between devices, per_device(): lax.ppermute(pool_own, 'seq', hop_pairs('seq', ny, 2, ny - hop))  9.91 us
    ppermute x1, starting transfers between devices, per_device(): lax.ppermute(pool_own, 'seq', hop_pairs('seq', ny, 2, ny - hop))  3.94 us
    ppermute x2, starting transfers between devices, shifted(): lax.ppermute(block, 'seq', [(i, i + by) for i in range(size) if 0 <= i +...  3.65 us
  transfers between devices with their start and end apart: 5, of which 2 were waited for; matrix products, arithmetic and copies ran while one was open for 2% of the time, Pallas kernels for 6%

profile of v5, /device:TPU:0, one launch (start us, length us, event | category | flops | bytes accessed | tf_op | source)
XLA Modules:
  0.0 179.8 jit_solution(15398111659760228464)
XLA Ops:
  0.6 1.0 slice_bitcast_fusion
  1.6 2.4 %collective-permute-start = (bf16[64,768]{1,0:T(8,128)(2,1)S(1)}, bf16[64,768]{1,0:T(8,128)(2,1)S(1)}, u32[]{:S(2)}, u32[]{:S(2)}) collective-permute-start(bf16[64,768]{1,0:T(8,128)(2,1)S(1)} %get-tuple-element.113), channel_id=1, source_target_pairs={{0,8},{8,16},{16,24},{1,9},{9,17},{17,25},{2,10},{10,18},{18,26},{... | collective-permute-start | bytes 294920 | tf_op jit(solution)/shard_map/ppermute | solution.py:912
  4.0 1.3 collective-permute-start.1
  5.5 0.8 reduce-window.9
  6.3 1.3 pad.4.taps.refs_13_
  7.7 0.6 concatenate.6.info
  8.3 0.0 collective-permute-done.left
  8.3 1.0 collective-permute-done.1.right
  9.3 0.6 copy-done.8
  10.0 7.0 %project.1 = (bf16[512,768]{1,0:T(8,128)(2,1)}, bf16[640,768]{1,0:T(8,128)(2,1)}, bf16[640,768]{1,0:T(8,128)(2,1)}, bf16[2,128,768]{2,1,0:T(8,128)(2,1)}, bf16[7...) custom-call(s32[16]{0:T(128)} %concatenate.6.info, bf16[512,768]{1,0:T(8,128)(2,1)} %bitcast.26, bf16[64,768]{1,0:T(8,128)(2,1)} %copy-done.7, ...), custom_call_target="tpu_custom_call" | custom-call | flops 2113929216 | bytes 8609792 | tf_op jit(solution)/shard_map/project/pallas_call | solution.py:917
  16.9 3.9 %collective-permute-start.2 = (bf16[2,128,768]{2,1,0:T(8,128)(2,1)}, bf16[2,128,768]{2,1,0:T(8,128)(2,1)S(1)}, u32[]{:S(2)}, u32[]{:S(2)}) collective-permute-start(bf16[2,128,768]{2,1,0:T(8,128)(2,1)} %get-tuple-element.61.rest_0_.refs_8_), channel_id=1, source_target_pairs={{0,16},{8,24},{16,0},{24,8},{1,17},{9,25},{17,1},{25,9},{2,18},{10... | collective-permute-start | bytes 1179656 | tf_op jit(solution)/shard_map/ppermute | solution.py:1028
  20.9 0.0 collective-permute-start.3
  20.9 9.9 %collective-permute-done.2.rest_1_.refs_9_ = bf16[2,128,768]{2,1,0:T(8,128)(2,1)S(1)} collective-permute-done((bf16[2,128,768]{2,1,0:T(8,128)(2,1)}, bf16[2,128,768]{2,1,0:T(8,128)(2,1)S(1)}, u32[]{:S(2)}, u32[]{:S(2)}) %collective-permute-start.2) | collective-permute-done | bytes 393248 | tf_op jit(solution)/shard_map/ppermute | solution.py:1028
  30.8 0.1 collective-permute-start.4
  31.0 0.6 concatenate.7.vecs.refs_15_
  31.6 10.4 %near_forward.1 = (bf16[12,4,256,128]{3,2,1,0:T(8,128)(2,1)}, f32[768,512]{1,0:T(8,128)}, f32[6,8,512]{2,1,0:T(8,128)}) custom-call(s32[16]{0:T(128)} %concatenate.6.info, bf16[512,768]{1,0:T(8,128)(2,1)} %get-tuple-element.56.q.refs_0_, bf16[640,768]{1,0:T(8,128)(2,1)} %get-tuple-element.57.k.refs_6_, bf16[640,768]{1,0:T(8,128)(2,1)} %get-tuple-element.58.v.refs_7_), custom_call_target="tpu_custom_call" | custom-call | flops 1610612736 | bytes 7569408 | tf_op jit(solution)/shard_map/near_forward/pallas_call | solution.py:917
  42.1 0.0 collective-permute-done.3.rest_2_.refs_10_
  42.1 0.7 copy-done.5
  42.8 0.1 copy-done.6
  43.0 15.3 %pool_forward.1 = (bf16[12,512,512]{2,1,0:T(8,128)(2,1)}, f32[512,768]{1,0:T(8,128)}, f32[512,768]{1,0:T(8,128)}, f32[512,768]{1,0:T(8,128)}) custom-call(s32[16]{0:T(128)} %concatenate.6.info, bf16[512,768]{1,0:T(8,128)(2,1)} %get-tuple-element.56.q.refs_0_, f32[768,512]{1,0:T(8,128)} %get-tuple-element.59.o_near, f32[6,8,512]{2,1,0:T(8,128)} %get-tuple-element.60.st, ...), custom_call_target="tpu_custom_call" | custom-call | flops 3221225472 | bytes 15040512 | tf_op jit(solution)/shard_map/pool_forward/pallas_call | solution.py:917
  58.3 20.1 %dense.1 = (bf16[512,768]{1,0:T(8,128)(2,1)}, bf16[512,3072]{1,0:T(8,128)(2,1)}, bf16[512,3072]{1,0:T(8,128)(2,1)}, bf16[768,512]{1,0:T(8,128)(2,1)}, bf16[512,7...) custom-call(s32[16]{0:T(128)} %concatenate.6.info, ...), custom_call_target="tpu_custom_call" | custom-call | flops 5435817984 | bytes 26656768 | tf_op jit(solution)/shard_map/dense/pallas_call | solution.py:917
  78.4 96.7 %backward.1 = (f32[4,48,384]{2,1,0:T(8,128)}, f32[4,48,384]{2,1,0:T(8,128)}, f32[48,384]{1,0:T(8,128)}, f32[48,384]{1,0:T(8,128)}, f32[48,384]{1,0:T(8,128)}, /*...) custom-call(bf16[512,768]{1,0:T(8,128)(2,1)} %get-tuple-element.56.q.refs_0_, ...), custom_call_target="tpu_custom_call" | custom-call | flops 22951231488 | bytes 45686784 | tf_op jit(solution)/shard_map/backward/pallas_call | solution.py:1226
  175.1 3.3 %unpack.1 = (bf16[512,768]{1,0:T(8,128)(2,1)}, f32[24,768]{1,0:T(8,128)}, f32[24,768]{1,0:T(8,128)}, f32[24,768]{1,0:T(8,128)}, f32[24,768]{1,0:T(8,128)}, /*ind...) custom-call(s32[16]{0:T(128)} %concatenate.6.info, ...), custom_call_target="tpu_custom_call" | custom-call | bytes 3359584 | tf_op jit(solution)/shard_map/unpack/pallas_call | solution.py:917
  178.5 1.4 copy.27
  (21 shorter events, 0.0 us)
Async XLA Ops:
  1.6 6.7 %collective-permute-start = (bf16[64,768]{1,0:T(8,128)(2,1)S(1)}, bf16[64,768]{1,0:T(8,128)(2,1)S(1)}, u32[]{:S(2)}, u32[]{:S(2)}) collective-permute-start(bf16[64,768]{1,0:T(8,128)(2,1)S(1)} %get-tuple-element.113), channel_id=1, source_target_pairs={{0,8},{8,16},{16,24},{1,9},{9,17},{17,25},{2,10},{10,18},{18,26},{... | collective-permute-start | bytes 294920 | tf_op jit(solution)/shard_map/ppermute | solution.py:912
  4.0 5.3 %collective-permute-start.1 = (bf16[64,768]{1,0:T(8,128)(2,1)S(1)}, bf16[64,768]{1,0:T(8,128)(2,1)S(1)}, u32[]{:S(2)}, u32[]{:S(2)}) collective-permute-start(bf16[64,768]{1,0:T(8,128)(2,1)S(1)} %get-tuple-element.112), channel_id=1, source_target_pairs={{8,0},{16,8},{24,16},{9,1},{17,9},{25,17},{10,2},{18,10},{26,18},{... | collective-permute-start | bytes 294920 | tf_op jit(solution)/shard_map/ppermute | solution.py:912
  8.3 1.0 copy-start.7
  9.3 0.6 copy-start.8
  9.9 21.0 %copy-start = (f32[768]{0:T(1024)S(1)}, f32[768]{0:T(1024)}, u32[]{:S(2)}) copy-start(f32[768]{0:T(1024)} %param.22) | copy-start | bytes 9220
  9.9 21.0 %copy-start.1 = (f32[768]{0:T(1024)S(1)}, f32[768]{0:T(1024)}, u32[]{:S(2)}) copy-start(f32[768]{0:T(1024)} %param.23) | copy-start | bytes 9220
  9.9 21.0 %copy-start.2 = (f32[768]{0:T(1024)S(1)}, f32[768]{0:T(1024)}, u32[]{:S(2)}) copy-start(f32[768]{0:T(1024)} %param.24) | copy-start | bytes 9220
  9.9 21.0 %copy-start.3 = (f32[768]{0:T(1024)S(1)}, f32[768]{0:T(1024)}, u32[]{:S(2)}) copy-start(f32[768]{0:T(1024)} %param.25) | copy-start | bytes 9220
  16.9 13.9 %collective-permute-start.2 = (bf16[2,128,768]{2,1,0:T(8,128)(2,1)}, bf16[2,128,768]{2,1,0:T(8,128)(2,1)S(1)}, u32[]{:S(2)}, u32[]{:S(2)}) collective-permute-start(bf16[2,128,768]{2,1,0:T(8,128)(2,1)} %get-tuple-element.61.rest_0_.refs_8_), channel_id=1, source_target_pairs={{0,16},{8,24},{16,0},{24,8},{1,17},{9,25},{17,1},{25,9},{2,18},{10... | collective-permute-start | bytes 1179656 | tf_op jit(solution)/shard_map/ppermute | solution.py:1028
  20.9 21.2 %collective-permute-start.3 = (bf16[2,128,768]{2,1,0:T(8,128)(2,1)}, bf16[2,128,768]{2,1,0:T(8,128)(2,1)S(1)}, u32[]{:S(2)}, u32[]{:S(2)}) collective-permute-start(bf16[2,128,768]{2,1,0:T(8,128)(2,1)} %get-tuple-element.61.rest_0_.refs_8_), channel_id=1, source_target_pairs={{0,8},{8,0},{16,24},{24,16},{1,9},{9,1},{17,25},{25,17},{2,10},{10... | collective-permute-start | bytes 1179656 | tf_op jit(solution)/shard_map/ppermute | solution.py:1029
  30.8 11.3 %copy-start.4 = (bf16[2,128,768]{2,1,0:T(8,128)(2,1)}, bf16[2,128,768]{2,1,0:T(8,128)(2,1)S(1)}, u32[]{:S(2)}) copy-start(bf16[2,128,768]{2,1,0:T(8,128)(2,1)S(1)} %collective-permute-done.2.rest_1_.refs_9_) | copy-start | bytes 1179652
  30.8 11.3 %collective-permute-start.4 = (bf16[2,128,768]{2,1,0:T(8,128)(2,1)S(1)}, bf16[2,128,768]{2,1,0:T(8,128)(2,1)S(1)}, u32[]{:S(2)}, u32[]{:S(2)}) collective-permute-start(bf16[2,128,768]{2,1,0:T(8,128)(2,1)S(1)} %collective-permute-done.2.rest_1_.refs_9_), channel_id=1, source_target_pairs={{0,8},{8,0},{16,24},{24,16},{1,9},{9,1},{17,25},{25,17},{2,10},{10... | collective-permute-start | bytes 1179656 | tf_op jit(solution)/shard_map/ppermute | solution.py:1029
  42.1 0.7 copy-start.5
  42.1 0.9 copy-start.6

commit v6 on v5

--- a/solution.py
+++ b/solution.py
@@ -36,10 +36,10 @@
     return lax.broadcasted_iota(jnp.int32, shape, dim)
 
 
-def segment_of(info, place, row_len):
+def segment_of(ends, place, row_len):
     item = jnp.zeros_like(place)
-    for m in range(4):
-        item = item + (place >= info[m]).astype(jnp.int32)
+    for end in ends:
+        item = item + (place >= end).astype(jnp.int32)
     return jnp.where((place >= 0) & (place < row_len), item, -2)
 
 
@@ -48,9 +48,9 @@
     return jnp.where((lane < 64) == (head == 0), block, jnp.zeros_like(block))
 
 
-def tap_mask(info, tap, shift, count, row_len):
-    center = info[4] + 4 * (iota((count, 1), 0) + shift)
-    same = segment_of(info, center + tap - 2, row_len) == segment_of(info, center, row_len)
+def tap_mask(ends, start, tap, shift, count, row_len):
+    center = start + 4 * (iota((count, 1), 0) + shift)
+    same = segment_of(ends, center + tap - 2, row_len) == segment_of(ends, center, row_len)
     return (same & (center < row_len)).astype(F32)
 
 
@@ -97,111 +97,6 @@
                 target[block, z, x] = total[top : top + part, left : left + wide].astype(BF16)
 
 
-def project_kernel(info, tok, left, right, wq, wk, wv, taps, q_out, k_out, v_out, pool_out, tt_out, mask_out, x, cells, *, row_len):
-    count = tok.shape[0]
-    x[0:HALF] = left[...]
-    x[HALF : HALF + count] = tok[...]
-    x[HALF + count :] = right[...]
-    k_low = nn(x[...], wk[...]).astype(BF16)
-    k_out[...] = k_low
-    v_low = nn(x[...], wv[...]).astype(BF16)
-    v_out[...] = v_low
-    masks = [tap_mask(info, tap, 0, count // 4, row_len) for tap in range(5)]
-    for which, low in ((0, k_low), (1, v_low)):
-        wide = low.astype(F32)
-        for c in range(D // LANES):
-            lanes = slice(c * LANES, (c + 1) * LANES)
-            cells[c] = wide[:, lanes]
-            total = jnp.zeros((count // 4, LANES), F32)
-            for tap in range(5):
-                taken = cells.at[c][pl.ds(HALF + tap - 2, count // 4, stride=4), :]
-                total = total + taken * masks[tap] * taps[tap : tap + 1, lanes]
-            pool_out[which, :, lanes] = total.astype(BF16)
-    q_out[...] = (nn(tok[...], wq[...]).astype(BF16).astype(F32) * 0.125).astype(BF16)
-    tt_out[...] = tok[...].T
-    lane = iota((count // 4, LANES), 1)
-    for shift in range(2):
-        total = jnp.zeros((count // 4, LANES), F32)
-        for tap in range(5):
-            mask = tap_mask(info, tap, shift, count // 4, row_len)
-            total = jnp.where(lane == tap, mask, total)
-        mask_out[shift] = total
-
-
-def near_forward_kernel(info, q, k, v, e_out, o_out, st_out, bias, *, row_len):
-    count, span = q.shape[0], k.shape[0]
-    blocks = count // QB
-
-    @pl.when(pl.program_id(0) == 0)
-    def _():
-        for b in range(blocks):
-            query_place = info[4] + b * QB + iota((1, QB), 1)
-            key_place = info[4] - HALF + b * QB + iota((2 * QB, 1), 0)
-            same = segment_of(info, key_place, row_len) == segment_of(info, query_place, row_len)
-            near = jnp.abs(key_place - query_place) <= HALF
-            bias[b] = jnp.where(same & near, 0.0, -1e30)
-
-    vt = v[...].T
-    ones = jnp.ones((16, span), BF16)
-    st_out[...] = jnp.zeros_like(st_out)
-    for head in range(2):
-        qh = head_half(q[...], head)
-        va = jnp.concatenate([vt[head * 64 : head * 64 + 64], ones], axis=0)
-        for b in range(blocks):
-            cols = slice(b * QB, (b + 1) * QB)
-            keys = slice(b * QB, (b + 2) * QB)
-            s = nt(k[keys, :], qh[cols]) + bias[b]
-            top = jnp.max(s, axis=0, keepdims=True)
-            e = jnp.exp(s - top).astype(BF16)
-            e_out[head, b] = e
-            oa = nn(va[:, keys], e)
-            o_out[head * 64 : head * 64 + 64, cols] = oa[:64]
-            st_out[0, head : head + 1, cols] = top
-            st_out[0, 2 + head : 3 + head, cols] = oa[64:65]
-
-
-def pool_forward_kernel(info, q, o_near, st, *rest, row_len, pieces):
-    kv = rest[:pieces]
-    e_out, o_out, rn_out, rp_out, bias = rest[pieces:]
-    count = q.shape[0]
-    size = kv[0].shape[1]
-
-    @pl.when(pl.program_id(0) == 0)
-    def _():
-        query_place = info[4] + iota((1, count), 1)
-        query_item = segment_of(info, query_place, row_len)
-        for i in range(pieces):
-            key_place = 4 * (info[8 + i] * size + iota((size, 1), 0))
-            same = segment_of(info, key_place, row_len) == query_item
-            near = jnp.abs(key_place - query_place) <= 2 * PWIN
-            bias[i * size : (i + 1) * size] = jnp.where(same & near, 0.0, -1e30)
-
-    kp = jnp.concatenate([piece[0] for piece in kv], axis=0)
-    vt = jnp.concatenate([piece[1] for piece in kv], axis=0).T
-    ones = jnp.ones((16, pieces * size), BF16)
-    wide = min(256, count)
-    for b in range(count // wide):
-        cols = slice(b * wide, (b + 1) * wide)
-        outs, near_scale, pool_scale = [], [], []
-        for head in range(2):
-            qh = head_half(q[cols, :], head)
-            va = jnp.concatenate([vt[head * 64 : head * 64 + 64], ones], axis=0)
-            s = nt(kp, qh) + bias[:, cols]
-            near_top = st[0, head : head + 1, cols]
-            top = jnp.maximum(jnp.max(s, axis=0, keepdims=True), near_top)
-            e = jnp.exp(s - top).astype(BF16)
-            e_out[head, :, cols] = e
-            oa = nn(va, e)
-            fade = jnp.exp(near_top - top)
-            inverse = 1.0 / (fade * st[0, 2 + head : 3 + head, cols] + oa[64:65])
-            outs.append((fade * o_near[head * 64 : head * 64 + 64, cols] + oa[:64]) * inverse)
-            near_scale.append(jnp.broadcast_to(fade * inverse, (64, wide)))
-            pool_scale.append(jnp.broadcast_to(inverse, (64, wide)))
-        o_out[cols, :] = jnp.concatenate(outs, axis=0).T
-        rn_out[cols, :] = jnp.concatenate(near_scale, axis=0).T
-        rp_out[cols, :] = jnp.concatenate(pool_scale, axis=0).T
-
-
 def normal_parts(v):
     bell = jnp.exp(v * v * -0.5)
     t = 1.0 / (1.0 + jnp.abs(v) * (0.3275911 * 0.7071067811865476))
@@ -219,7 +114,7 @@
 
 
 def dense_kernel(
-    info, o, tok, og, vecs, w_out, w_in, w_back,
+    o, tok, og, vecs, w_out, w_in, w_back,
     mixed, act, slope, low_t, feed_grad, z_grad, unit_out, inv_out, att_t, sums,
     first, low, feed,
 ):
@@ -386,6 +281,230 @@
     for peer in peers:
         pl.semaphore_signal(barrier, inc=1, device_id=peer, device_id_type=MESH_ID)
     pl.semaphore_wait(barrier, len(peers))
+
+
+class Refs:
+    pass
+
+
+FORWARD_NEAR = 1
+FORWARD_POOL = 1 + PAIRS
+FORWARD_LAST = 2 * PAIRS
+
+
+def forward_kernel(*refs, names):
+    r = Refs()
+    for name, ref in zip(names, refs):
+        setattr(r, name, ref)
+    seq, _, size, _ = r.pieces.shape
+    ny = seq // 2
+    count, row_len = 4 * size, 4 * size * seq
+    span = count + 2 * HALF
+    step = pl.program_id(0)
+    here, row = lax.axis_index("seq"), lax.axis_index("dp")
+    y, core = here // 2, here % 2
+    start = here * count
+    partner = (y * 2 + 1 - core, row)
+    right, left = ((here + 1) % seq, row), ((here + seq - 1) % seq, row)
+    ends = [r.lengths[0, 0]]
+    for m in range(1, 4):
+        ends.append(ends[-1] + r.lengths[0, m])
+
+    def copy(src, dst, slot, device):
+        return pltpu.make_async_remote_copy(
+            src_ref=src, dst_ref=dst, send_sem=r.s_sem.at[slot], recv_sem=r.r_sem.at[slot],
+            device_id=device, device_id_type=MESH_ID,
+        )
+
+    own = r.x.at[HALF : HALF + count]
+    to_right = copy(r.tok.at[count - HALF :], r.x.at[0:HALF], 0, right)
+    to_left = copy(r.tok.at[0:HALF], r.x.at[HALF + count :], 1, left)
+
+    def to_y(hop):
+        device = (((y + hop) % ny) * 2 + core, row)
+        return copy(r.pieces.at[0], r.pieces.at[ny - hop], 1 + hop, device)
+
+    def to_core(hop):
+        return copy(r.pieces.at[hop], r.pieces.at[ny + hop], 1 + ny + hop, partner)
+
+    loads = [
+        pltpu.make_async_copy(r.tok, own, r.l_sem.at[0]),
+        pltpu.make_async_copy(r.wk_any, r.wk, r.l_sem.at[1]),
+        pltpu.make_async_copy(r.wv_any, r.wv, r.l_sem.at[2]),
+        pltpu.make_async_copy(r.wq_any, r.wq, r.l_sem.at[3]),
+    ]
+    stores = [
+        pltpu.make_async_copy(r.qs, r.q_out, r.l_sem.at[4]),
+        pltpu.make_async_copy(r.ks, r.k_out, r.l_sem.at[5]),
+        pltpu.make_async_copy(r.vs, r.v_out, r.l_sem.at[6]),
+        pltpu.make_async_copy(r.tt, r.tt_out, r.l_sem.at[7]),
+        pltpu.make_async_copy(r.mask, r.mask_out, r.l_sem.at[8]),
+        pltpu.make_async_copy(r.tap, r.tap_out, r.l_sem.at[9]),
+    ]
+    store_pieces = pltpu.make_async_copy(r.pieces, r.pieces_out, r.l_sem.at[10])
+
+    @pl.when(step == 0)
+    def _():
+        for load in loads:
+            load.start()
+        greet([partner, right, left] + [(((y + hop) % ny) * 2 + core, row) for hop in range(1, ny)])
+
+        @pl.when(here < seq - 1)
+        def _():
+            to_right.start()
+
+        @pl.when(here > 0)
+        def _():
+            to_left.start()
+
+        @pl.when(here == 0)
+        def _():
+            r.x[0:HALF] = jnp.zeros((HALF, D), BF16)
+
+        @pl.when(here == seq - 1)
+        def _():
+            r.x[HALF + count :] = jnp.zeros((HALF, D), BF16)
+
+        pick = (iota((8, 5), 0) == iota((8, 5), 1)).astype(F32)
+        r.tap[...] = nt(pick, r.pool_weight[...], precision=lax.Precision.HIGHEST)
+        lane = iota((size, LANES), 1)
+        masks = [[tap_mask(ends, start, tap, shift, size, row_len) for tap in range(5)] for shift in range(2)]
+        for shift in range(2):
+            total = jnp.zeros((size, LANES), F32)
+            for tap in range(5):
+                total = jnp.where(lane == tap, masks[shift][tap], total)
+            r.mask[shift] = total
+        loads[0].wait()
+        inner = slice(HALF, HALF + count)
+        for weight, load, cells in ((r.wk, loads[1], r.ks), (r.wv, loads[2], r.vs)):
+            load.wait()
+            cells[inner] = nn(r.x[inner], weight[...]).astype(BF16)
+
+        @pl.when(here > 0)
+        def _():
+            to_right.wait_recv()
+
+        @pl.when(here < seq - 1)
+        def _():
+            to_left.wait_recv()
+
+        for weight, cells in ((r.wk, r.ks), (r.wv, r.vs)):
+            for outer in (slice(0, HALF), slice(HALF + count, span)):
+                cells[outer] = nn(r.x[outer], weight[...]).astype(BF16)
+        for which, source in ((0, r.ks), (1, r.vs)):
+            for c in range(PAIRS):
+                lanes = slice(c * LANES, (c + 1) * LANES)
+                r.cells[c] = source[:, lanes].astype(F32)
+                total = jnp.zeros((size, LANES), F32)
+                for tap in range(5):
+                    taken = r.cells.at[c][pl.ds(HALF + tap - 2, size, stride=4), :]
+                    total = total + taken * masks[0][tap] * r.tap[tap : tap + 1, lanes]
+                r.pieces[0, which, :, lanes] = total.astype(BF16)
+        for hop in range(1, ny):
+            to_y(hop).start()
+        to_core(0).start()
+        loads[3].wait()
+        r.qs[...] = (nn(r.x[inner], r.wq[...]).astype(BF16).astype(F32) * 0.125).astype(BF16)
+        r.tt[...] = r.x[inner].T
+        for store in stores:
+            store.start()
+        for b in range(count // QB):
+            query_place = start + b * QB + iota((1, QB), 1)
+            key_place = start - HALF + b * QB + iota((2 * QB, 1), 0)
+            same = segment_of(ends, key_place, row_len) == segment_of(ends, query_place, row_len)
+            near = jnp.abs(key_place - query_place) <= HALF
+            r.near_bias[b] = jnp.where(same & near, 0.0, -1e30)
+
+    @pl.when((step >= FORWARD_NEAR) & (step < FORWARD_POOL))
+    def _():
+        p = step - FORWARD_NEAR
+        lanes = pl.ds(pl.multiple_of(p * LANES, LANES), LANES)
+        vt = r.vs[:, lanes].T
+        ones = jnp.ones((16, span), BF16)
+        for head in range(2):
+            qh = head_half(r.qs[:, lanes], head)
+            va = jnp.concatenate([vt[head * 64 : head * 64 + 64], ones], axis=0)
+            for b in range(count // QB):
+                cols = slice(b * QB, (b + 1) * QB)
+                keys = slice(b * QB, (b + 2) * QB)
+                s = nt(r.ks[keys, lanes], qh[cols]) + r.near_bias[b]
+                top = jnp.max(s, axis=0, keepdims=True)
+                e = jnp.exp(s - top).astype(BF16)
+                r.near_e[head, b] = e
+                oa = nn(va[:, keys], e)
+                r.o_near[p, head * 64 : head * 64 + 64, cols] = oa[:64]
+                r.stats[p, head : head + 1, cols] = top
+                r.stats[p, 2 + head : 3 + head, cols] = oa[64:65]
+
+    @pl.when(step == FORWARD_POOL - 2)
+    def _():
+        query_place = start + iota((1, count), 1)
+        query_item = segment_of(ends, query_place, row_len)
+        for i in range(seq):
+            owner = ((y + i % ny) % ny) * 2 + (core + i // ny) % 2
+            key_place = 4 * (owner * size + iota((size, 1), 0))
+            same = segment_of(ends, key_place, row_len) == query_item
+            near = jnp.abs(key_place - query_place) <= 2 * PWIN
+            r.pool_bias[i * size : (i + 1) * size] = jnp.where(same & near, 0.0, -1e30)
+
+    @pl.when(step == FORWARD_POOL - 1)
+    def _():
+        for hop in range(1, ny):
+            to_y(ny - hop).wait_recv()
+            to_core(hop).start()
+
+    @pl.when(step == FORWARD_POOL)
+    def _():
+        for hop in range(ny):
+            to_core(hop).wait_recv()
+        store_pieces.start()
+
+    @pl.when(step >= FORWARD_POOL)
+    def _():
+        p = step - FORWARD_POOL
+        lanes = pl.ds(pl.multiple_of(p * LANES, LANES), LANES)
+        kp = jnp.concatenate([r.pieces[i, 0, :, lanes] for i in range(seq)], axis=0)
+        vt = jnp.concatenate([r.pieces[i, 1, :, lanes] for i in range(seq)], axis=0).T
+        ones = jnp.ones((16, seq * size), BF16)
+        wide = min(256, count)
+        for b in range(count // wide):
+            cols = slice(b * wide, (b + 1) * wide)
+            outs, near_scale, pool_scale = [], [], []
+            for head in range(2):
+                qh = head_half(r.qs[cols, lanes], head)
+                va = jnp.concatenate([vt[head * 64 : head * 64 + 64], ones], axis=0)
+                s = nt(kp, qh) + r.pool_bias[:, cols]
+                near_top = r.stats[p, head : head + 1, cols]
+                top = jnp.maximum(jnp.max(s, axis=0, keepdims=True), near_top)
+                e = jnp.exp(s - top).astype(BF16)
+                r.pool_e[head, :, cols] = e
+                oa = nn(va, e)
+                fade = jnp.exp(near_top - top)
+                inverse = 1.0 / (fade * r.stats[p, 2 + head : 3 + head, cols] + oa[64:65])
+                rows = slice(head * 64, head * 64 + 64)
+                outs.append((fade * r.o_near[p, rows, cols] + oa[:64]) * inverse)
+                near_scale.append(jnp.broadcast_to(fade * inverse, (64, wide)))
+                pool_scale.append(jnp.broadcast_to(inverse, (64, wide)))
+            r.o_out[cols, :] = jnp.concatenate(outs, axis=0).T
+            r.rn_out[cols, :] = jnp.concatenate(near_scale, axis=0).T
+            r.rp_out[cols, :] = jnp.concatenate(pool_scale, axis=0).T
+
+    @pl.when(step == FORWARD_LAST)
+    def _():
+        for store in stores + [store_pieces]:
+            store.wait()
+        for hop in range(1, ny):
+            to_y(hop).wait_send()
+        for hop in range(ny):
+            to_core(hop).wait_send()
+
+        @pl.when(here < seq - 1)
+        def _():
+            to_right.wait_send()
+
+        @pl.when(here > 0)
+        def _():
+            to_left.wait_send()
 
 
 CHUNKS = FF // D
@@ -494,15 +613,11 @@
     ),
 }
 
-class Refs:
-    pass
-
-
 def backward_kernel(*refs, names, pieces):
     r = Refs()
     for name, ref in zip(names, refs):
         setattr(r, name, ref)
-    kv = [getattr(r, "piece%d" % i) for i in range(pieces)]
+    kv = [r.piece.at[i] for i in range(pieces)]
     seq, ny = pieces, pieces // 2
     step = pl.program_id(0)
     count = r.q.shape[0]
@@ -907,17 +1022,12 @@
     outs[11][...] = small[0:rows, 8:13]
 
 
-def shifted(block, by):
-    size = lax.axis_size("seq")
-    return lax.ppermute(block, "seq", [(i, i + by) for i in range(size) if 0 <= i + by < size])
-
-
-def call(kernel, info, args, in_specs, outs, out_specs, grid, scratch, flops, name):
+def call(kernel, args, in_specs, outs, out_specs, grid, scratch, flops, name):
     moved = sum(a.size * a.dtype.itemsize for a in list(args) + list(outs))
     return pl.pallas_call(
         kernel,
         grid_spec=pltpu.PrefetchScalarGridSpec(
-            num_scalar_prefetch=1,
+            num_scalar_prefetch=0,
             grid=grid,
             in_specs=in_specs,
             out_specs=out_specs,
@@ -929,22 +1039,22 @@
         ),
         cost_estimate=pl.CostEstimate(flops=flops, bytes_accessed=moved, transcendentals=0),
         name=name,
-    )(info, *args)
+    )(*args)
 
 
 def whole(array):
     rank = len(array.shape)
-    return pl.BlockSpec(array.shape, lambda i, info: (0,) * rank)
+    return pl.BlockSpec(array.shape, lambda i: (0,) * rank)
 
 
 def columns(array, width=LANES):
     rank = len(array.shape)
-    return pl.BlockSpec(array.shape[:-1] + (width,), lambda i, info: (0,) * (rank - 1) + (i,))
+    return pl.BlockSpec(array.shape[:-1] + (width,), lambda i: (0,) * (rank - 1) + (i,))
 
 
 def leading(array, size):
     rank = len(array.shape)
-    return pl.BlockSpec((size,) + array.shape[1:], lambda i, info: (i,) + (0,) * (rank - 1))
+    return pl.BlockSpec((size,) + array.shape[1:], lambda i: (i,) + (0,) * (rank - 1))
 
 
 def per_device(
@@ -969,28 +1079,8 @@
     row_len = count * seq
     span = count + 2 * HALF
     size = count // 4
-    here = lax.axis_index("seq")
-    core, y = here % 2, here // 2
-    owners = []
-    for other in range(2):
-        for hop in range(ny):
-            owners.append(((y + hop) % ny) * 2 + jnp.bitwise_xor(core, other))
-    afters = []
-    for owner in owners:
-        after = jnp.minimum(owner + 1, seq - 1)
-        afters.append(jnp.bitwise_xor(after % 2, core) * ny + (after // 2 - y) % ny)
-    zero = jnp.zeros((), jnp.int32)
-    info = jnp.concatenate(
-        [
-            jnp.cumsum(item_lengths[0]).astype(jnp.int32),
-            jnp.stack([here * count, core, y, zero] + owners + afters).astype(jnp.int32),
-        ]
-    )
     tok = tokens[0]
     og = out_grad[0]
-    left = shifted(tok[count - HALF :], 1)
-    right = shifted(tok[:HALF], -1)
-    taps = jnp.pad(pool_weight.T, ((0, 3), (0, 0)))
     vecs = jnp.concatenate(
         [jnp.stack([norm1_gain, norm1_bias, norm2_gain, norm2_bias]), jnp.zeros((4, D), F32)]
     )
@@ -998,75 +1088,84 @@
     def shape(dims, kind):
         return jax.ShapeDtypeStruct(dims, kind)
 
-    args = (tok, left, right, w_query, w_key, w_value, taps)
-    outs = (
-        shape((count, D), BF16),
-        shape((span, D), BF16),
-        shape((span, D), BF16),
-        shape((2, size, D), BF16),
-        shape((D, count), BF16),
-        shape((2, size, LANES), F32),
-    )
-    queries, keys, values, pool_own, tok_t, tap_masks = call(
-        partial(project_kernel, row_len=row_len),
-        info,
-        args,
-        [whole(a) for a in args],
-        outs,
-        [whole(a) for a in outs],
-        (1,),
-        [
-            pltpu.VMEM((span, D), BF16),
-            pltpu.VMEM((D // LANES, span, LANES), F32),
-        ],
-        2 * D * D * (count + 2 * span),
-        "project",
-    )
-
-    pieces = [pool_own]
-    for hop in range(1, ny):
-        pieces.append(lax.ppermute(pool_own, "seq", hop_pairs("seq", ny, 2, ny - hop)))
-    pieces = pieces + [lax.ppermute(piece, "seq", hop_pairs("seq", 2, 1, 1)) for piece in pieces]
-
     blocks = count // QB
-    args = (queries, keys, values)
-    outs = (
-        shape((H, blocks, 2 * QB, QB), BF16),
-        shape((D, count), F32),
-        shape((PAIRS, 8, count), F32),
-    )
-    near_e, o_near, stats = call(
-        partial(near_forward_kernel, row_len=row_len),
-        info,
-        args,
-        [columns(a) for a in args],
-        outs,
-        [leading(outs[0], 2), leading(outs[1], LANES), leading(outs[2], 1)],
-        (PAIRS,),
-        [pltpu.VMEM((blocks, 2 * QB, QB), F32)],
-        4 * H * 256 * 256 * count,
-        "near_forward",
-    )
-
     pool_all = seq * size
-    args = (queries, o_near, stats) + tuple(pieces)
-    outs = (
-        shape((H, pool_all, count), BF16),
-        shape((count, D), F32),
-        shape((count, D), F32),
-        shape((count, D), F32),
-    )
-    pool_e, attention, near_scale, pool_scale = call(
-        partial(pool_forward_kernel, row_len=row_len, pieces=seq),
-        info,
-        args,
-        [columns(queries), leading(o_near, LANES), leading(stats, 1)] + [columns(p) for p in pieces],
-        outs,
-        [leading(outs[0], 2)] + [columns(a) for a in outs[1:]],
-        (PAIRS,),
-        [pltpu.VMEM((pool_all, count), F32)],
-        4 * H * 512 * 256 * count,
-        "pool_forward",
+    anywhere = pl.BlockSpec(memory_space=pl.ANY)
+
+    def in_first(i):
+        return jnp.clip(i - FORWARD_NEAR, 0, PAIRS - 1)
+
+    def in_second(i):
+        return jnp.clip(i - FORWARD_POOL, 0, PAIRS - 1)
+
+    ins = [
+        ("lengths", item_lengths, pl.BlockSpec(memory_space=pltpu.SMEM)),
+        ("pool_weight", pool_weight, whole(pool_weight)),
+        ("tok", tok, anywhere),
+        ("wq_any", w_query, anywhere),
+        ("wk_any", w_key, anywhere),
+        ("wv_any", w_value, anywhere),
+    ]
+    near_shape = shape((H, blocks, 2 * QB, QB), BF16)
+    pool_shape = shape((H, pool_all, count), BF16)
+    wide_shape = shape((count, D), F32)
+    outs = [
+        ("q_out", shape((count, D), BF16), anywhere),
+        ("k_out", shape((span, D), BF16), anywhere),
+        ("v_out", shape((span, D), BF16), anywhere),
+        ("tt_out", shape((D, count), BF16), anywhere),
+        ("mask_out", shape((2, size, LANES), F32), anywhere),
+        ("tap_out", shape((8, D), F32), anywhere),
+        ("pieces_out", shape((seq, 2, size, D), BF16), anywhere),
+        ("near_e", near_shape, pl.BlockSpec((2, blocks, 2 * QB, QB), lambda i: (in_first(i), 0, 0, 0))),
+        ("pool_e", pool_shape, pl.BlockSpec((2, pool_all, count), lambda i: (in_second(i), 0, 0))),
+        ("o_out", wide_shape, pl.BlockSpec((count, LANES), lambda i: (0, in_second(i)))),
+        ("rn_out", wide_shape, pl.BlockSpec((count, LANES), lambda i: (0, in_second(i)))),
+        ("rp_out", wide_shape, pl.BlockSpec((count, LANES), lambda i: (0, in_second(i)))),
+    ]
+    scratch = [
+        ("x", pltpu.VMEM((span, D), BF16)),
+        ("wq", pltpu.VMEM((D, D), BF16)),
+        ("wk", pltpu.VMEM((D, D), BF16)),
+        ("wv", pltpu.VMEM((D, D), BF16)),
+        ("qs", pltpu.VMEM((count, D), BF16)),
+        ("ks", pltpu.VMEM((span, D), BF16)),
+        ("vs", pltpu.VMEM((span, D), BF16)),
+        ("tt", pltpu.VMEM((D, count), BF16)),
+        ("mask", pltpu.VMEM((2, size, LANES), F32)),
+        ("tap", pltpu.VMEM((8, D), F32)),
+        ("cells", pltpu.VMEM((PAIRS, span, LANES), F32)),
+        ("pieces", pltpu.VMEM((seq, 2, size, D), BF16)),
+        ("o_near", pltpu.VMEM((PAIRS, LANES, count), F32)),
+        ("stats", pltpu.VMEM((PAIRS, 8, count), F32)),
+        ("near_bias", pltpu.VMEM((blocks, 2 * QB, QB), F32)),
+        ("pool_bias", pltpu.VMEM((pool_all, count), F32)),
+        ("s_sem", pltpu.SemaphoreType.DMA((2 + seq,))),
+        ("r_sem", pltpu.SemaphoreType.DMA((2 + seq,))),
+        ("l_sem", pltpu.SemaphoreType.DMA((11,))),
+    ]
+    (queries, keys, values, tok_t, tap_masks, taps, pieces, near_e, pool_e, attention, near_scale, pool_scale) = (
+        pl.pallas_call(
+            partial(forward_kernel, names=[entry[0] for entry in ins + outs + scratch]),
+            grid_spec=pltpu.PrefetchScalarGridSpec(
+                num_scalar_prefetch=0,
+                grid=(FORWARD_LAST + 1,),
+                in_specs=[entry[2] for entry in ins],
+                out_specs=[entry[2] for entry in outs],
+                scratch_shapes=[entry[1] for entry in scratch],
+            ),
+            out_shape=[entry[1] for entry in outs],
+            compiler_params=pltpu.CompilerParams(
+                collective_id=1,
+                has_side_effects=True,
+                vmem_limit_bytes=60 * MB,
+                dimension_semantics=("arbitrary",),
+            ),
+            cost_estimate=pl.CostEstimate(
+                flops=4 * H * 768 * 256 * count + 6 * count * D * D, bytes_accessed=16 * MB, transcendentals=0
+            ),
+            name="forward",
+        )(*[entry[1] for entry in ins])
     )
 
     dp = lax.axis_size("dp")
@@ -1092,10 +1191,9 @@
     )
     mixed, act, slope, low_t, feed_grad, z_grad, unit_one, inv_one, att_t, sums = call(
         dense_kernel,
-        info,
         args,
         [whole(a) for a in args[:5]]
-        + [columns(w_in, D), pl.BlockSpec((D, D), lambda i, info: (i, 0))],
+        + [columns(w_in, D), pl.BlockSpec((D, D), lambda i: (i, 0))],
         outs,
         [whole(outs[0]), columns(outs[1], D), columns(outs[2], D)] + [whole(a) for a in outs[3:]],
         (CHUNKS,),
@@ -1146,14 +1244,12 @@
     block("near_e", near_e, lead_spec(near_e, in_near))
     block("keys", keys, col_spec(keys, in_late))
     block("values", values, col_spec(values, in_late))
-    for i, piece in enumerate(pieces):
-        block("piece%d" % i, piece, col_spec(piece, in_pool))
+    block("piece", pieces, col_spec(pieces, in_pool))
     block("masks", tap_masks, all_spec(tap_masks))
     block("taps", taps, col_spec(taps, in_late))
     block("sums", sums, all_spec(sums))
     block("vecs", vecs, all_spec(vecs))
     block("inv", inv_one, all_spec(inv_one))
-    anywhere = pl.BlockSpec(memory_space=pl.ANY)
     for name, array in (
         ("win_any", w_in),
         ("wback_any", w_back),
@@ -1260,8 +1356,7 @@
         shape((rows, 5), F32),
     )
     done = call(
-        lambda info, *refs: unpack_kernel(*refs),
-        info,
+        unpack_kernel,
         tuple(totals),
         [whole(a) for a in totals],
         outs,

time: 180 us -> 158 us (0.88)
  waiting for transfers between devices: 10.9 us -> 0 us
  starting transfers between devices: 7.71 us -> 0 us
  local copies, waits for them, and re-layouts: 6.48 us -> 3.72 us
    pallas_call x5 -> x2, Pallas kernels: 56.2 us -> 22.3 us  [call(): pl.pallas_call(kernel, grid_spec=pltpu.PrefetchScalarGridSpec(num_scalar_...]
    pallas_call x0 -> x1, Pallas kernels: none -> 33.9 us  [per_device(): pl.pallas_call(partial(forward_kernel, names=[entry[0] for entry in ins +...]
    ppermute x5 -> x0, waiting for transfers between devices: 10.9 us -> none  [the longest x1 9.91 us: per_device(): lax.ppermute(pool_own, 'seq', hop_pairs('seq', ny, 2, ny - hop))]
    ppermute x5 -> x0, starting transfers between devices: 7.71 us -> none  [the longest x1 3.94 us: per_device(): lax.ppermute(pool_own, 'seq', hop_pairs('seq', ny, 2, ny - hop))]
  transfers between devices with their start and end apart: 5 -> 0, of which waited for: 2 -> 0; matrix products, arithmetic and copies ran while one was open for 2% -> 0% of each run, Pallas kernels for 6% -> 0%
where the time goes in v6:
time: 158 us
  Pallas kernels  153 us (97%)
  local copies, waits for them, and re-layouts  3.72 us (2%)
    pallas_call x1, Pallas kernels, per_device(): pl.pallas_call(partial(backward_kernel, names=names, pieces=seq), grid_sp...  96.9 us
    pallas_call x1, Pallas kernels, per_device(): pl.pallas_call(partial(forward_kernel, names=[entry[0] for entry in ins +...  33.9 us
    pallas_call x2, Pallas kernels, call(): pl.pallas_call(kernel, grid_spec=pltpu.PrefetchScalarGridSpec(num_scalar_...  22.3 us

profile of v6, /device:TPU:0, one launch (start us, length us, event | category | flops | bytes accessed | tf_op | source)
XLA Modules:
  0.0 157.6 jit_solution(16538268271637556274)
XLA Ops:
  0.6 1.7 %copy.27.refs_1_ = f32[768,5]{1,0:T(8,128)} copy(f32[768,5]{0,1:T(8,128)} %param.26) | data formatting | bytes 30720 | tf_op args[12]
  2.3 0.0 copy-start
  2.3 0.0 copy-start.1
  2.3 0.0 copy-start.2
  2.3 0.0 copy-start.3
  2.3 33.9 %forward.1 = (bf16[512,768]{1,0:T(8,128)(2,1)}, bf16[640,768]{1,0:T(8,128)(2,1)}, bf16[640,768]{1,0:T(8,128)(2,1)}, bf16[768,512]{1,0:T(8,128)(2,1)}, f32[2,128,...) custom-call(s32[1,4]{1,0:T(1,128)} %refs_0_.1, ...), custom_call_target="tpu_custom_call" | custom-call | flops 6643777536 | bytes 16777216 | tf_op jit(solution)/shard_map/forward/pallas_call | solution.py:1148
  36.2 0.0 copy-done
  36.2 0.0 copy-done.1
  36.2 0.0 copy-done.2
  36.3 0.0 copy-done.3
  36.3 0.6 concatenate.3.vecs.refs_12_
  36.9 19.7 %dense.1 = (bf16[512,768]{1,0:T(8,128)(2,1)}, bf16[512,3072]{1,0:T(8,128)(2,1)}, bf16[512,3072]{1,0:T(8,128)(2,1)}, bf16[768,512]{1,0:T(8,128)(2,1)}, bf16[512,7...) custom-call(f32[512,768]{1,0:T(8,128)} %get-tuple-element.55.o.refs_, ...), custom_call_target="tpu_custom_call" | custom-call | flops 5435817984 | bytes 26656768 | tf_op jit(solution)/shard_map/dense/pallas_call | solution.py:1027
  56.6 96.9 %backward.1 = (f32[4,48,384]{2,1,0:T(8,128)}, f32[4,48,384]{2,1,0:T(8,128)}, f32[48,384]{1,0:T(8,128)}, f32[48,384]{1,0:T(8,128)}, f32[48,384]{1,0:T(8,128)}, /*...) custom-call(bf16[512,768]{1,0:T(8,128)(2,1)} %get-tuple-element.57.refs_0_, ...), custom_call_target="tpu_custom_call" | custom-call | flops 22951231488 | bytes 45686784 | tf_op jit(solution)/shard_map/backward/pallas_call | solution.py:1322
  153.5 2.7 %unpack.1 = (bf16[512,768]{1,0:T(8,128)(2,1)}, f32[24,768]{1,0:T(8,128)}, f32[24,768]{1,0:T(8,128)}, f32[24,768]{1,0:T(8,128)}, f32[24,768]{1,0:T(8,128)}, /*ind...) custom-call(f32[4,48,384]{2,1,0:T(8,128)} %get-tuple-element.77.t_in, ...), custom_call_target="tpu_custom_call" | custom-call | bytes 3359584 | tf_op jit(solution)/shard_map/unpack/pallas_call | solution.py:1027
  156.2 1.4 copy.28
  (5 shorter events, 0.0 us)
Async XLA Ops:
  2.3 33.9 %copy-start = (f32[768]{0:T(1024)S(1)}, f32[768]{0:T(1024)}, u32[]{:S(2)}) copy-start(f32[768]{0:T(1024)} %param.22) | copy-start | bytes 9220
  2.3 33.9 %copy-start.1 = (f32[768]{0:T(1024)S(1)}, f32[768]{0:T(1024)}, u32[]{:S(2)}) copy-start(f32[768]{0:T(1024)} %param.23) | copy-start | bytes 9220
  2.3 33.9 %copy-start.2 = (f32[768]{0:T(1024)S(1)}, f32[768]{0:T(1024)}, u32[]{:S(2)}) copy-start(f32[768]{0:T(1024)} %param.24) | copy-start | bytes 9220
  2.3 33.9 %copy-start.3 = (f32[768]{0:T(1024)S(1)}, f32[768]{0:T(1024)}, u32[]{:S(2)}) copy-start(f32[768]{0:T(1024)} %param.25) | copy-start | bytes 9220

commit v7 on v6

--- a/solution.py
+++ b/solution.py
@@ -339,7 +339,6 @@
         pltpu.make_async_copy(r.vs, r.v_out, r.l_sem.at[6]),
         pltpu.make_async_copy(r.tt, r.tt_out, r.l_sem.at[7]),
         pltpu.make_async_copy(r.mask, r.mask_out, r.l_sem.at[8]),
-        pltpu.make_async_copy(r.tap, r.tap_out, r.l_sem.at[9]),
     ]
     store_pieces = pltpu.make_async_copy(r.pieces, r.pieces_out, r.l_sem.at[10])
 
@@ -365,15 +364,9 @@
         def _():
             r.x[HALF + count :] = jnp.zeros((HALF, D), BF16)
 
-        pick = (iota((8, 5), 0) == iota((8, 5), 1)).astype(F32)
-        r.tap[...] = nt(pick, r.pool_weight[...], precision=lax.Precision.HIGHEST)
-        lane = iota((size, LANES), 1)
-        masks = [[tap_mask(ends, start, tap, shift, size, row_len) for tap in range(5)] for shift in range(2)]
-        for shift in range(2):
-            total = jnp.zeros((size, LANES), F32)
-            for tap in range(5):
-                total = jnp.where(lane == tap, masks[shift][tap], total)
-            r.mask[shift] = total
+        for i in range(7):
+            mask = tap_mask(ends, start, i % 5, i // 5, size, row_len)
+            r.mask[i] = jnp.broadcast_to(mask, (size, LANES))
         loads[0].wait()
         inner = slice(HALF, HALF + count)
         for weight, load, cells in ((r.wk, loads[1], r.ks), (r.wv, loads[2], r.vs)):
@@ -398,7 +391,7 @@
                 total = jnp.zeros((size, LANES), F32)
                 for tap in range(5):
                     taken = r.cells.at[c][pl.ds(HALF + tap - 2, size, stride=4), :]
-                    total = total + taken * masks[0][tap] * r.tap[tap : tap + 1, lanes]
+                    total = total + taken * r.mask[tap] * r.pool_weight[tap : tap + 1, lanes]
                 r.pieces[0, which, :, lanes] = total.astype(BF16)
         for hop in range(1, ny):
             to_y(hop).start()
@@ -509,109 +502,74 @@
 
 CHUNKS = FF // D
 BUFFERS = ("sum", "core", "first", "second", "third", "out", "inn")
-POOL = CHUNKS + 1
-NEAR = POOL + PAIRS
-LATE = NEAR + PAIRS
-LAST = LATE + PAIRS
-ORDERS = {
-    "in0": "zxy",
-    "in1": "xzy",
-    "in2": "yzx",
-    "in3": "yzx",
-    "b0": "xzy",
-    "b1": "xzy",
-    "b2": "zxy",
-    "b3": "xyz",
-    "out": "yzx",
-    "q": "xyz",
-    "k": "xyz",
-    "v": "yxz",
-    "small": "yzx",
+ATTEND = CHUNKS + 1
+LAG = 3
+LATE = ATTEND + PAIRS
+LAST = LATE + LAG - 1
+SPLIT = 4 * LANES
+PARTS = (("A", 0, SPLIT), ("B", SPLIT, D))
+NAMES = ("in0", "in1", "in2", "in3", "b0", "b1", "b2", "b3", "out", "q", "kA", "vA", "kB", "vB", "small", "query", "tokens")
+(IN0, IN1, IN2, IN3, B0, B1, B2, B3, OUT, Q, KA, VA, KB, VB, SMALL, QUERY, TOKENS) = range(17)
+XYZ = "xyz"
+XZY = "xzy"
+YXZ = "yxz"
+YZX = "yzx"
+ZYX = "zyx"
+ORDERS = dict(zip(NAMES, (XYZ, ZYX, YXZ, XYZ, XYZ, YZX, XYZ, XZY, ZYX, XYZ, YZX, YXZ, YXZ, XZY, YXZ)))
+PLAN = {
+    (2, 0): (
+        (IN1, 0),
+    ),
+    (2, 1): (
+        (IN0, 0),
+    ),
+    (3, 0): (
+        (IN2, 0),
+    ),
+    (4, 1): (
+        (IN3, 0), (B1, 0),
+    ),
+    (5, 0): (
+        (B0, 0), (OUT, 0),
+    ),
+    (6, 0): (
+        (IN0, 1),
+    ),
+    (6, 1): (
+        (B2, 0),
+    ),
+    (7, 0): (
+        (IN2, 1),
+    ),
+    (8, 0): (
+        (B1, 1), (IN3, 1),
+    ),
+    (9, 0): (
+        (B3, 0), (IN0, 2),
+    ),
+    (9, 1): (
+        (B0, 1),
+    ),
+    (10, 0): (
+        (IN3, 2), (IN2, 2),
+    ),
+    (10, 1): (
+        (B2, 1),
+    ),
+    (11, 1): (
+        (B3, 1), (IN1, 1), (B1, 2), (QUERY, 0), (B0, 2), (KA, 0), (Q, 0),
+    ),
+    (12, 1): (
+        (IN1, 2), (IN0, 3), (VA, 0), (B2, 2),
+    ),
+    (13, 1): (
+        (VB, 0), (KB, 0), (IN2, 3), (KA, 1), (SMALL, 0), (Q, 1), (VA, 1), (VB, 1), (VA, 2),
+        (B3, 2), (IN1, 3), (KB, 1), (Q, 2), (OUT, 1), (SMALL, 1), (KB, 2), (OUT, 2), (KA, 2),
+        (SMALL, 2), (IN3, 3), (VB, 2), (TOKENS, 0), (VB, 3), (OUT, 3), (B0, 3), (B1, 3), (B2, 3),
+        (B3, 3), (Q, 3), (KA, 3), (VA, 3), (KB, 3), (SMALL, 3),
+    ),
 }
-PLAN = {
-    1: (
-        ("in0", 0),
-    ),
-    3: (
-        ("in1", 0),
-    ),
-    4: (
-        ("b0", 0),
-        ("in3", 0),
-        ("b2", 0),
-    ),
-    8: (
-        ("out", 0),
-    ),
-    9: (
-        ("b1", 0),
-    ),
-    10: (
-        ("in1", 1),
-    ),
-    11: (
-        ("b0", 1),
-    ),
-    13: (
-        ("b3", 0),
-    ),
-    14: (
-        ("b1", 1),
-    ),
-    15: (
-        ("in2", 0),
-    ),
-    17: (
-        ("query", 0),
-        ("in3", 1),
-    ),
-    19: (
-        ("q", 0),
-    ),
-    20: (
-        ("in2", 1),
-        ("b3", 1),
-    ),
-    23: (
-        ("in0", 1),
-        ("b1", 2),
-        ("q", 1),
-        ("in3", 2),
-        ("out", 1),
-        ("k", 0),
-        ("small", 0),
-        ("v", 0),
-        ("tokens", 0),
-        ("b3", 2),
-        ("small", 1),
-        ("q", 2),
-        ("k", 1),
-        ("b2", 1),
-        ("v", 1),
-        ("small", 2),
-        ("b0", 2),
-        ("b2", 2),
-        ("k", 2),
-        ("q", 3),
-        ("in0", 2),
-        ("in3", 3),
-        ("b1", 3),
-        ("in2", 2),
-        ("small", 3),
-        ("out", 2),
-        ("in1", 2),
-        ("v", 2),
-        ("out", 3),
-        ("b3", 3),
-        ("in0", 3),
-        ("in1", 3),
-        ("in2", 3),
-        ("b0", 3),
-        ("b2", 3),
-        ("k", 3),
-        ("v", 3),
-    ),
-}
+
 
 def backward_kernel(*refs, names, pieces):
     r = Refs()
@@ -631,8 +589,11 @@
     senders = {"small": r.s_send}
     for f in range(CHUNKS):
         senders["in%d" % f] = r.a_send.at[f]
-    for place, name in enumerate(("out", "q", "k", "v")):
+    for place, name in enumerate(("out", "q")):
         senders[name] = r.a_send.at[place]
+    for part, _, _ in PARTS:
+        for name in ("k" + part, "v" + part):
+            senders[name] = getattr(r, name + "_send")
     for u in range(units_back):
         senders["b%d" % u] = r.b_send.at[u]
     sums = {}
@@ -690,7 +651,9 @@
 
     @pl.when(step == 0)
     def _():
-        for load in chunk_loads(0) + load_feed + [load_unit, load_att]:
+        for load in chunk_loads(0)[1:2] + load_feed[:1] + chunk_loads(0)[3:] + load_feed[1:2]:
+            load.start()
+        for load in chunk_loads(0)[:1] + chunk_loads(0)[2:3] + load_feed[2:]:
             load.start()
         z, x = row // nx, row % nx
         peers = [partner, right, left]
@@ -698,20 +661,69 @@
         peers += [(here, z * nx + (x + hop) % nx) for hop in range(1, nx)]
         peers += [(here, ((z + hop) % nz) * nx + x) for hop in range(1, nz)]
         greet(peers)
-        for load in load_feed:
+        for load in load_feed[:2]:
             load.wait()
+
+    def query_gradient():
+        sums["in1"].sent_core(0)
+        for block in range(ny):
+            store_chunks(r.a_send.at[1, block], nn(r.lt[rows_of(block, 1 - core), :], r.tbuf[0]))
+        sums["q"].start(0)
+        for block in range(ny):
+            store_chunks(sums["q"].keep.at[0, block], nn(r.lt[rows_of(block, core), :], r.tbuf[0]))
+
+    def tokens_gradient():
+        for load in (load_wq, load_wk, load_wv):
+            load.wait()
+        total = r.sg[...] + nt(r.tbuf[0], r.wbuf[1])
+        total = total + nt(r.tbuf[1], r.wbuf[2])
+        r.tokens_grad[...] = (total + nt(r.tbuf[2], r.wbuf[3])).astype(BF16)
+
+    results = {"out": r.t_out, "q": r.t_query, "small": r.t_small}
+    for part, _, _ in PARTS:
+        for name in ("k" + part, "v" + part):
+            results[name] = getattr(r, "t_" + name)
+    for f in range(CHUNKS):
+        results["in%d" % f] = r.t_in.at[f]
+    for u in range(units_back):
+        results["b%d" % u] = r.t_back.at[u]
+
+    def run(name, stage):
+        if name == "query":
+            query_gradient()
+        elif name == "tokens":
+            tokens_gradient()
+        elif name in sums:
+            done = getattr(sums[name], ("core", "one", "two", "three")[stage])(0)
+            if stage == 3:
+                results[name][...] = done
+
+    def run_plan(half):
+        for (when, part), todo in PLAN.items():
+            if part == half:
+
+                @pl.when(step == when)
+                def _(todo=todo):
+                    for index, stage in todo:
+                        run(NAMES[index], stage)
 
     @pl.when(step < CHUNKS)
     def _():
         f = step
         slot = f % 2
-        for load in chunk_loads(f):
+        early, late = chunk_loads(f)[1::2], chunk_loads(f)[0::2]
+        for load in early:
             load.wait()
 
         @pl.when(f < CHUNKS - 1)
         def _():
             for load in chunk_loads(f + 1):
                 load.start()
+
+        @pl.when(f == 1)
+        def _():
+            load_unit.start()
+            load_att.start()
 
         @pl.when(f == CHUNKS - 1)
         def _():
@@ -730,6 +742,14 @@
                 sums["in%d" % i].start(0)
                 for block in range(ny):
                     store_chunks(sums["in%d" % i].keep.at[0, block], kept[block])
+
+        run_plan(0)
+        for load in late:
+            load.wait()
+
+        @pl.when(f == 0)
+        def _():
+            load_feed[2].wait()
 
         r.sg[...] += nt(inner_grad, r.wbuf[slot])
         back = nn(r.tbuf[slot].T, r.fg[...])
@@ -751,6 +771,10 @@
         def _():
             for u in range(units_back):
                 sums["b%d" % u].start(0)
+
+    @pl.when(step == LATE - 1)
+    def _():
+        load_tt.wait()
 
     @pl.when(step == CHUNKS)
     def _():
@@ -791,9 +815,16 @@
         for c in range(PAIRS):
             r.acc[1, c] = attended_grad[:, c * LANES : (c + 1) * LANES]
 
-    @pl.when((step >= POOL) & (step < NEAR))
-    def _():
-        p = step - POOL
+    def pool_on(p):
+        pool_core(p).wait_recv()
+        for hop in range(1, ny):
+            for which in range(2):
+                r.p_keep[p, hop, which] = r.p_keep[p, hop, which] + r.p_in[p, hop, which]
+            pool_y(p, hop).start()
+
+    @pl.when((step >= ATTEND) & (step < LATE))
+    def _():
+        p = step - ATTEND
         r.gb[...] = (r.acc[1, p] * r.rp[...]).astype(BF16)
         delta = score_delta(r.gb[...], r.o[...])
         kp = jnp.concatenate([piece[0] for piece in kv], axis=0)
@@ -827,18 +858,12 @@
                 target[p, i % ny, which, size:] = total[rows, :].astype(BF16)
         pool_core(p).start()
 
-    @pl.when((step > POOL) & (step <= NEAR))
-    def _():
-        p = step - POOL - 1
-        pool_core(p).wait_recv()
-        for hop in range(1, ny):
-            for which in range(2):
-                r.p_keep[p, hop, which] = r.p_keep[p, hop, which] + r.p_in[p, hop, which]
-            pool_y(p, hop).start()
-
-    @pl.when((step >= NEAR) & (step < LATE))
-    def _():
-        p = step - NEAR
+        @pl.when(p > 0)
+        def _():
+            pool_on(p - 1)
+
+        run_plan(0)
+
         r.gb[...] = (r.acc[1, p] * r.rn[...]).astype(BF16)
         delta = score_delta(r.gb[...], r.o[...])
         kt = r.keys[...].T
@@ -876,25 +901,13 @@
         def _():
             halo(p, 1).start()
 
-    def query_gradient():
-        load_tt.wait()
-        sums["in1"].sent_core(0)
-        for block in range(ny):
-            store_chunks(r.a_send.at[1, block], nn(r.lt[rows_of(block, 1 - core), :], r.tbuf[0]))
-        sums["q"].start(0)
-        for block in range(ny):
-            store_chunks(sums["q"].keep.at[0, block], nn(r.lt[rows_of(block, core), :], r.tbuf[0]))
-
-    def tokens_gradient():
-        for load in (load_wq, load_wk, load_wv):
-            load.wait()
-        total = r.sg[...] + nt(r.tbuf[0], r.wbuf[1])
-        total = total + nt(r.tbuf[1], r.wbuf[2])
-        r.tokens_grad[...] = (total + nt(r.tbuf[2], r.wbuf[3])).astype(BF16)
-
-    @pl.when((step >= LATE) & (step < LAST))
-    def _():
-        p = step - LATE
+        @pl.when(p == PAIRS - 1)
+        def _():
+            pool_on(p)
+
+    @pl.when(step >= ATTEND + LAG)
+    def _():
+        p = step - ATTEND - LAG
         lanes = pl.ds(pl.multiple_of(p * LANES, LANES), LANES)
         for hop in range(1, ny):
             pool_y(p, hop).wait_recv()
@@ -913,7 +926,7 @@
 
         moves = ((2, 0, 0), (3, 1, 0), (4, 2, 0), (0, 2, 1), (1, 3, 1))
         sums = [jnp.zeros((1, LANES), F32)] * 5
-        for which, source in ((0, r.keys), (1, r.values)):
+        for which, source in ((0, r.keys_late), (1, r.values_late)):
             grad = r.acc.at[which, p]
             r.cells[...] = source[...].astype(F32)
             total = r.p_keep[p, 0, which].astype(F32) + r.p_in[p, 0, which].astype(F32)
@@ -921,28 +934,35 @@
                 total = total + r.p_y[p, hop - 1, which].astype(F32)
             r.g[...] = total
             for tap, place, shift in moves:
-                mask = r.masks[shift, :, tap : tap + 1]
+                mask = r.masks[5 * shift + tap]
                 spread = r.g[shift : shift + size, :] * mask * r.taps[tap : tap + 1, :]
                 grad[pl.ds(place, size, stride=4), :] += spread
             for tap in range(5):
                 taken = r.cells[pl.ds(HALF + tap - 2, size, stride=4), :]
-                product = r.g[0:size, :] * r.masks[0, :, tap : tap + 1] * taken
+                product = r.g[0:size, :] * r.masks[tap] * taken
                 sums[tap] = sums[tap] + jnp.sum(product, axis=0, keepdims=True)
             r.tbuf[1 + which, :, lanes] = grad[...].astype(BF16)
         for tap in range(5):
             r.small[8 + tap : 9 + tap, lanes] = sums[tap]
 
-    @pl.when(step == LAST)
-    def _():
-        for name, place, low in (("k", 2, 1), ("v", 3, 2)):
-            sums["in%d" % place].sent_core(0)
+    def key_gradients(part, first, last):
+        for name, low in (("k" + part, 1), ("v" + part, 2)):
             for block in range(ny):
                 rows = rows_of(block, 1 - core)
-                store_chunks(r.a_send.at[place, block], nn(r.lt[rows, :], r.tbuf[low]))
+                store_chunks(senders[name].at[block], nn(r.lt[rows, :], r.tbuf[low, :, first:last]))
             sums[name].start(0)
             keep = sums[name].keep
             for block in range(ny):
-                store_chunks(keep.at[0, block], nn(r.lt[rows_of(block, core), :], r.tbuf[low]))
+                rows = rows_of(block, core)
+                store_chunks(keep.at[0, block], nn(r.lt[rows, :], r.tbuf[low, :, first:last]))
+
+    @pl.when(step == LATE)
+    def _():
+        key_gradients(*PARTS[0])
+
+    @pl.when(step == LAST)
+    def _():
+        key_gradients(*PARTS[1])
         r.small_t[...] = r.small[...].T
         few = D // (seq * nz * nx)
         for block in range(ny):
@@ -955,32 +975,11 @@
                         part[z, x, 0:few] = vectors[start : start + few].astype(BF16)
         sums["small"].start(0)
 
-    results = {"out": r.t_out, "q": r.t_query, "k": r.t_key, "v": r.t_value, "small": r.t_small}
-    for f in range(CHUNKS):
-        results["in%d" % f] = r.t_in.at[f]
-    for u in range(units_back):
-        results["b%d" % u] = r.t_back.at[u]
-
-    def run(name, stage):
-        if name == "query":
-            query_gradient()
-        elif name == "tokens":
-            tokens_gradient()
-        elif name in sums:
-            done = getattr(sums[name], ("core", "one", "two", "three")[stage])(0)
-            if stage == 3:
-                results[name][...] = done
-
-    for when, todo in PLAN.items():
-
-        @pl.when(step == when)
-        def _(todo=todo):
-            for name, stage in todo:
-                run(name, stage)
+    run_plan(1)
 
     @pl.when(step == LAST)
     def _():
-        reused = ["in%d" % f for f in range(CHUNKS)]
+        reused = ["in0", "in1"]
         for name in sums:
             if name not in reused:
                 sums[name].sent_core(0)
@@ -1001,12 +1000,15 @@
                 halo(p, 1).wait_send()
 
 
-def unpack_kernel(t_in, t_back, t_query, t_key, t_value, t_out, t_small, tg, *outs):
+def unpack_kernel(t_in, t_back, t_query, t_ka, t_kb, t_va, t_vb, t_out, t_small, tg, *outs):
     tokens_grad, query, key, value, out, inn, back = outs[:7]
     rows = query.shape[0]
     tokens_grad[...] = tg[...]
-    for source, target in ((t_query, query), (t_key, key), (t_value, value), (t_out, out)):
+    for source, target in ((t_query, query), (t_out, out)):
         target[...] = unfold_rows(source[...], rows)
+    for one, two, target in ((t_ka, t_kb, key), (t_va, t_vb, value)):
+        target[:, 0:SPLIT] = unfold_rows(one[...], rows)
+        target[:, SPLIT:] = unfold_rows(two[...], rows)
     for u in range(CHUNKS):
         inn[:, u * D : (u + 1) * D] = unfold_rows(t_in[u], rows)
     units, part, wide = t_back.shape
@@ -1019,7 +1021,7 @@
     turned = jnp.concatenate([small, jnp.zeros((pad, LANES), F32)], axis=0).T
     for i in range(4):
         outs[7 + i][...] = turned[i : i + 1, 0:rows]
-    outs[11][...] = small[0:rows, 8:13]
+    outs[11][...] = turned[8:13, 0:rows]
 
 
 def call(kernel, args, in_specs, outs, out_specs, grid, scratch, flops, name):
@@ -1081,9 +1083,8 @@
     size = count // 4
     tok = tokens[0]
     og = out_grad[0]
-    vecs = jnp.concatenate(
-        [jnp.stack([norm1_gain, norm1_bias, norm2_gain, norm2_bias]), jnp.zeros((4, D), F32)]
-    )
+    taps = pool_weight.T
+    vecs = jnp.stack([norm1_gain, norm1_bias, norm2_gain, norm2_bias])
 
     def shape(dims, kind):
         return jax.ShapeDtypeStruct(dims, kind)
@@ -1100,7 +1101,7 @@
 
     ins = [
         ("lengths", item_lengths, pl.BlockSpec(memory_space=pltpu.SMEM)),
-        ("pool_weight", pool_weight, whole(pool_weight)),
+        ("pool_weight", taps, whole(taps)),
         ("tok", tok, anywhere),
         ("wq_any", w_query, anywhere),
         ("wk_any", w_key, anywhere),
@@ -1114,8 +1115,7 @@
         ("k_out", shape((span, D), BF16), anywhere),
         ("v_out", shape((span, D), BF16), anywhere),
         ("tt_out", shape((D, count), BF16), anywhere),
-        ("mask_out", shape((2, size, LANES), F32), anywhere),
-        ("tap_out", shape((8, D), F32), anywhere),
+        ("mask_out", shape((7, size, LANES), F32), anywhere),
         ("pieces_out", shape((seq, 2, size, D), BF16), anywhere),
         ("near_e", near_shape, pl.BlockSpec((2, blocks, 2 * QB, QB), lambda i: (in_first(i), 0, 0, 0))),
         ("pool_e", pool_shape, pl.BlockSpec((2, pool_all, count), lambda i: (in_second(i), 0, 0))),
@@ -1132,8 +1132,7 @@
         ("ks", pltpu.VMEM((span, D), BF16)),
         ("vs", pltpu.VMEM((span, D), BF16)),
         ("tt", pltpu.VMEM((D, count), BF16)),
-        ("mask", pltpu.VMEM((2, size, LANES), F32)),
-        ("tap", pltpu.VMEM((8, D), F32)),
+        ("mask", pltpu.VMEM((7, size, LANES), F32)),
         ("cells", pltpu.VMEM((PAIRS, span, LANES), F32)),
         ("pieces", pltpu.VMEM((seq, 2, size, D), BF16)),
         ("o_near", pltpu.VMEM((PAIRS, LANES, count), F32)),
@@ -1144,7 +1143,7 @@
         ("r_sem", pltpu.SemaphoreType.DMA((2 + seq,))),
         ("l_sem", pltpu.SemaphoreType.DMA((11,))),
     ]
-    (queries, keys, values, tok_t, tap_masks, taps, pieces, near_e, pool_e, attention, near_scale, pool_scale) = (
+    (queries, keys, values, tok_t, tap_masks, pieces, near_e, pool_e, attention, near_scale, pool_scale) = (
         pl.pallas_call(
             partial(forward_kernel, names=[entry[0] for entry in ins + outs + scratch]),
             grid_spec=pltpu.PrefetchScalarGridSpec(
@@ -1224,27 +1223,23 @@
         rest = (0,) * len(array.shape)
         return pl.BlockSpec(array.shape, lambda i: rest)
 
-    def in_pool(i):
-        return jnp.clip(i - POOL, 0, PAIRS - 1)
-
-    def in_near(i):
-        return jnp.clip(i - NEAR, 0, PAIRS - 1)
-
-    def in_both(i):
-        return jnp.clip(i - POOL, 0, 2 * PAIRS - 1) % PAIRS
+    def in_pair(i):
+        return jnp.clip(i - ATTEND, 0, PAIRS - 1)
 
     def in_late(i):
-        return jnp.clip(i - NEAR, 0, 2 * PAIRS - 1) % PAIRS
-
-    block("q", queries, col_spec(queries, in_both))
-    block("o", attention, col_spec(attention, in_both))
-    block("rp", pool_scale, col_spec(pool_scale, in_pool))
-    block("rn", near_scale, col_spec(near_scale, in_near))
-    block("pool_e", pool_e, lead_spec(pool_e, in_pool))
-    block("near_e", near_e, lead_spec(near_e, in_near))
-    block("keys", keys, col_spec(keys, in_late))
-    block("values", values, col_spec(values, in_late))
-    block("piece", pieces, col_spec(pieces, in_pool))
+        return jnp.clip(i - ATTEND - LAG, 0, PAIRS - 1)
+
+    block("q", queries, col_spec(queries, in_pair))
+    block("o", attention, col_spec(attention, in_pair))
+    block("rp", pool_scale, col_spec(pool_scale, in_pair))
+    block("rn", near_scale, col_spec(near_scale, in_pair))
+    block("pool_e", pool_e, lead_spec(pool_e, in_pair))
+    block("near_e", near_e, lead_spec(near_e, in_pair))
+    block("keys", keys, col_spec(keys, in_pair))
+    block("values", values, col_spec(values, in_pair))
+    block("keys_late", keys, col_spec(keys, in_late))
+    block("values_late", values, col_spec(values, in_late))
+    block("piece", pieces, col_spec(pieces, in_pair))
     block("masks", tap_masks, all_spec(tap_masks))
     block("taps", taps, col_spec(taps, in_late))
     block("sums", sums, all_spec(sums))
@@ -1271,8 +1266,10 @@
         ("t_in", shape((CHUNKS,) + half_one.shape[3:], F32)),
         ("t_back", shape((half_back.shape[0],) + half_back.shape[4:], F32)),
         ("t_query", shape(half_one.shape[3:], F32)),
-        ("t_key", shape(half_one.shape[3:], F32)),
-        ("t_value", shape(half_one.shape[3:], F32)),
+        ("t_kA", shape(folded(rows, SPLIT), F32)),
+        ("t_kB", shape(folded(rows, D - SPLIT), F32)),
+        ("t_vA", shape(folded(rows, SPLIT), F32)),
+        ("t_vB", shape(folded(rows, D - SPLIT), F32)),
         ("t_out", shape(half_one.shape[3:], F32)),
         ("t_small", shape(half_small.shape[3:], F32)),
         ("tokens_grad", shape((count, D), BF16)),
@@ -1309,6 +1306,10 @@
     ]
     sizes = {name: half_one.shape for name in ORDERS}
     sizes["small"] = half_small.shape
+    for part, first, after in PARTS:
+        for name in ("k" + part, "v" + part):
+            sizes[name] = half_one.shape[:3] + folded(rows, after - first)
+            scratch.append((name + "_send", pltpu.VMEM(sizes[name], BF16)))
     for u in range(CHUNKS):
         if u < half_back.shape[0]:
             sizes["b%d" % u] = half_back.shape[1:]
@@ -1353,7 +1354,7 @@
         shape((1, rows), F32),
         shape((1, rows), F32),
         shape((1, rows), F32),
-        shape((rows, 5), F32),
+        shape((5, rows), F32),
     )
     done = call(
         unpack_kernel,
@@ -1379,7 +1380,7 @@
         done[8].reshape(rows),
         done[9].reshape(rows),
         done[10].reshape(rows),
-        done[11],
+        done[11].T,
     )
 
 

time: 158 us -> 145 us (0.918)
  Pallas kernels: 153 us -> 143 us
  local copies, waits for them, and re-layouts: 3.72 us -> 0.03 us
    pallas_call x1, Pallas kernels: 96.9 us -> 88.3 us  [per_device(): pl.pallas_call(partial(backward_kernel, names=names, pieces=seq), grid_sp...]
    unnamed x10 -> x8, local copies, waits for them, and re-layouts: 3.06 us -> 0.02 us
where the time goes in v7:
time: 145 us
  Pallas kernels  143 us (99%)
    pallas_call x1, Pallas kernels, per_device(): pl.pallas_call(partial(backward_kernel, names=names, pieces=seq), grid_sp...  88.3 us
    pallas_call x1, Pallas kernels, per_device(): pl.pallas_call(partial(forward_kernel, names=[entry[0] for entry in ins +...  32.8 us
    pallas_call x2, Pallas kernels, call(): pl.pallas_call(kernel, grid_spec=pltpu.PrefetchScalarGridSpec(num_scalar_...  22.2 us

profile of v7, /device:TPU:0, one launch (start us, length us, event | category | flops | bytes accessed | tf_op | source)
XLA Modules:
  0.0 144.9 jit_solution(16642444678888388352)
XLA Ops:
  0.6 0.0 copy-start
  0.7 0.0 copy-start.1
  0.7 0.0 copy-start.2
  0.7 0.0 copy-start.3
  0.7 32.8 %forward.1 = (bf16[512,768]{1,0:T(8,128)(2,1)}, bf16[640,768]{1,0:T(8,128)(2,1)}, bf16[640,768]{1,0:T(8,128)(2,1)}, bf16[768,512]{1,0:T(8,128)(2,1)}, f32[7,128,...) custom-call(s32[1,4]{1,0:T(1,128)} %refs_0_.1, ...), custom_call_target="tpu_custom_call" | custom-call | flops 6643777536 | bytes 16777216 | tf_op jit(solution)/shard_map/forward/pallas_call | solution.py:1147
  33.5 0.0 copy-done
  33.5 0.0 copy-done.1
  33.5 0.0 copy-done.2
  33.6 0.0 copy-done.3
  33.6 0.6 pad_maximum_fusion.vecs.refs_14_
  34.2 19.6 %dense.1 = (bf16[512,768]{1,0:T(8,128)(2,1)}, bf16[512,3072]{1,0:T(8,128)(2,1)}, bf16[512,3072]{1,0:T(8,128)(2,1)}, bf16[768,512]{1,0:T(8,128)(2,1)}, bf16[512,7...) custom-call(f32[512,768]{1,0:T(8,128)} %get-tuple-element.56.o.refs_, ...), custom_call_target="tpu_custom_call" | custom-call | flops 5435817984 | bytes 26644480 | tf_op jit(solution)/shard_map/dense/pallas_call | solution.py:1029
  53.8 88.3 %backward.1 = (f32[4,48,384]{2,1,0:T(8,128)}, f32[4,48,384]{2,1,0:T(8,128)}, f32[48,384]{1,0:T(8,128)}, f32[48,256]{1,0:T(8,128)}, f32[48,128]{1,0:T(8,128)}, /*...) custom-call(bf16[512,768]{1,0:T(8,128)(2,1)} %get-tuple-element.58.r, ...), custom_call_target="tpu_custom_call" | custom-call | flops 22951231488 | bytes 47959040 | tf_op jit(solution)/shard_map/backward/pallas_call | solution.py:1323
  142.1 2.7 %unpack.1 = (bf16[512,768]{1,0:T(8,128)(2,1)}, f32[24,768]{1,0:T(8,128)}, f32[24,768]{1,0:T(8,128)}, f32[24,768]{1,0:T(8,128)}, f32[24,768]{1,0:T(8,128)}, /*ind...) custom-call(f32[4,48,384]{2,1,0:T(8,128)} %get-tuple-element.77.t_in, ...), custom_call_target="tpu_custom_call" | custom-call | bytes 3359584 | tf_op jit(solution)/shard_map/unpack/pallas_call | solution.py:1029
  (4 shorter events, 0.0 us)
Async XLA Ops:
  0.6 32.8 %copy-start = (f32[768]{0:T(1024)S(1)}, f32[768]{0:T(1024)}, u32[]{:S(2)}) copy-start(f32[768]{0:T(1024)} %param.25) | copy-start | bytes 9220
  0.7 32.9 %copy-start.1 = (f32[768]{0:T(1024)S(1)}, f32[768]{0:T(1024)}, u32[]{:S(2)}) copy-start(f32[768]{0:T(1024)} %param.24) | copy-start | bytes 9220
  0.7 32.9 %copy-start.2 = (f32[768]{0:T(1024)S(1)}, f32[768]{0:T(1024)}, u32[]{:S(2)}) copy-start(f32[768]{0:T(1024)} %param.23) | copy-start | bytes 9220
  0.7 32.9 %copy-start.3 = (f32[768]{0:T(1024)S(1)}, f32[768]{0:T(1024)}, u32[]{:S(2)}) copy-start(f32[768]{0:T(1024)} %param.22) | copy-start | bytes 9220

commit v8 on v7

--- a/solution.py
+++ b/solution.py
@@ -514,59 +514,49 @@
 XZY = "xzy"
 YXZ = "yxz"
 YZX = "yzx"
+ZXY = "zxy"
 ZYX = "zyx"
-ORDERS = dict(zip(NAMES, (XYZ, ZYX, YXZ, XYZ, XYZ, YZX, XYZ, XZY, ZYX, XYZ, YZX, YXZ, YXZ, XZY, YXZ)))
+ORDERS = dict(zip(NAMES, (ZYX, XZY, XZY, YXZ, ZXY, XZY, YXZ, XYZ, XYZ, XYZ, XYZ, YXZ, ZXY, XZY, YZX)))
 PLAN = {
+    (1, 0): (
+        (IN0, 0),
+    ),
     (2, 0): (
         (IN1, 0),
-    ),
-    (2, 1): (
-        (IN0, 0),
     ),
     (3, 0): (
         (IN2, 0),
     ),
     (4, 1): (
-        (IN3, 0), (B1, 0),
+        (B3, 0), (B2, 0), (B1, 0), (B0, 0), (IN3, 0),
     ),
-    (5, 0): (
-        (B0, 0), (OUT, 0),
+    (5, 1): (
+        (OUT, 0), (IN1, 1), (IN0, 1),
     ),
-    (6, 0): (
-        (IN0, 1),
+    (8, 0): (
+        (IN0, 2),
     ),
-    (6, 1): (
-        (B2, 0),
-    ),
-    (7, 0): (
+    (8, 1): (
         (IN2, 1),
     ),
-    (8, 0): (
-        (B1, 1), (IN3, 1),
-    ),
-    (9, 0): (
-        (B3, 0), (IN0, 2),
-    ),
     (9, 1): (
-        (B0, 1),
+        (IN1, 2), (B2, 1),
     ),
     (10, 0): (
-        (IN3, 2), (IN2, 2),
+        (B3, 1), (B1, 1), (IN3, 1),
     ),
     (10, 1): (
-        (B2, 1),
+        (QUERY, 0), (OUT, 1), (B2, 2), (B0, 1),
     ),
     (11, 1): (
-        (B3, 1), (IN1, 1), (B1, 2), (QUERY, 0), (B0, 2), (KA, 0), (Q, 0),
-    ),
-    (12, 1): (
-        (IN1, 2), (IN0, 3), (VA, 0), (B2, 2),
+        (Q, 0), (IN3, 2), (IN2, 2),
     ),
     (13, 1): (
-        (VB, 0), (KB, 0), (IN2, 3), (KA, 1), (SMALL, 0), (Q, 1), (VA, 1), (VB, 1), (VA, 2),
-        (B3, 2), (IN1, 3), (KB, 1), (Q, 2), (OUT, 1), (SMALL, 1), (KB, 2), (OUT, 2), (KA, 2),
-        (SMALL, 2), (IN3, 3), (VB, 2), (TOKENS, 0), (VB, 3), (OUT, 3), (B0, 3), (B1, 3), (B2, 3),
-        (B3, 3), (Q, 3), (KA, 3), (VA, 3), (KB, 3), (SMALL, 3),
+        (KA, 0), (VA, 0), (B3, 2), (B0, 2), (B1, 2), (TOKENS, 0), (KB, 0), (VB, 0), (SMALL, 0),
+        (OUT, 2), (Q, 1), (SMALL, 1), (VA, 1), (VB, 1), (KA, 1), (Q, 2), (VA, 2), (SMALL, 2),
+        (KA, 2), (KB, 1), (VB, 2), (KB, 2), (IN0, 3), (IN1, 3), (IN2, 3), (IN3, 3), (B0, 3),
+        (B1, 3), (B2, 3), (B3, 3), (OUT, 3), (SMALL, 3), (VB, 3), (KB, 3), (Q, 3), (VA, 3),
+        (KA, 3),
     ),
 }
 

time: 145 us -> 148 us (1.021)
  Pallas kernels: 143 us -> 147 us
    pallas_call x1, Pallas kernels: 88.3 us -> 91.5 us  [per_device(): pl.pallas_call(partial(backward_kernel, names=names, pieces=seq), grid_sp...]
where the time goes in v8:
time: 148 us
  Pallas kernels  147 us (99%)
    pallas_call x1, Pallas kernels, per_device(): pl.pallas_call(partial(backward_kernel, names=names, pieces=seq), grid_sp...  91.5 us
    pallas_call x1, Pallas kernels, per_device(): pl.pallas_call(partial(forward_kernel, names=[entry[0] for entry in ins +...  32.8 us
    pallas_call x2, Pallas kernels, call(): pl.pallas_call(kernel, grid_spec=pltpu.PrefetchScalarGridSpec(num_scalar_...  22.2 us

profile of v8, /device:TPU:0, one launch (start us, length us, event | category | flops | bytes accessed | tf_op | source)
XLA Modules:
  0.0 148.1 jit_solution(14735936057961592092)
XLA Ops:
  0.6 0.0 copy-start
  0.7 0.0 copy-start.1
  0.7 0.0 copy-start.2
  0.7 0.0 copy-start.3
  0.7 32.8 %forward.1 = (bf16[512,768]{1,0:T(8,128)(2,1)}, bf16[640,768]{1,0:T(8,128)(2,1)}, bf16[640,768]{1,0:T(8,128)(2,1)}, bf16[768,512]{1,0:T(8,128)(2,1)}, f32[7,128,...) custom-call(s32[1,4]{1,0:T(1,128)} %refs_0_.1, ...), custom_call_target="tpu_custom_call" | custom-call | flops 6643777536 | bytes 16777216 | tf_op jit(solution)/shard_map/forward/pallas_call | solution.py:1137
  33.5 0.0 copy-done
  33.5 0.0 copy-done.1
  33.5 0.0 copy-done.2
  33.6 0.0 copy-done.3
  33.6 0.6 pad_maximum_fusion.vecs.refs_14_
  34.2 19.6 %dense.1 = (bf16[512,768]{1,0:T(8,128)(2,1)}, bf16[512,3072]{1,0:T(8,128)(2,1)}, bf16[512,3072]{1,0:T(8,128)(2,1)}, bf16[768,512]{1,0:T(8,128)(2,1)}, bf16[512,7...) custom-call(f32[512,768]{1,0:T(8,128)} %get-tuple-element.56.o.refs_, ...), custom_call_target="tpu_custom_call" | custom-call | flops 5435817984 | bytes 26644480 | tf_op jit(solution)/shard_map/dense/pallas_call | solution.py:1019
  53.8 91.5 %backward.1 = (f32[4,48,384]{2,1,0:T(8,128)}, f32[4,48,384]{2,1,0:T(8,128)}, f32[48,384]{1,0:T(8,128)}, f32[48,256]{1,0:T(8,128)}, f32[48,128]{1,0:T(8,128)}, /*...) custom-call(bf16[512,768]{1,0:T(8,128)(2,1)} %get-tuple-element.58.r, ...), custom_call_target="tpu_custom_call" | custom-call | flops 22951231488 | bytes 47959040 | tf_op jit(solution)/shard_map/backward/pallas_call | solution.py:1313
  145.3 2.7 %unpack.1 = (bf16[512,768]{1,0:T(8,128)(2,1)}, f32[24,768]{1,0:T(8,128)}, f32[24,768]{1,0:T(8,128)}, f32[24,768]{1,0:T(8,128)}, f32[24,768]{1,0:T(8,128)}, /*ind...) custom-call(f32[4,48,384]{2,1,0:T(8,128)} %get-tuple-element.77.t_in, ...), custom_call_target="tpu_custom_call" | custom-call | bytes 3359584 | tf_op jit(solution)/shard_map/unpack/pallas_call | solution.py:1019
  (4 shorter events, 0.0 us)
Async XLA Ops:
  0.6 32.8 %copy-start = (f32[768]{0:T(1024)S(1)}, f32[768]{0:T(1024)}, u32[]{:S(2)}) copy-start(f32[768]{0:T(1024)} %param.25) | copy-start | bytes 9220
  0.7 32.9 %copy-start.1 = (f32[768]{0:T(1024)S(1)}, f32[768]{0:T(1024)}, u32[]{:S(2)}) copy-start(f32[768]{0:T(1024)} %param.24) | copy-start | bytes 9220
  0.7 32.9 %copy-start.2 = (f32[768]{0:T(1024)S(1)}, f32[768]{0:T(1024)}, u32[]{:S(2)}) copy-start(f32[768]{0:T(1024)} %param.23) | copy-start | bytes 9220
  0.7 32.9 %copy-start.3 = (f32[768]{0:T(1024)S(1)}, f32[768]{0:T(1024)}, u32[]{:S(2)}) copy-start(f32[768]{0:T(1024)} %param.22) | copy-start | bytes 9220

commit v9 on v7

--- a/solution.py
+++ b/solution.py
@@ -542,31 +542,31 @@
         (IN2, 1),
     ),
     (8, 0): (
-        (B1, 1), (IN3, 1),
+        (B1, 1), (IN3, 1), (IN1, 1),
     ),
     (9, 0): (
         (B3, 0), (IN0, 2),
     ),
     (9, 1): (
-        (B0, 1),
+        (B0, 1), (OUT, 1),
     ),
     (10, 0): (
-        (IN3, 2), (IN2, 2),
+        (IN3, 2), (IN2, 2), (IN1, 2),
     ),
     (10, 1): (
         (B2, 1),
     ),
     (11, 1): (
-        (B3, 1), (IN1, 1), (B1, 2), (QUERY, 0), (B0, 2), (KA, 0), (Q, 0),
+        (B3, 1), (OUT, 2), (B1, 2), (QUERY, 0), (B0, 2), (KA, 0), (Q, 0),
     ),
     (12, 1): (
-        (IN1, 2), (IN0, 3), (VA, 0), (B2, 2),
+        (VA, 0), (B2, 2),
     ),
     (13, 1): (
-        (VB, 0), (KB, 0), (IN2, 3), (KA, 1), (SMALL, 0), (Q, 1), (VA, 1), (VB, 1), (VA, 2),
-        (B3, 2), (IN1, 3), (KB, 1), (Q, 2), (OUT, 1), (SMALL, 1), (KB, 2), (OUT, 2), (KA, 2),
+        (VB, 0), (KB, 0), (KA, 1), (SMALL, 0), (Q, 1), (VA, 1), (VB, 1), (VA, 2),
+        (B3, 2), (KB, 1), (Q, 2), (SMALL, 1), (KB, 2), (KA, 2),
         (SMALL, 2), (IN3, 3), (VB, 2), (TOKENS, 0), (VB, 3), (OUT, 3), (B0, 3), (B1, 3), (B2, 3),
-        (B3, 3), (Q, 3), (KA, 3), (VA, 3), (KB, 3), (SMALL, 3),
+        (B3, 3), (IN0, 3), (IN1, 3), (IN2, 3), (Q, 3), (KA, 3), (VA, 3), (KB, 3), (SMALL, 3),
     ),
 }
 

time: 145 us -> 145 us (level)
  no operation moved by 1% of the time
where the time goes in v9:
time: 145 us
  Pallas kernels  143 us (99%)
    pallas_call x1, Pallas kernels, per_device(): pl.pallas_call(partial(backward_kernel, names=names, pieces=seq), grid_sp...  88.3 us
    pallas_call x1, Pallas kernels, per_device(): pl.pallas_call(partial(forward_kernel, names=[entry[0] for entry in ins +...  32.8 us
    pallas_call x2, Pallas kernels, call(): pl.pallas_call(kernel, grid_spec=pltpu.PrefetchScalarGridSpec(num_scalar_...  22.2 us

profile of v9, /device:TPU:0, one launch (start us, length us, event | category | flops | bytes accessed | tf_op | source)
XLA Modules:
  0.0 144.9 jit_solution(3655324765664010275)
XLA Ops:
  0.6 0.0 copy-start
  0.7 0.0 copy-start.1
  0.7 0.0 copy-start.2
  0.7 0.0 copy-start.3
  0.7 32.8 %forward.1 = (bf16[512,768]{1,0:T(8,128)(2,1)}, bf16[640,768]{1,0:T(8,128)(2,1)}, bf16[640,768]{1,0:T(8,128)(2,1)}, bf16[768,512]{1,0:T(8,128)(2,1)}, f32[7,128,...) custom-call(s32[1,4]{1,0:T(1,128)} %refs_0_.1, ...), custom_call_target="tpu_custom_call" | custom-call | flops 6643777536 | bytes 16777216 | tf_op jit(solution)/shard_map/forward/pallas_call | solution.py:1147
  33.5 0.0 copy-done
  33.5 0.0 copy-done.1
  33.5 0.0 copy-done.2
  33.6 0.0 copy-done.3
  33.6 0.6 pad_maximum_fusion.vecs.refs_14_
  34.2 19.6 %dense.1 = (bf16[512,768]{1,0:T(8,128)(2,1)}, bf16[512,3072]{1,0:T(8,128)(2,1)}, bf16[512,3072]{1,0:T(8,128)(2,1)}, bf16[768,512]{1,0:T(8,128)(2,1)}, bf16[512,7...) custom-call(f32[512,768]{1,0:T(8,128)} %get-tuple-element.56.o.refs_, ...), custom_call_target="tpu_custom_call" | custom-call | flops 5435817984 | bytes 26644480 | tf_op jit(solution)/shard_map/dense/pallas_call | solution.py:1029
  53.8 88.3 %backward.1 = (f32[4,48,384]{2,1,0:T(8,128)}, f32[4,48,384]{2,1,0:T(8,128)}, f32[48,384]{1,0:T(8,128)}, f32[48,256]{1,0:T(8,128)}, f32[48,128]{1,0:T(8,128)}, /*...) custom-call(bf16[512,768]{1,0:T(8,128)(2,1)} %get-tuple-element.58.r, ...), custom_call_target="tpu_custom_call" | custom-call | flops 22951231488 | bytes 47959040 | tf_op jit(solution)/shard_map/backward/pallas_call | solution.py:1323
  142.1 2.7 %unpack.1 = (bf16[512,768]{1,0:T(8,128)(2,1)}, f32[24,768]{1,0:T(8,128)}, f32[24,768]{1,0:T(8,128)}, f32[24,768]{1,0:T(8,128)}, f32[24,768]{1,0:T(8,128)}, /*ind...) custom-call(f32[4,48,384]{2,1,0:T(8,128)} %get-tuple-element.77.t_in, ...), custom_call_target="tpu_custom_call" | custom-call | bytes 3359584 | tf_op jit(solution)/shard_map/unpack/pallas_call | solution.py:1029
  (4 shorter events, 0.0 us)
Async XLA Ops:
  0.6 32.8 %copy-start = (f32[768]{0:T(1024)S(1)}, f32[768]{0:T(1024)}, u32[]{:S(2)}) copy-start(f32[768]{0:T(1024)} %param.25) | copy-start | bytes 9220
  0.7 32.9 %copy-start.1 = (f32[768]{0:T(1024)S(1)}, f32[768]{0:T(1024)}, u32[]{:S(2)}) copy-start(f32[768]{0:T(1024)} %param.24) | copy-start | bytes 9220
  0.7 32.9 %copy-start.2 = (f32[768]{0:T(1024)S(1)}, f32[768]{0:T(1024)}, u32[]{:S(2)}) copy-start(f32[768]{0:T(1024)} %param.23) | copy-start | bytes 9220
  0.7 32.9 %copy-start.3 = (f32[768]{0:T(1024)S(1)}, f32[768]{0:T(1024)}, u32[]{:S(2)}) copy-start(f32[768]{0:T(1024)} %param.22) | copy-start | bytes 9220
